TPU v7x, 128 devices: a whole 4x4x4 slice. The times are simulated.
128 devices in a mesh: dp: 64 (over z_lo, y, x, core), chan: 2 (over z_hi).
Axes of the slice: x: 4, y: 4, z: 4 (z_hi: 2, z_lo: 2; z = z_hi * 2 + z_lo), core: 2. Of those that a mesh axis runs over, the one named last changes fastest.
Arguments:
- tokens: bfloat16 [32768, 768], P('dp', 'chan'), may hold values from -6 to 6
- lengths: int32 [64], P('dp'), may hold values from 1 to 512, 20480 in all
- norm_gain: float32 [2, 2, 768], P(None, None, 'chan'), may hold values from 0.1 to 1.9
- norm_bias: float32 [2, 2, 768], P(None, None, 'chan'), may hold values from -3 to 3
- in_weight: bfloat16 [2, 768, 3, 768], P(None, None, None, 'chan'), may hold values from -0.21875 to 0.21875
- in_bias: float32 [2, 3, 768], P(None, None, 'chan'), may hold values from -3 to 3
- short_weight: float32 [2, 3, 3, 768], P(None, None, None, 'chan'), may hold values from -3 to 3
- short_bias: float32 [2, 3, 768], P(None, None, 'chan'), may hold values from -3 to 3
- filter_first: float32 [2, 33, 64], replicated, may hold values from -1 to 1
- filter_inner: float32 [2, 2, 64, 64], replicated, may hold values from -1 to 1
- filter_biases: float32 [2, 3, 64], replicated, may hold values from -3.140625 to 3.140625
- filter_out: float32 [2, 64, 768], P(None, None, 'chan'), may hold values from -0.125 to 0.125
- filter_skip: float32 [2, 768], P(None, 'chan'), may hold values from -4 to 4
- out_weight: bfloat16 [2, 768, 768], P(None, 'chan'), may hold values from -0.21875 to 0.21875
- out_bias: float32 [2, 768], P(None, 'chan'), may hold values from -3 to 3
- up_weight: bfloat16 [2, 768, 3072], P(None, None, 'chan'), may hold values from -0.21875 to 0.21875
- up_bias: float32 [2, 3072], P(None, 'chan'), may hold values from -3 to 3
- down_weight: bfloat16 [2, 3072, 768], P(None, 'chan'), may hold values from -0.15625 to 0.15625
- down_bias: float32 [2, 768], P(None, 'chan'), may hold values from -3 to 3
- cotangent: bfloat16 [32768, 768], P('dp', 'chan'), may hold values from -6 to 6
Outputs:
- result: bfloat16 [32768, 768], P('dp', 'chan')
- grad_tokens: float32 [32768, 768], P('dp', 'chan')
- grad_norm_gain: float32 [2, 2, 768], P(None, None, 'chan')
- grad_norm_bias: float32 [2, 2, 768], P(None, None, 'chan')
- grad_in_weight: float32 [2, 768, 3, 768], P(None, None, None, 'chan')
- grad_in_bias: float32 [2, 3, 768], P(None, None, 'chan')
- grad_short_weight: float32 [2, 3, 3, 768], P(None, None, None, 'chan')
- grad_short_bias: float32 [2, 3, 768], P(None, None, 'chan')
- grad_filter_first: float32 [2, 33, 64], replicated
- grad_filter_inner: float32 [2, 2, 64, 64], replicated
- grad_filter_biases: float32 [2, 3, 64], replicated
- grad_filter_out: float32 [2, 64, 768], P(None, None, 'chan')
- grad_filter_skip: float32 [2, 768], P(None, 'chan')
- grad_out_weight: float32 [2, 768, 768], P(None, 'chan')
- grad_out_bias: float32 [2, 768], P(None, 'chan')
- grad_up_weight: float32 [2, 768, 3072], P(None, None, 'chan')
- grad_up_bias: float32 [2, 3072], P(None, 'chan')
- grad_down_weight: float32 [2, 3072, 768], P(None, 'chan')
- grad_down_bias: float32 [2, 768], P(None, 'chan')
Inputs may be any that keep to these rules, and one draw needn't show every extreme that they name: `lengths`: valid tokens of a sequence fill the first slots of its 512 slots, and some sequence fills all of them.
All inputs are finite; a program needn't handle non-finite values. No bound on the sum of `lengths` on one device may be relied on, other than what follows from the above.
Results may differ from a plain program's by a relative error of at most 0.018.
Values may be sent and summed in bfloat16 or wider, within the bound.
No kernel may reach another device: no remote copies, remote signals or barrier semaphores. Data moves between devices by JAX's collectives and lax.ppermute only.
A program may use at most 256 MiB of HBM per device.

v0:
```python
import math

import jax
import jax.numpy as jnp
from jax import lax
from jax.sharding import PartitionSpec as P

D = 768


HIGH = lax.Precision.HIGHEST
EPSILON = 1e-05


def positions(length, emb):
    bands = (emb - 1) // 2
    steps = jnp.arange(length, dtype=jnp.float32)
    times = steps / (length - 1)
    freqs = 0.0001 + (bands - 1 - 0.0001) * jnp.arange(bands, dtype=jnp.float32) / (bands - 1)
    angle = 2 * math.pi * steps[:, None] * freqs[None, :] / length
    feats = jnp.concatenate([times[:, None], jnp.cos(angle), -jnp.sin(angle)], 1)
    return (feats, times)


def decay_rates(channel, width):
    slow = math.log(0.01) / 1.5
    fast = math.log(0.01) / 0.3
    return jnp.abs(slow + (fast - slow) * channel.astype(jnp.float32) / (width - 1))


def spectral_tables(length):
    size = 2 * length
    freq = jnp.arange(length + 1, dtype=jnp.int32)
    steps = jnp.arange(length, dtype=jnp.int32)
    phase = freq[:, None] * steps[None, :] % size
    angle = phase.astype(jnp.float32) * (2 * math.pi / size)
    weights = jnp.where((freq == 0) | (freq == length), 1.0, 2.0).astype(jnp.float32) / size
    return (jnp.cos(angle), jnp.sin(angle), weights)


def mixer_core(mixed, core, feats, times, rates, tables, seq_count):
    short_w, short_b, first_w, inner_w, filt_b, out_fw, skip = core
    length = feats.shape[0]
    chans = mixed.shape[-1]
    mixed = mixed.reshape(seq_count, length, 3, chans)
    padded = jnp.pad(mixed, ((0, 0), (2, 0), (0, 0), (0, 0)))
    conv = (
        short_w[0] * padded[:, :length]
        + short_w[1] * padded[:, 1 : length + 1]
        + short_w[2] * padded[:, 2:]
        + short_b
    )
    hidden = jnp.sin(jnp.dot(feats, first_w, precision=HIGH) + filt_b[0])
    hidden = jnp.sin(jnp.dot(hidden, inner_w[0], precision=HIGH) + filt_b[1])
    hidden = jnp.sin(jnp.dot(hidden, inner_w[1], precision=HIGH) + filt_b[2])
    kernel = jnp.dot(hidden, out_fw, precision=HIGH) * (
        jnp.exp(-times[:, None] * rates[None, :]) + 0.05
    )
    value = conv[:, :, 2] * conv[:, :, 1]
    cosine, sine, weights = tables
    real_in = jnp.einsum("ft,stc->sfc", cosine, value, precision=HIGH)
    imag_in = -jnp.einsum("ft,stc->sfc", sine, value, precision=HIGH)
    real_kern = jnp.dot(cosine, kernel, precision=HIGH)
    imag_kern = -jnp.dot(sine, kernel, precision=HIGH)
    real_out = real_in * real_kern - imag_in * imag_kern
    imag_out = real_in * imag_kern + imag_in * real_kern
    result = jnp.einsum("ft,sfc->stc", cosine * weights[:, None], real_out, precision=HIGH)
    result = result - jnp.einsum("ft,sfc->stc", sine * weights[:, None], imag_out, precision=HIGH)
    value = result + skip * value
    return (value * conv[:, :, 0]).reshape(seq_count * length, chans)


def row_norm(stream, gain, shift):
    total, squares = lax.psum((jnp.sum(stream, -1), jnp.sum(stream * stream, -1)), "chan")
    mean = total / D
    scale = lax.rsqrt(squares / D - mean * mean + EPSILON)
    scaled = (stream - mean[:, None]) * scale[:, None]
    return (scaled, scale, (scaled * gain + shift).astype(jnp.bfloat16))


def project_rows(normed, weight):
    piece = lax.all_gather(normed, "chan", axis=1, tiled=True)
    total = jnp.dot(piece, weight, preferred_element_type=jnp.float32)
    return (total, piece)


def spread_sum(partial_value):
    return lax.psum_scatter(
        partial_value.astype(jnp.bfloat16), "chan", scatter_dimension=1, tiled=True
    ).astype(jnp.float32)


def pull_back(grad_rows, weight, kept):
    piece = lax.all_gather(grad_rows, "chan", axis=1, tiled=True)
    total = lax.dot_general(
        piece, weight, (((1,), (1,)), ((), ())), preferred_element_type=jnp.float32
    )
    block = lax.dot_general(
        kept, piece, (((0,), (0,)), ((), ())), preferred_element_type=jnp.float32
    )
    return (total, block)


def gather_back(grad_rows, weight):
    partial_value = lax.dot_general(
        grad_rows, weight, (((1,), (1,)), ((), ())), preferred_element_type=jnp.float32
    )
    return lax.psum_scatter(
        partial_value.astype(jnp.bfloat16), "chan", scatter_dimension=1, tiled=True
    ).astype(jnp.float32)


def norm_back(dnormed, scaled, scale, gain):
    dscaled = dnormed * gain
    first, second = lax.psum((jnp.sum(dscaled, -1), jnp.sum(dscaled * scaled, -1)), "chan")
    dstream = scale[:, None] * (dscaled - first[:, None] / D - scaled * second[:, None] / D)
    return (dstream, jnp.sum(dnormed * scaled, 0), jnp.sum(dnormed, 0))


def filter_sum(first_g, inner_g, biases_g):
    return lax.psum((first_g, inner_g, biases_g), ("dp", "chan"))


def shards(
    tokens,
    lengths,
    norm_gain,
    norm_bias,
    in_weight,
    in_bias,
    short_weight,
    short_bias,
    filter_first,
    filter_inner,
    filter_biases,
    filter_out,
    filter_skip,
    out_weight,
    out_bias,
    up_weight,
    up_bias,
    down_weight,
    down_bias,
    cotangent,
):
    seq_count = lengths.shape[0]
    length = tokens.shape[0] // seq_count
    chans = tokens.shape[1]
    layers = norm_gain.shape[0]
    positions_mask = (jnp.arange(length, dtype=jnp.int32)[None, :] < lengths[:, None]).astype(
        jnp.float32
    )
    token_mask = positions_mask.reshape(-1, 1)
    feats, times = positions(length, filter_first.shape[1])
    channel = lax.axis_index("chan") * chans + jnp.arange(chans, dtype=jnp.int32)
    rates = decay_rates(channel, D)
    tables = spectral_tables(length)

    def core_of(layer):
        return (
            short_weight[layer],
            short_bias[layer],
            filter_first[layer],
            filter_inner[layer],
            filter_biases[layer],
            filter_out[layer],
            filter_skip[layer],
        )

    stream = tokens.astype(jnp.float32)
    saved = []
    for layer in range(layers):
        gain, shift = (norm_gain[layer], norm_bias[layer])
        scaled_one, scale_one, normed_one = row_norm(stream, gain[0], shift[0])
        in_matrix = in_weight[layer].reshape(in_weight.shape[1], -1)
        mixed, whole_one = project_rows(normed_one, in_matrix)
        mixed = (mixed + in_bias[layer].reshape(-1)).reshape(-1, 3, chans)
        gated = mixer_core(mixed, core_of(layer), feats, times, rates, tables, seq_count).astype(
            jnp.bfloat16
        )
        branch = (
            spread_sum(jnp.dot(gated, out_weight[layer], preferred_element_type=jnp.float32))
            + out_bias[layer]
        )
        stream = stream + token_mask * branch
        scaled_two, scale_two, normed_two = row_norm(stream, gain[1], shift[1])
        inner, whole_two = project_rows(normed_two, up_weight[layer])
        inner = inner + up_bias[layer]
        active = jax.nn.gelu(inner).astype(jnp.bfloat16)
        branch_two = (
            spread_sum(jnp.dot(active, down_weight[layer], preferred_element_type=jnp.float32))
            + down_bias[layer]
        )
        stream = stream + token_mask * branch_two
        saved.append(
            (
                scaled_one,
                scale_one,
                whole_one,
                in_matrix,
                mixed,
                gated,
                scaled_two,
                scale_two,
                whole_two,
                inner,
                active,
            )
        )
    result = stream.astype(jnp.bfloat16)
    grad = cotangent.astype(jnp.float32)
    collected = [None] * layers
    for layer in reversed(range(layers)):
        (
            scaled_one,
            scale_one,
            whole_one,
            in_matrix,
            mixed,
            gated,
            scaled_two,
            scale_two,
            whole_two,
            inner,
            active,
        ) = saved[layer]
        gain = norm_gain[layer]
        grad_mlp = (token_mask * grad).astype(jnp.bfloat16)
        dactive, grad_down = pull_back(grad_mlp, down_weight[layer], active)
        grad_downb = jnp.sum(grad_mlp.astype(jnp.float32), 0)
        dinner = jax.vjp(jax.nn.gelu, inner)[1](dactive)[0].astype(jnp.bfloat16)
        grad_up = lax.dot_general(
            whole_two, dinner, (((0,), (0,)), ((), ())), preferred_element_type=jnp.float32
        )
        grad_upb = jnp.sum(dinner.astype(jnp.float32), 0)
        dnormed = gather_back(dinner, up_weight[layer])
        dstream, gain_two, shift_two = norm_back(dnormed, scaled_two, scale_two, gain[1])
        grad = grad + dstream
        grad_mix = (token_mask * grad).astype(jnp.bfloat16)
        dgated, grad_outw = pull_back(grad_mix, out_weight[layer], gated)
        grad_outb = jnp.sum(grad_mix.astype(jnp.float32), 0)

        def core_fn(mixed_in, core_in):
            return mixer_core(mixed_in, core_in, feats, times, rates, tables, seq_count)

        core_back = jax.vjp(core_fn, mixed, core_of(layer))[1]
        dmixed, dcore = core_back(dgated)
        dmixed = dmixed.reshape(dmixed.shape[0], -1).astype(jnp.bfloat16)
        grad_in = lax.dot_general(
            whole_one, dmixed, (((0,), (0,)), ((), ())), preferred_element_type=jnp.float32
        )
        grad_in = grad_in.reshape(grad_in.shape[0], 3, chans)
        grad_inb = jnp.sum(dmixed.astype(jnp.float32), 0).reshape(3, chans)
        dnormed = gather_back(dmixed, in_matrix)
        dstream, gain_one, shift_one = norm_back(dnormed, scaled_one, scale_one, gain[0])
        grad = grad + dstream
        grad_first, grad_inner, grad_fbias = filter_sum(dcore[2], dcore[3], dcore[4])
        grad_gain = jnp.stack([gain_one, gain_two])
        grad_shift = jnp.stack([shift_one, shift_two])
        grad_shortw, grad_shortb, grad_fout, grad_skip = (dcore[0], dcore[1], dcore[5], dcore[6])
        summed = (
            grad_gain,
            grad_shift,
            grad_in,
            grad_inb,
            grad_shortw,
            grad_shortb,
            grad_fout,
            grad_skip,
            grad_outw,
            grad_outb,
            grad_up,
            grad_upb,
            grad_down,
            grad_downb,
        )
        collected[layer] = (summed, (grad_first, grad_inner, grad_fbias))
    stacked = [
        jnp.stack([collected[layer][0][member] for layer in range(layers)]) for member in range(14)
    ]
    shared = [
        jnp.stack([collected[layer][1][member] for layer in range(layers)]) for member in range(3)
    ]
    stacked = lax.psum(
        (
            stacked[0],
            stacked[1],
            stacked[2],
            stacked[3],
            stacked[4],
            stacked[5],
            stacked[6],
            stacked[7],
            stacked[8],
            stacked[9],
            stacked[10],
            stacked[11],
            stacked[12],
            stacked[13],
        ),
        "dp",
    )
    return (
        result,
        grad,
        stacked[0],
        stacked[1],
        stacked[2],
        stacked[3],
        stacked[4],
        stacked[5],
        shared[0],
        shared[1],
        shared[2],
        stacked[6],
        stacked[7],
        stacked[8],
        stacked[9],
        stacked[10],
        stacked[11],
        stacked[12],
        stacked[13],
    )


def solution(mesh):
    placed = (
        P("dp", "chan"),
        P("dp"),
        P(None, None, "chan"),
        P(None, None, "chan"),
        P(None, None, None, "chan"),
        P(None, None, "chan"),
        P(None, None, None, "chan"),
        P(None, None, "chan"),
        P(),
        P(),
        P(),
        P(None, None, "chan"),
        P(None, "chan"),
        P(None, "chan", None),
        P(None, "chan"),
        P(None, None, "chan"),
        P(None, "chan"),
        P(None, "chan", None),
        P(None, "chan"),
        P("dp", "chan"),
    )
    return jax.shard_map(
        shards,
        mesh=mesh,
        in_specs=placed,
        out_specs=(
            P("dp", "chan"),
            P("dp", "chan"),
            P(None, None, "chan"),
            P(None, None, "chan"),
            P(None, None, None, "chan"),
            P(None, None, "chan"),
            P(None, None, None, "chan"),
            P(None, None, "chan"),
            P(),
            P(),
            P(),
            P(None, None, "chan"),
            P(None, "chan"),
            P(None, "chan", None),
            P(None, "chan"),
            P(None, None, "chan"),
            P(None, "chan"),
            P(None, "chan", None),
            P(None, "chan"),
        ),
        check_vma=False,
    )
```

profile of v0, /device:TPU:1, one launch (start us, length us, event | category | flops | bytes accessed | tf_op | source)
XLA Modules:
  0.0 1897.3 jit_solution(5983350480449043785)
XLA Ops:
  17.0 7.2 fusion.63
  24.2 7.1 convolution_bitcast_fusion.16
  33.0 6.7 all-reduce.40
  40.4 11.3 all_gather.24
  51.6 3.9 fusion.403
  57.7 4.1 convolution_add_fusion.1
  67.6 5.7 convolution_bitcast_fusion.15
  73.3 5.7 convolution_bitcast_fusion.17
  79.9 6.2 fusion.104
  86.1 6.7 fusion.73
  97.9 4.0 copy.80
  103.7 17.9 reduce-scatter.25.cloned.1.call-done
  123.5 6.0 all-reduce.39
  132.7 11.0 all_gather.25
  149.3 4.5 fusion.53
  163.9 7.4 convolution_bitcast_fusion.13
  171.2 7.1 fusion.62
  181.5 6.0 all-reduce.38
  189.2 9.9 all_gather.26
  205.7 4.7 add_add_fusion
  210.4 5.7 convolution_bitcast_fusion.12
  216.2 5.7 convolution_bitcast_fusion.14
  221.9 6.6 fusion.102
  228.6 6.5 fusion.72
  240.6 8.9 all_gather.28
  249.5 15.2 reduce-scatter.29.cloned.1.call-done
  266.8 6.0 all-reduce.37
  274.3 11.0 all_gather.27
  289.5 6.7 convert_reduce_fusion
  302.1 23.0 %reduce-scatter.33.cloned.1.call-done = bf16[384,512]{1,0:T(8,128)(2,1)} async-done(((bf16[768,512]{1,0:T(8,128)(2,1)}), bf16[384,512]{1,0:T(8,128)(2,1)}) %reduce-scatter.33.cloned.1.call-update) | async-done | bytes 393232
  327.0 6.0 all-reduce.36
  336.0 11.2 all_gather.29
  349.7 5.7 convolution_bitcast_fusion.10
  355.5 6.2 convolution_bitcast_fusion.11
  363.4 6.0 convolution_bitcast_fusion.20
  369.5 6.5 fusion.200
  387.6 5.4 fusion.59
  396.0 5.6 convolution_bitcast_fusion.2
  401.7 4.4 convolution_bitcast_fusion
  406.7 8.6 fusion.111
  417.6 6.7 fusion.67
  438.7 6.0 all-reduce.35
  445.9 3.7 convert_reduce_fusion.10
  449.6 9.2 all_gather.30
  458.7 5.4 convert_reduce_fusion.1
  479.9 4.3 convolution_bitcast_fusion.1
  484.2 6.8 pad_maximum_fusion.1
  491.0 4.6 pad_maximum_fusion
  495.6 4.1 reduce-scatter.37.cloned.1.call-done
  501.9 6.0 all-reduce.34
  510.5 11.5 all_gather.31
  523.0 5.7 convolution_bitcast_fusion.8
  528.7 6.0 convolution_bitcast_fusion.9
  534.7 6.5 fusion.114
  541.3 6.2 convolution_bitcast_fusion.18
  549.4 7.4 fusion.66
  556.8 6.6 fusion.207
  601.0 145.6 %all-reduce.45.cloned.1.call-done = (f32[1,33,64]{2,1,0:T(8,128)}, f32[1,33,64]{2,1,0:T(8,128)}, f32[1,2,64,64]{3,2,1,0:T(8,128)}, f32[1,2,64,64]{3,2,1,0:T(8,12...) async-done(((f32[1,33,64]{2,1,0:T(8,128)}, f32[1,33,64]{2,1,0:T(8,128)}, f32[1,2,64,64]{3,2,1,0:T(8,128)}, f32[1,2,64,64]{3,2,1,0:T(8,128)}, f32[1,3,64]{2,1,0:T(4,128)}, ...) | async-done | bytes 83984 | tf_op jit(solution)/shard_map/psum | solution.py:121
  750.8 5.3 all-reduce.33
  758.0 472.2 %all-reduce.47.cloned.1.call-done = (f32[2,2,384]{2,1,0:T(2,128)}, f32[2,2,384]{2,1,0:T(2,128)}, f32[2,3,384]{2,1,0:T(4,128)}, f32[2,3,3,384]{3,2,1,0:T(4,128)},...) async-done(((f32[2,2,384]{2,1,0:T(2,128)}, f32[2,2,384]{2,1,0:T(2,128)}, f32[2,3,384]{2,1,0:T(4,128)}, ...) | async-done | bytes 79888 | tf_op jit(solution)/shard_map/psum | solution.py:284
  1234.2 632.9 %all-reduce.49.cloned.1.call-done = (f32[2,768,3,384]{3,1,2,0:T(8,128)}, f32[2,64,384]{2,1,0:T(8,128)}, f32[2,384,768]{2,1,0:T(8,128)}, f32[2,768,1536]{2,1,0:T(8,128)}, f32[2,1536,768]{2,1,0:T(8,128)}) async-done(((f32[2,768,3,384]{3,1,2,0:T(8,128)}, f32[2,64,384]{2,1,0:T(8,128)}, f32[2,384,768]{2,1,0:T(8,128)}, f32[2,768,1536]{2,1,0:T(8,128)}, f32[2,1536,768]{2,1,0:T(8,128)}), ...) | async-done | bytes 28508176 | tf_op jit(solution)/shard_map/psum | solution.py:284
  1869.6 7.2 copy.172
  1880.1 4.8 copy.177
  1886.2 3.7 copy.179
  (656 shorter events, 197.9 us)
Async XLA Ops:
  7.2 8.9 copy-start.73
  7.2 114.4 %reduce-scatter.25.cloned.1.call-start = ((), (), s32[]{:S(2)}) async-start(), calls=%async_computation.8 | async-start | bytes 1179648
  7.3 9.7 copy-start.148
  7.3 78.7 %copy-start.183 = (f32[513]{0:T(1024)}, f32[513]{0:T(1024)S(1)}, u32[]{:S(2)}) copy-start(f32[513]{0:T(1024)S(1)} %select_multiply_fusion) | copy-start | bytes 6160
  7.4 8.7 copy-start.144
  11.8 12.4 copy-start.52
  14.0 10.2 copy-start.56
  67.6 25.3 %copy-start.14 = (f32[1,512,3,384]{1,3,2,0:T(8,128)}, f32[1,512,3,384]{1,3,2,0:T(8,128)S(1)}, u32[]{:S(2)}) copy-start(f32[1,512,3,384]{1,3,2,0:T(8,128)S(1)} %add_add_fusion.1) | copy-start | bytes 7077892
  73.3 12.8 copy-start.212
  96.3 83.1 %reduce-scatter.27.cloned.1.call-start = ((), (), s32[]{:S(2)}) async-start(), calls=%async_computation.9 | async-start | bytes 1179648
  97.8 32.4 %copy-start.18 = (bf16[512,384]{0,1:T(8,128)(2,1)}, bf16[512,384]{0,1:T(8,128)(2,1)S(1)}, u32[]{:S(2)}) copy-start(bf16[512,384]{0,1:T(8,128)(2,1)S(1)} %copy.85) | copy-start | bytes 1179652
  130.2 13.4 copy-start.114
  130.2 13.4 copy-start.117
  156.3 108.4 %reduce-scatter.29.cloned.1.call-start = ((), (), s32[]{:S(2)}) async-start(), calls=%async_computation.10 | async-start | bytes 1179648
  181.5 17.6 copy-start.1
  188.2 10.9 copy-start.129
  188.2 10.9 copy-start.130
  188.2 11.8 copy-start.40
  188.2 11.8 copy-start.173
  210.4 24.6 %copy-start.16 = (f32[1,512,3,384]{1,3,2,0:T(8,128)}, f32[1,512,3,384]{1,3,2,0:T(8,128)S(1)}, u32[]{:S(2)}) copy-start(f32[1,512,3,384]{1,3,2,0:T(8,128)S(1)} %add_add_fusion) | copy-start | bytes 7077892
  216.2 12.4 copy-start.216
  240.5 84.5 %reduce-scatter.33.cloned.1.call-start = ((), (), s32[]{:S(2)}) async-start(), calls=%async_computation.12 | async-start | bytes 1179648
  273.4 11.9 copy-start.119
  273.4 11.9 copy-start.122
  286.2 11.1 slice-start.7
  299.6 25.4 %copy-start.108 = (f32[384]{0:T(512)S(1)}, f32[384]{0:T(512)}, u32[]{:S(2)}) copy-start(f32[384]{0:T(512)} %get-tuple-element.254) | copy-start | bytes 4612
  299.6 25.4 %copy-start.120 = (f32[512]{0:T(512)S(1)}, f32[512]{0:T(512)}, u32[]{:S(2)}) copy-start(f32[512]{0:T(512)} %copy-done.119) | copy-start | bytes 6148
  302.0 134.4 %reduce-scatter.35.cloned.1.call-start = ((), (), s32[]{:S(2)}) async-start(), calls=%async_computation.13 | async-start | bytes 1179648
  333.7 13.5 copy-start.17
  355.4 13.9 copy-start.208
  387.0 58.9 %reduce-scatter.31.cloned.1.call-start = ((), (), s32[]{:S(2)}) async-start(), calls=%async_computation.11 | async-start | bytes 1179648
  406.1 11.4 copy-start.146
  406.1 11.4 copy-start.150
  406.1 93.5 %reduce-scatter.37.cloned.1.call-start = ((), (), s32[]{:S(2)}) async-start(), calls=%async_computation.14 | async-start | bytes 1179648
  406.6 9.2 copy-start.167
  406.6 9.8 copy-start.169
  406.6 10.3 copy-start.170
  406.6 10.9 copy-start.209
  406.6 10.9 copy-start.211
  406.7 10.9 copy-start.217
  406.7 10.9 copy-start.219
  436.4 9.5 copy-start.109
  436.4 9.5 copy-start.121
  445.9 18.2 slice-start.9
  474.7 120.9 %reduce-scatter.39.cloned.1.call-start = ((), (), s32[]{:S(2)}) async-start(), calls=%async_computation.15 | async-start | bytes 1179648
  479.9 11.1 slice-start
  479.9 11.1 slice-start.2
  491.0 8.7 copy-start.4
  491.0 8.7 copy-start.106
  491.0 8.7 copy-start.115
  499.7 8.9 copy-start.26
  508.6 13.4 copy-start.15
  510.5 11.5 copy-start.51
  572.6 174.0 %all-reduce.45.cloned.1.call-start = ((), (), s32[]{:S(2)}) async-start(), calls=%async_computation.16 | async-start | bytes 352256 | tf_op jit(solution)/shard_map/psum | solution.py:121
  594.6 635.6 %all-reduce.47.cloned.1.call-start = ((), (), s32[]{:S(2)}) async-start(), calls=%async_computation.17 | async-start | bytes 190464 | tf_op jit(solution)/shard_map/psum | solution.py:284
  598.3 1268.8 %all-reduce.49.cloned.1.call-start = ((), (), s32[]{:S(2)}) async-start(), calls=%async_computation.18 | async-start | bytes 57016320 | tf_op jit(solution)/shard_map/psum | solution.py:284
  599.1 157.0 %copy-start.13 = (f32[512,384]{0,1:T(8,128)S(1)}, f32[512,384]{0,1:T(8,128)}, u32[]{:S(2)}) copy-start(f32[512,384]{0,1:T(8,128)} %get-tuple-element.164) | copy-start | bytes 2359300
  599.1 157.0 %copy-start.43 = (bf16[384,512]{1,0:T(8,128)(2,1)S(1)}, bf16[384,512]{1,0:T(8,128)(2,1)}, u32[]{:S(2)}) copy-start(bf16[384,512]{1,0:T(8,128)(2,1)} %reduce-scatter.39.cloned.1.call-done) | copy-start | bytes 1179652
  599.1 156.9 %copy-start.107 = (f32[384]{0:T(512)S(1)}, f32[384]{0:T(512)}, u32[]{:S(2)}) copy-start(f32[384]{0:T(512)} %get-tuple-element.253) | copy-start | bytes 4612
  599.1 156.9 %copy-start.116 = (f32[512]{0:T(512)S(1)}, f32[512]{0:T(512)}, u32[]{:S(2)}) copy-start(f32[512]{0:T(512)} %copy-done.114) | copy-start | bytes 6148
  599.1 156.9 %copy-start.118 = (f32[512]{0:T(512)S(1)}, f32[512]{0:T(512)}, u32[]{:S(2)}) copy-start(f32[512]{0:T(512)} %copy-done.117) | copy-start | bytes 6148
  599.1 156.9 %copy-start.153 = (f32[512]{0:T(512)S(1)}, f32[512]{0:T(512)}, u32[]{:S(2)}) copy-start(f32[512]{0:T(512)} %copy-done.152) | copy-start | bytes 6148
  599.1 156.9 %copy-start.163 = (f32[512]{0:T(512)S(1)}, f32[512]{0:T(512)}, u32[]{:S(2)}) copy-start(f32[512]{0:T(512)} %get-tuple-element.148) | copy-start | bytes 6148
  1869.6 10.5 copy-start.5
  (178 other events, 763.0 us)
Sparse Core Ops, SparseCore 0:
  96.4 25.1 reduce-scatter.24
  156.4 22.8 reduce-scatter.26
  240.6 23.9 reduce-scatter.28
  302.1 22.8 reduce-scatter.32
  387.1 22.8 reduce-scatter.34
  412.4 20.8 reduce-scatter.30
  474.8 24.8 reduce-scatter.36
  572.7 22.8 reduce-scatter.38
  602.5 144.0 all-reduce.44
  751.7 478.3 all-reduce.46
  1234.8 632.1 all-reduce.48
where the time goes:
time: 1910 us; the launch traced here: 1900 us
  waiting for transfers between devices  1310 us (69%)
  matrix products  252 us (13%)
  blocking collectives  132 us (7%)
  local copies, waits for them, and re-layouts  98.3 us (5%)
  other arithmetic  84.1 us (4%)
    psum x2, waiting for transfers between devices, shards(): lax.psum((stacked[0], stacked[1], stacked[2], stacked[3], stacked[4], sta...  1110 us
    psum x1, waiting for transfers between devices, filter_sum(): return lax.psum((first_g, inner_g, biases_g), ('dp', 'chan'))  146 us
    unnamed x494, local copies, waits for them, and re-layouts  68.5 us
    unnamed x19, waiting for transfers between devices  62.1 us
    all_gather x4, blocking collectives, project_rows(): piece = lax.all_gather(normed, 'chan', axis=1, tiled=True)  43.1 us
    all_gather x4, blocking collectives, pull_back(): piece = lax.all_gather(grad_rows, 'chan', axis=1, tiled=True)  40.7 us
  transfers between devices with their start and end apart: 11, of which 9 were waited for; matrix products, arithmetic and copies ran while one was open for 7% of the time, Pallas kernels for 0%

commit v1 on v0

v1 whole, which is shorter than its diff:
```python
import functools
import math

import jax
import jax.numpy as jnp
import ml_dtypes
import numpy as np
from jax import lax
from jax.experimental import pallas as pl
from jax.experimental.pallas import tpu as pltpu
from jax.sharding import Mesh
from jax.sharding import PartitionSpec as P

D = 768
T = 512
H = T // 2
C = 384
FH = 1536
EPSILON = 1e-05
HIGH = lax.Precision.HIGHEST
F32 = jnp.float32
BF = jnp.bfloat16
VMEM_LIMIT = 56 * 2**20

ORDER = np.concatenate([np.arange(0, T, 2), np.arange(1, T, 2)])


def split_table(t):
    hi = t.astype(ml_dtypes.bfloat16)
    lo = (t - hi.astype(np.float64)).astype(ml_dtypes.bfloat16)
    return hi, lo


def wave_tables():
    n = np.arange(H)
    even = 2 * math.pi * (np.outer(n, 2 * n) % (2 * T)) / (2 * T)
    odd = 2 * math.pi * (np.outer(n, 2 * n + 1) % (2 * T)) / (2 * T)
    alt = np.where(n % 2 == 0, 1.0, -1.0)
    out = []
    for ang in (even, odd):
        co, si = np.cos(ang), np.sin(ang)
        si[0] = alt
        hi, lo = split_table(np.concatenate([co, si], 0))
        out.append(np.concatenate([hi, lo, hi], 1))
        hi, lo = split_table(np.concatenate([co.T, si.T], 1))
        out.append(np.concatenate([hi, lo, hi], 1))
    fe, ie, fo, io = out
    return fe, fo, ie, io


FE, FO, IE, IO = wave_tables()


def dot(a, b):
    return lax.dot_general(a, b, (((1,), (0,)), ((), ())), preferred_element_type=F32)


def dot_nt(a, b):
    return lax.dot_general(a, b, (((1,), (1,)), ((), ())), preferred_element_type=F32)


def dot_tn(a, b):
    return lax.dot_general(a, b, (((0,), (0,)), ((), ())), preferred_element_type=F32)


def normalize(x):
    mean = jnp.mean(x, -1, keepdims=True)
    scale = lax.rsqrt(jnp.mean(x * x, -1, keepdims=True) - mean * mean + EPSILON)
    return (x - mean) * scale, scale


def norm_pull(dn, x, gain):
    xhat, scale = normalize(x)
    ds = dn * gain
    first = jnp.mean(ds, -1, keepdims=True)
    second = jnp.mean(ds * xhat, -1, keepdims=True)
    return scale * (ds - first - xhat * second), dn * xhat


def row_mask(start, rows, length):
    r = start + lax.broadcasted_iota(jnp.int32, (rows, 1), 0)
    slot = jnp.where(r < H, 2 * r, 2 * (r - H) + 1)
    return (slot < length).astype(F32)


def down_one(x):
    r = lax.broadcasted_iota(jnp.int32, x.shape, 0)
    return jnp.where(r == 0, 0.0, pltpu.roll(x, 1, 0))


def up_one(x):
    r = lax.broadcasted_iota(jnp.int32, x.shape, 0)
    return jnp.where(r == x.shape[0] - 1, 0.0, pltpu.roll(x, x.shape[0] - 1, 0))


def put_split(ref, value, rows, lanes):
    hi = value.astype(BF)
    lo = (value - hi.astype(F32)).astype(BF)
    step = ref.shape[0] // 3
    ref[pl.ds(rows, value.shape[0]), lanes] = hi
    ref[pl.ds(step + rows, value.shape[0]), lanes] = hi
    ref[pl.ds(2 * step + rows, value.shape[0]), lanes] = lo


def top_row(shape):
    return lax.broadcasted_iota(jnp.int32, shape, 0) == 0


def butterfly(even, odd, lanes):
    ce, se = even[pl.ds(0, H), lanes], even[pl.ds(H, H), lanes]
    co, so = odd[pl.ds(0, H), lanes], odd[pl.ds(H, H), lanes]
    top = top_row(ce.shape)
    return ce + co, ce - co, jnp.where(top, se, se + so), jnp.where(top, so, se - so)


def spectrum_product(a, k, conj):
    a1, a2, b1, b2 = a
    k1, k2, l1, l2 = k
    top = top_row(a1.shape)
    aa, bb, cc, dd = a1 * k1, b1 * l1, a2 * k2, b2 * l2
    if conj:
        y1 = jnp.where(top, aa, aa + bb)
        y2 = jnp.where(top, cc, cc + dd)
        m1 = jnp.where(top, bb + dd, b1 * k1 - a1 * l1)
        m2 = jnp.where(top, b2 * l1 - b1 * l2, b2 * k2 - a2 * l2)
    else:
        y1 = jnp.where(top, aa, aa - bb)
        y2 = jnp.where(top, cc, cc - dd)
        m1 = jnp.where(top, bb - dd, a1 * l1 + b1 * k1)
        m2 = jnp.where(top, b1 * l2 + b2 * l1, a2 * l2 + b2 * k2)
    return y1, y2, m1, m2


def put_inverse(rhs_e, rhs_o, y, lanes):
    y1, y2, m1, m2 = y
    top = top_row(y1.shape)
    unit = 1.0 / T
    w = jnp.where(top, 0.5 * unit, unit)
    put_split(rhs_e, (y1 + y2) * w, 0, lanes)
    put_split(rhs_o, (y1 - y2) * w, 0, lanes)
    put_split(rhs_e, jnp.where(top, m1, m1 + m2) * unit, H, lanes)
    put_split(rhs_o, jnp.where(top, m2, m1 - m2) * unit, H, lanes)


def lanes_of(block):
    return pl.ds(block * 128, 128)


def short_conv(u_ref, sw_ref, sb_ref, block):
    out = []
    for s in range(3):
        at = lanes_of(s * (C // 128) + block)
        ue, uo = u_ref[pl.ds(0, H), at], u_ref[pl.ds(H, H), at]
        t0, t1, t2 = (sw_ref[j : j + 1, at] for j in range(3))
        bias = sb_ref[0:1, at]
        uo_d = down_one(uo)
        we = t2 * ue + t1 * uo_d + t0 * down_one(ue) + bias
        wo = t2 * uo + t1 * ue + t0 * uo_d + bias
        out.append((we, wo))
    return out


def filter_spectrum(k_ref, fe_ref, fo_ref, out_ref, rhs_e, rhs_o, se, so):
    for b in range(C // 128):
        at = lanes_of(b)
        put_split(rhs_e, k_ref[0, pl.ds(0, H), at], 0, at)
        put_split(rhs_o, k_ref[0, pl.ds(H, H), at], 0, at)
    se[...] = dot(fe_ref[...], rhs_e[...])
    so[...] = dot(fo_ref[...], rhs_o[...])
    for b in range(C // 128):
        at = lanes_of(b)
        for i, v in enumerate(butterfly(se, so, at)):
            out_ref[0, i, :, at] = v


def add_branch(x_ref, own_ref, other_ref, vec_ref, row, length, start, rows):
    at = pl.ds(start, rows)
    y = own_ref[at, :].astype(F32) + other_ref[at, :].astype(F32) + vec_ref[row : row + 1, :]
    return x_ref[at, :] + row_mask(start, rows, length) * y


RB = 128


def row_loop(body, init=0):
    def step(i, c):
        return body(pl.multiple_of(i * RB, RB), c)

    return lax.fori_loop(0, T // RB, step, init)


def mixer_forward(joined, *refs):
    if joined:
        len_ref, x_ref, own_ref, other_ref, prev_ref = refs[:5]
        refs = refs[5:]
    else:
        x_ref = refs[0]
        refs = refs[1:]
    (vec_ref, inw_ref, inb_ref, sw_ref, sb_ref, ks_ref, skip_ref, fe_ref, fo_ref, ie_ref, io_ref, outw_ref) = refs[:12]
    refs = refs[12:]
    if joined:
        xo_ref = refs[0]
        refs = refs[1:]
    u_ref, qs_ref, g_ref, p_ref, a_s, w0_s, q_s, rhs_e, rhs_o, se, so, rhs2_e, rhs2_o, z_s = refs

    def first(start, c):
        at = pl.ds(start, RB)
        if joined:
            x = add_branch(x_ref, own_ref, other_ref, prev_ref, 5, len_ref[0], start, RB)
            xo_ref[at, :] = x
        else:
            x = x_ref[at, :]
        xhat, _ = normalize(x)
        a_s[at, :] = (xhat * vec_ref[0:1, :] + vec_ref[1:2, :]).astype(BF)
        return c

    row_loop(first)
    for s in range(3):
        at = pl.ds(s * C, C)
        u_ref[:, at] = dot(a_s[...], inw_ref[s]) + inb_ref[0:1, at]
    for b in range(C // 128):
        at = lanes_of(b)
        (w0e, w0o), (w1e, w1o), (w2e, w2o) = short_conv(u_ref, sw_ref, sb_ref, b)
        w0_s[pl.ds(0, H), at] = w0e
        w0_s[pl.ds(H, H), at] = w0o
        qe, qo = w2e * w1e, w2o * w1o
        q_s[pl.ds(0, H), at] = qe
        q_s[pl.ds(H, H), at] = qo
        put_split(rhs_e, qe, 0, at)
        put_split(rhs_o, qo, 0, at)
    se[...] = dot(fe_ref[...], rhs_e[...])
    so[...] = dot(fo_ref[...], rhs_o[...])
    for b in range(C // 128):
        at = lanes_of(b)
        spec = butterfly(se, so, at)
        for i, v in enumerate(spec):
            qs_ref[i, :, at] = v
        y = spectrum_product(spec, [ks_ref[0, i, :, at] for i in range(4)], False)
        put_inverse(rhs2_e, rhs2_o, y, at)
    se[pl.ds(0, H), :] = dot(ie_ref[...], rhs2_e[...])
    se[pl.ds(H, H), :] = dot(io_ref[...], rhs2_o[...])

    def last(start, c):
        at = pl.ds(start, RB)
        g = se[at, :] + skip_ref[0:1, :] * q_s[at, :]
        g_ref[at, :] = g
        z_s[at, :] = (g * w0_s[at, :]).astype(BF)
        return c

    row_loop(last)
    p_ref[...] = dot(z_s[...], outw_ref[...]).astype(BF)


def gelu_parts(h):
    c0 = math.sqrt(2 / math.pi)
    hh = h * h
    t = jnp.tanh(c0 * (h + 0.044715 * (hh * h)))
    half = 0.5 * (1.0 + t)
    return half, t, hh, c0


def ff_forward(len_ref, x_ref, own_ref, other_ref, vec_ref, up_ref, upb_ref, dn_ref, xo_ref, h_ref, p_ref, b_s, acc):
    j = pl.program_id(0)

    @pl.when(j == 0)
    def _():
        def first(start, c):
            at = pl.ds(start, RB)
            x = add_branch(x_ref, own_ref, other_ref, vec_ref, 4, len_ref[0], start, RB)
            xo_ref[at, :] = x
            xhat, _ = normalize(x)
            b_s[at, :] = (xhat * vec_ref[2:3, :] + vec_ref[3:4, :]).astype(BF)
            return c

        row_loop(first)

    h = dot(b_s[...], up_ref[...]) + upb_ref[...]
    h_ref[...] = h
    half, _, _, _ = gelu_parts(h)
    part = dot((h * half).astype(BF), dn_ref[...])

    @pl.when(j == 0)
    def _():
        acc[...] = part

    @pl.when(j > 0)
    def _():
        acc[...] += part

    @pl.when(j == pl.num_programs(0) - 1)
    def _():
        p_ref[...] = acc[...].astype(BF)


def ff_backward(joined, *refs):
    len_ref, g_ref = refs[:2]
    refs = refs[2:]
    if joined:
        own_ref, other_ref, xn_ref, nvec_ref = refs[:4]
        refs = refs[4:]
    x_ref, h_ref, vec_ref, up_ref, dn_ref = refs[:5]
    refs = refs[5:]
    if joined:
        go_ref, ngrad_ref = refs[:2]
        refs = refs[2:]
    gup_ref, gdn_ref, gupb_ref, gdnb_ref, p_ref, dm_s, b_s, acc = refs
    j = pl.program_id(0)

    @pl.when(j == 0)
    def _():
        def first(start, c):
            at = pl.ds(start, RB)
            g = g_ref[at, :].astype(F32)
            sums, s1, s2 = c
            if joined:
                dn = own_ref[at, :].astype(F32) + other_ref[at, :].astype(F32)
                dx, dg = norm_pull(dn, xn_ref[at, :], nvec_ref[0:1, :])
                g = g + dx
                go_ref[at, :] = g
                s1 = s1 + jnp.sum(dg, 0, keepdims=True)
                s2 = s2 + jnp.sum(dn, 0, keepdims=True)
            dm = (row_mask(start, RB, len_ref[0]) * g).astype(BF)
            dm_s[at, :] = dm
            xhat, _ = normalize(x_ref[at, :])
            b_s[at, :] = (xhat * vec_ref[2:3, :] + vec_ref[3:4, :]).astype(BF)
            return sums + jnp.sum(dm.astype(F32), 0, keepdims=True), s1, s2

        zero = jnp.zeros((1, D), F32)
        sums, s1, s2 = row_loop(first, (zero, zero, zero))
        gdnb_ref[...] = sums
        if joined:
            ngrad_ref[0:1, :] = s1
            ngrad_ref[1:2, :] = s2

    h = h_ref[...]
    half, t, hh, c0 = gelu_parts(h)
    e = (h * half).astype(BF)
    slope = half + 0.5 * c0 * h * (1.0 - t * t) * (1.0 + 3 * 0.044715 * hh)
    dh = (dot_nt(dm_s[...], dn_ref[...]) * slope).astype(BF)
    gupb_ref[...] = jnp.sum(dh.astype(F32), 0, keepdims=True)
    part = dot_nt(dh, up_ref[...])
    gdn_ref[...] = dot_tn(e, dm_s[...]).astype(BF)
    gup_ref[...] = dot_tn(b_s[...], dh).astype(BF)

    @pl.when(j == 0)
    def _():
        acc[...] = part

    @pl.when(j > 0)
    def _():
        acc[...] += part

    @pl.when(j == pl.num_programs(0) - 1)
    def _():
        p_ref[...] = acc[...].astype(BF)


def mixer_backward(
    len_ref, g_in_ref, own_ref, other_ref, x1_ref, x0_ref, u_ref, qs_ref, g_ref, ks_ref, vec_ref, inw_ref, outw_ref,
    sw_ref, sb_ref, skip_ref, fe_ref, fo_ref, ie_ref, io_ref,
    go_ref, ngrad_ref, goutw_ref, goutb_ref, ginw_ref, ginb_ref, gsw_ref, gsb_ref, gskip_ref, dk_ref, p_ref,
    dy_s, a_s, dz_s, z_s, dg_s, w1_s, w2_s, dw0_s, rhs_e, rhs_o, se, so, rhs2_e, rhs2_o, inv_s, du_s,
):
    def first(start, c):
        at = pl.ds(start, RB)
        sums, s1, s2 = c
        dn = own_ref[at, :].astype(F32) + other_ref[at, :].astype(F32)
        dx, dg = norm_pull(dn, x1_ref[at, :], vec_ref[2:3, :])
        g = g_in_ref[at, :].astype(F32) + dx
        go_ref[at, :] = g
        dy = (row_mask(start, RB, len_ref[0]) * g).astype(BF)
        dy_s[at, :] = dy
        xhat, _ = normalize(x0_ref[at, :])
        a_s[at, :] = (xhat * vec_ref[0:1, :] + vec_ref[1:2, :]).astype(BF)
        return (
            sums + jnp.sum(dy.astype(F32), 0, keepdims=True),
            s1 + jnp.sum(dg, 0, keepdims=True),
            s2 + jnp.sum(dn, 0, keepdims=True),
        )

    zero = jnp.zeros((1, D), F32)
    sums, s1, s2 = row_loop(first, (zero, zero, zero))
    goutb_ref[...] = sums
    ngrad_ref[0:1, :] = s1
    ngrad_ref[1:2, :] = s2
    dz_s[...] = dot_nt(dy_s[...], outw_ref[...])
    halves = (pl.ds(0, H), pl.ds(H, H))
    for b in range(C // 128):
        at = lanes_of(b)
        w0, w1, w2 = short_conv(u_ref, sw_ref, sb_ref, b)
        dskip = 0.0
        for i, (rows, rhs) in enumerate(zip(halves, (rhs_e, rhs_o))):
            dz, g = dz_s[rows, at], g_ref[rows, at]
            z_s[rows, at] = (g * w0[i]).astype(BF)
            dw0_s[rows, at] = dz * g
            dg = dz * w0[i]
            dg_s[rows, at] = dg
            dskip = dskip + jnp.sum(dg * (w2[i] * w1[i]), 0, keepdims=True)
            w1_s[rows, at] = w1[i]
            w2_s[rows, at] = w2[i]
            put_split(rhs, dg, 0, at)
        gskip_ref[0:1, at] = dskip
    se[...] = dot(fe_ref[...], rhs_e[...])
    so[...] = dot(fo_ref[...], rhs_o[...])
    for b in range(C // 128):
        at = lanes_of(b)
        spec = butterfly(se, so, at)
        put_inverse(rhs2_e, rhs2_o, spectrum_product(spec, [ks_ref[0, i, :, at] for i in range(4)], True), at)
        put_inverse(rhs2_e, rhs2_o, spectrum_product(spec, [qs_ref[i, :, at] for i in range(4)], True), pl.ds(C + b * 128, 128))
    inv_s[pl.ds(0, H), :] = dot(ie_ref[...], rhs2_e[...])
    inv_s[pl.ds(H, H), :] = dot(io_ref[...], rhs2_o[...])
    dk_ref[...] = inv_s[:, pl.ds(C, C)]
    for b in range(C // 128):
        at = lanes_of(b)
        dw = [[dw0_s[rows, at] for rows in halves], [], []]
        for rows in halves:
            dq = inv_s[rows, at] + skip_ref[0:1, at] * dg_s[rows, at]
            dw[1].append(dq * w2_s[rows, at])
            dw[2].append(dq * w1_s[rows, at])
        for s in range(3):
            to = lanes_of(s * (C // 128) + b)
            ue, uo = u_ref[halves[0], to], u_ref[halves[1], to]
            t0, t1, t2 = (sw_ref[j : j + 1, to] for j in range(3))
            de, do = dw[s]
            de_u, do_u = up_one(de), up_one(do)
            due = (t2 * de + t1 * do + t0 * de_u).astype(BF)
            duo = (t2 * do + t1 * de_u + t0 * do_u).astype(BF)
            du_s[halves[0], to] = due
            du_s[halves[1], to] = duo
            uo_d = down_one(uo)
            gsw_ref[0:1, to] = jnp.sum(de * down_one(ue) + do * uo_d, 0, keepdims=True)
            gsw_ref[1:2, to] = jnp.sum(de * uo_d + do * ue, 0, keepdims=True)
            gsw_ref[2:3, to] = jnp.sum(de * ue + do * uo, 0, keepdims=True)
            gsb_ref[0:1, to] = jnp.sum(de + do, 0, keepdims=True)
            ginb_ref[0:1, to] = jnp.sum(due.astype(F32) + duo.astype(F32), 0, keepdims=True)
    part = dot_nt(du_s[:, pl.ds(0, C)], inw_ref[0])
    for s in range(1, 3):
        part += dot_nt(du_s[:, pl.ds(s * C, C)], inw_ref[s])
    p_ref[...] = part.astype(BF)
    goutw_ref[...] = dot_tn(z_s[...], dy_s[...]).astype(BF)
    for s in range(3):
        ginw_ref[s] = dot_tn(a_s[...], du_s[:, pl.ds(s * C, C)]).astype(BF)


def sds(shape, dtype=F32):
    return jax.ShapeDtypeStruct(shape, dtype)


def params(flops, nbytes):
    return dict(
        compiler_params=pltpu.CompilerParams(vmem_limit_bytes=VMEM_LIMIT),
        cost_estimate=pl.CostEstimate(flops=int(flops), bytes_accessed=int(nbytes), transcendentals=0),
    )


SMEM = pl.BlockSpec(memory_space=pltpu.SMEM)
WHOLE = pl.BlockSpec(memory_space=pltpu.VMEM)


def spectrum_scratch():
    return [pltpu.VMEM((3 * H, C), BF)] * 2 + [pltpu.VMEM((T, C), F32)] * 2


def run_filter_spectrum(kernels):
    layers = kernels.shape[0]
    fixed = lambda shape: pl.BlockSpec(shape, lambda l: (0,) * len(shape))
    return pl.pallas_call(
        filter_spectrum,
        grid=(layers,),
        in_specs=[pl.BlockSpec((1, T, C), lambda l: (l, 0, 0)), fixed(FE.shape), fixed(FO.shape)],
        out_specs=pl.BlockSpec((1, 4, H, C), lambda l: (l, 0, 0, 0)),
        out_shape=sds((layers, 4, H, C)),
        scratch_shapes=spectrum_scratch(),
        name="filter_spectrum",
        **params(2e9, 8e6),
    )(kernels, FE, FO)


def run_mixer_forward(joint, x, vec, inw, inb, sw, sb, ks, skip, outw):
    joined = joint is not None
    args = ([joint[0], x, joint[1], joint[2], joint[3]] if joined else [x]) + [
        vec, inw, inb, sw, sb, ks, skip, FE, FO, IE, IO, outw]
    outs = ([sds((T, D))] if joined else []) + [sds((T, 3 * C)), sds((4, H, C)), sds((T, C)), sds((T, D), BF)]
    return pl.pallas_call(
        functools.partial(mixer_forward, joined),
        in_specs=([SMEM] if joined else []) + [WHOLE] * (len(args) - joined),
        out_specs=[WHOLE] * len(outs),
        out_shape=outs,
        scratch_shapes=[pltpu.VMEM((T, D), BF), pltpu.VMEM((T, C), F32), pltpu.VMEM((T, C), F32)]
        + spectrum_scratch()
        + [pltpu.VMEM((6 * H, C), BF)] * 2
        + [pltpu.VMEM((T, C), BF)],
        name="mixer_forward",
        **params(6e9, 1.2e7),
    )(*args)


FC = 512


def run_ff_forward(length, x, own, other, vec, up, upb, dn):
    fixed = lambda shape: pl.BlockSpec(shape, lambda j: (0,) * len(shape))
    return pl.pallas_call(
        ff_forward,
        grid=(FH // FC,),
        in_specs=[
            SMEM, fixed((T, D)), fixed((T, D)), fixed((T, D)), fixed(vec.shape),
            pl.BlockSpec((D, FC), lambda j: (0, j)),
            pl.BlockSpec((1, FC), lambda j: (0, j)),
            pl.BlockSpec((FC, D), lambda j: (j, 0)),
        ],
        out_specs=[fixed((T, D)), pl.BlockSpec((T, FC), lambda j: (0, j)), fixed((T, D))],
        out_shape=[sds((T, D)), sds((T, FH)), sds((T, D), BF)],
        scratch_shapes=[pltpu.VMEM((T, D), BF), pltpu.VMEM((T, D), F32)],
        name="ff_forward",
        **params(5e9, 1.2e7),
    )(length, x, own, other, vec, up, upb, dn)


def run_ff_backward(length, g, joint, x, h, vec, up, dn):
    joined = joint is not None
    fixed = lambda shape: pl.BlockSpec(shape, lambda j: (0,) * len(shape))
    args = [length, g] + (list(joint) if joined else []) + [x, h, vec, up, dn]
    in_specs = [SMEM, fixed((T, D))]
    if joined:
        in_specs += [fixed((T, D))] * 3 + [fixed(joint[3].shape)]
    in_specs += [
        fixed((T, D)),
        pl.BlockSpec((T, FC), lambda j: (0, j)),
        fixed(vec.shape),
        pl.BlockSpec((D, FC), lambda j: (0, j)),
        pl.BlockSpec((FC, D), lambda j: (j, 0)),
    ]
    out_specs = [fixed((T, D)), fixed((2, D))] if joined else []
    outs = [sds((T, D)), sds((2, D))] if joined else []
    out_specs += [
        pl.BlockSpec((D, FC), lambda j: (0, j)),
        pl.BlockSpec((FC, D), lambda j: (j, 0)),
        pl.BlockSpec((1, FC), lambda j: (0, j)),
        fixed((1, D)),
        fixed((T, D)),
    ]
    outs += [sds((D, FH), BF), sds((FH, D), BF), sds((1, FH)), sds((1, D)), sds((T, D), BF)]
    return pl.pallas_call(
        functools.partial(ff_backward, joined),
        grid=(FH // FC,),
        in_specs=in_specs,
        out_specs=out_specs,
        out_shape=outs,
        scratch_shapes=[pltpu.VMEM((T, D), BF), pltpu.VMEM((T, D), BF), pltpu.VMEM((T, D), F32)],
        name="ff_backward",
        **params(1e10, 2e7),
    )(*args)


def run_mixer_backward(length, g_in, own, other, x1, x0, u, qs, g, ks, vec, inw, outw, sw, sb, skip):
    args = [length, g_in, own, other, x1, x0, u, qs, g, ks, vec, inw, outw, sw, sb, skip, FE, FO, IE, IO]
    outs = [
        sds((T, D)), sds((2, D)), sds((C, D), BF), sds((1, D)), sds((3, D, C), BF), sds((1, 3 * C)),
        sds((3, 3 * C)), sds((1, 3 * C)), sds((1, C)), sds((T, C)), sds((T, D), BF),
    ]
    tc = pltpu.VMEM((T, C), F32)
    return pl.pallas_call(
        mixer_backward,
        in_specs=[SMEM] + [WHOLE] * (len(args) - 1),
        out_specs=[WHOLE] * len(outs),
        out_shape=outs,
        scratch_shapes=[
            pltpu.VMEM((T, D), BF), pltpu.VMEM((T, D), BF), tc, pltpu.VMEM((T, C), BF), tc, tc, tc, tc,
            *spectrum_scratch(),
            pltpu.VMEM((6 * H, 2 * C), BF), pltpu.VMEM((6 * H, 2 * C), BF),
            pltpu.VMEM((T, 2 * C), F32), pltpu.VMEM((T, 3 * C), BF),
        ],
        name="mixer_backward",
        **params(1e10, 2e7),
    )(*args)


def positions(length, emb):
    bands = (emb - 1) // 2
    steps = jnp.asarray(ORDER, jnp.float32)
    times = steps / (length - 1)
    freqs = 0.0001 + (bands - 1 - 0.0001) * jnp.arange(bands, dtype=jnp.float32) / (bands - 1)
    angle = 2 * math.pi * steps[:, None] * freqs[None, :] / length
    feats = jnp.concatenate([times[:, None], jnp.cos(angle), -jnp.sin(angle)], 1)
    return (feats, times)


def decay_rates(channel, width):
    slow = math.log(0.01) / 1.5
    fast = math.log(0.01) / 0.3
    return jnp.abs(slow + (fast - slow) * channel.astype(jnp.float32) / (width - 1))


def filter_net(first_w, inner_w, biases, out_w, feats, decay):
    hidden = jnp.sin(jnp.dot(feats, first_w, precision=HIGH) + biases[0])
    hidden = jnp.sin(jnp.dot(hidden, inner_w[0], precision=HIGH) + biases[1])
    hidden = jnp.sin(jnp.dot(hidden, inner_w[1], precision=HIGH) + biases[2])
    return jnp.dot(hidden, out_w, precision=HIGH) * decay


SWAP = [(0, 1), (1, 0)]
PLANE = ("y", "x")


def swap(x, axis):
    return lax.ppermute(x, axis, SWAP)


def in_order(mine, own, other, axis):
    low = mine == 0
    return jnp.concatenate([jnp.where(low, own, other), jnp.where(low, other, own)], axis)


def total(part, core, axis=0):
    half = part.shape[axis] // 2
    keep = lax.dynamic_slice_in_dim(part, core * half, half, axis)
    give = lax.dynamic_slice_in_dim(part, (1 - core) * half, half, axis)
    mine = (keep.astype(F32) + swap(give, "c").astype(F32)).astype(part.dtype)
    mine = lax.psum_scatter(mine, PLANE, scatter_dimension=0, tiled=True)
    mine = (mine.astype(F32) + swap(mine, "zl").astype(F32)).astype(part.dtype)
    mine = lax.all_gather(mine, PLANE, axis=0, tiled=True)
    return in_order(core, mine, swap(mine, "c"), axis).astype(F32)


def shards(
    tokens, lengths, norm_gain, norm_bias, in_weight, in_bias, short_weight, short_bias, filter_first, filter_inner,
    filter_biases, filter_out, filter_skip, out_weight, out_bias, up_weight, up_bias, down_weight, down_bias, cotangent,
):
    layers = norm_gain.shape[0]
    half_at = lax.axis_index("zh")
    core = lax.axis_index("c")

    tokens_other = swap(tokens, "zh")
    rows = jnp.concatenate(
        [norm_gain[:, 0], norm_bias[:, 0], norm_gain[:, 1], norm_bias[:, 1], out_bias, down_bias], 0
    )
    rows = in_order(half_at, rows, swap(rows, "zh"), 1).reshape(6, layers, D)
    vecs = [jnp.pad(rows[:, l], ((0, 2), (0, 0))) for l in range(layers)]
    cot_other = swap(cotangent, "zh")

    def by_parity(x):
        return x.reshape(H, 2, D).transpose(1, 0, 2).reshape(T, D)

    def by_slot(x):
        return x.reshape(2, H, -1).transpose(1, 0, 2).reshape(T, -1)

    x = by_parity(in_order(half_at, tokens, tokens_other, 1)).astype(F32)

    feats, times = positions(T, filter_first.shape[1])
    channel = half_at * C + jnp.arange(C, dtype=jnp.int32)
    decay = jnp.exp(-times[:, None] * decay_rates(channel, D)[None, :]) + 0.05
    nets, pulls = [], []
    for l in range(layers):
        k, pull = jax.vjp(
            lambda a, b, c, d: filter_net(a, b, c, d, feats, decay),
            filter_first[l], filter_inner[l], filter_biases[l], filter_out[l],
        )
        nets.append(k)
        pulls.append(pull)
    spectra = run_filter_spectrum(jnp.stack(nets))

    inw = in_weight.transpose(0, 2, 1, 3)
    inb = in_bias.reshape(layers, 1, 3 * C)
    sw = short_weight.reshape(layers, 3, 3 * C)
    sb = short_bias.reshape(layers, 1, 3 * C)
    skip = filter_skip.reshape(layers, 1, C)
    upb = up_bias.reshape(layers, 1, FH)
    ks = [spectra[l : l + 1] for l in range(layers)]

    saved = []
    joint = None
    for l in range(layers):
        made = run_mixer_forward(joint, x, vecs[l], inw[l], inb[l], sw[l], sb[l], ks[l], skip[l], out_weight[l])
        if joint is not None:
            x, made = made[0], made[1:]
        u, qs, g, p = made
        x1, h, p2 = run_ff_forward(lengths, x, p, swap(p, "zh"), vecs[l], up_weight[l], upb[l], down_weight[l])
        saved.append((x, u, qs, g, x1, h))
        p2_other = swap(p2, "zh")
        joint = (lengths, p2, p2_other, vecs[l])
        x = x1

    def my_half(x):
        return lax.dynamic_slice_in_dim(x, half_at * C, C, 1)

    slot = jnp.asarray(ORDER, jnp.int32)[:, None]
    mask = (slot < lengths[0]).astype(F32)
    y = my_half(joint[1]).astype(F32) + my_half(joint[2]).astype(F32) + down_bias[layers - 1]
    result = by_slot((my_half(x) + mask * y).astype(BF))

    grad = by_parity(in_order(half_at, cotangent, cot_other, 1))
    joint = None
    big = [None] * layers
    small = [None] * layers
    norms = {}
    for l in reversed(range(layers)):
        x0, u, qs, g, x1, h = saved[l]
        made = run_ff_backward(lengths, grad, joint, x1, h, vecs[l], up_weight[l], down_weight[l])
        if joint is not None:
            grad, norms[l + 1, 0] = made[:2]
            made = made[2:]
        gup, gdn, gupb, gdnb, p = made
        made = run_mixer_backward(
            lengths, grad, p, swap(p, "zh"), x1, x0, u, qs, g, ks[l], vecs[l], inw[l], out_weight[l], sw[l], sb[l], skip[l]
        )
        grad, norms[l, 1], goutw, goutb, ginw, ginb, gsw, gsb, gskip, dk, p = made
        joint = (p, swap(p, "zh"), x0, vecs[l])
        big[l] = [total(gup, core), total(gdn, core), total(goutw, core, 1)]
        big[l].append(total(ginw.reshape(3 * D, C), core).reshape(3, D, C))
        gfilter = pulls[l](dk)
        small[l] = (gupb, gdnb, goutb, ginb, gsw, gsb, gskip, gfilter)

    own, other, x0, vec = joint
    dn = own.astype(F32) + other.astype(F32)
    dx, dg = norm_pull(dn, x0, vec[0:1])
    grad = by_slot(my_half(grad + dx))
    norms[0, 0] = jnp.stack([jnp.sum(dg, 0), jnp.sum(dn, 0)])

    pieces = []
    for l in range(layers):
        gupb, gdnb, goutb, ginb, gsw, gsb, gskip, gfilter = small[l]
        pieces += [
            my_half(norms[l, 0]), my_half(norms[l, 1]), my_half(gdnb), my_half(goutb), gupb.reshape(4, C),
            ginb.reshape(3, C), gsw.reshape(9, C), gsb.reshape(3, C), gskip, gfilter[3],
        ]
    shared = jnp.concatenate([m.reshape(-1) for l in range(layers) for m in small[l][7][:3]])
    n_shared = shared.shape[0]
    shared = jnp.pad(shared, (0, -n_shared % C)).reshape(-1, C)
    pack = jnp.concatenate(pieces, 0)
    n_rows = pack.shape[0]
    pack = jnp.concatenate([pack, shared], 0)
    pack = total(jnp.pad(pack, ((0, -pack.shape[0] % 32), (0, 0))), core)
    shared = pack[n_rows : n_rows + shared.shape[0]]
    shared = (shared + swap(shared, "zh")).reshape(-1)[:n_shared].reshape(layers, -1)
    pack = pack[:n_rows].reshape(layers, -1, C)
    n0 = filter_first[0].size
    n1 = filter_inner[0].size
    g_first = shared[:, :n0].reshape(filter_first.shape)
    g_inner = shared[:, n0 : n0 + n1].reshape(filter_inner.shape)
    g_fbias = shared[:, n0 + n1 :].reshape(filter_biases.shape)

    def stack(i):
        return jnp.stack([big[l][i] for l in range(layers)])

    return (
        result,
        grad,
        pack[:, 0:4:2],
        pack[:, 1:4:2],
        stack(3).transpose(0, 2, 1, 3),
        pack[:, 10:13],
        pack[:, 13:22].reshape(short_weight.shape),
        pack[:, 22:25],
        g_first,
        g_inner,
        g_fbias,
        pack[:, 26:90],
        pack[:, 25],
        stack(2),
        pack[:, 5],
        stack(0),
        pack[:, 6:10].reshape(layers, FH),
        stack(1),
        pack[:, 4],
    )


def solution(mesh):
    names = ("zl", "y", "x", "c", "zh")
    fine = Mesh(mesh.devices.reshape(2, 4, 4, 2, 2), names)
    dp = ("zl", "y", "x", "c")
    rows = P(dp, "zh")
    third, fourth = P(None, None, "zh"), P(None, None, None, "zh")
    second, middle = P(None, "zh"), P(None, "zh", None)
    placed = (
        rows, P(dp), third, third, fourth, third, fourth, third, P(), P(), P(), third, second, middle, second, third,
        second, middle, second, rows,
    )
    return jax.shard_map(
        shards,
        mesh=fine,
        in_specs=placed,
        out_specs=(
            rows, rows, third, third, fourth, third, fourth, third, P(), P(), P(), third, second, middle, second, third,
            second, middle, second,
        ),
        check_vma=False,
    )
```

time: 1910 us -> 1080 us (0.57)
  waiting for transfers between devices: 1310 us -> 620 us
  matrix products: 252 us -> 22.8 us
  Pallas kernels: 0 us -> 113 us
  starting transfers between devices: 1.04 us -> 80.3 us
  blocking collectives: 132 us -> 94.5 us
  local copies, waits for them, and re-layouts: 98.3 us -> 66.3 us
  other arithmetic: 84.1 us -> 58.4 us
    psum x3 -> x0, waiting for transfers between devices: 1250 us -> none  [the longest x2 1110 us: shards(): lax.psum((stacked[0], stacked[1], stacked[2], stacked[3], stacked[4], sta...]
    dot_general x70 -> x22, matrix products: 252 us -> 22.8 us  [the longest x6 7.52 us: filter_net(): return jnp.dot(hidden, out_w, precision=HIGH) * decay]
    unnamed x19 -> x20, waiting for transfers between devices: 62.1 us -> 288 us
    all_gather x0 -> x4, waiting for transfers between devices: none -> 164 us  [total(): mine = lax.all_gather(mine, PLANE, axis=0, tiled=True)]
    ppermute x0 -> x39, waiting for transfers between devices: none -> 126 us  [swap(): return lax.ppermute(x, axis, SWAP)]
    pallas_call x0 -> x9, Pallas kernels: none -> 113 us  [the longest x2 36.4 us: run_mixer_backward(): pl.pallas_call(mixer_backward, in_specs=[SMEM] + [WHOLE] * (len(args) - 1...]
    ppermute x0 -> x39, starting transfers between devices: none -> 79.6 us  [swap(): return lax.ppermute(x, axis, SWAP)]
    unnamed x494 -> x197, local copies, waits for them, and re-layouts: 68.5 us -> 10.4 us
  transfers between devices with their start and end apart: 11 -> 52, of which waited for: 9 -> 26; matrix products, arithmetic and copies ran while one was open for 7% -> 12% of each run, Pallas kernels for 0% -> 5%
where the time goes in v1:
time: 1080 us; the launch traced here: 1070 us
  waiting for transfers between devices  620 us (57%)
  Pallas kernels  113 us (10%)
  blocking collectives  94.5 us (9%)
  starting transfers between devices  80.3 us (7%)
  local copies, waits for them, and re-layouts  66.3 us (6%)
  other arithmetic  58.4 us (5%)
  matrix products  22.8 us (2%)
  between operations  17 us (2%)
    unnamed x20, waiting for transfers between devices  288 us
    all_gather x4, waiting for transfers between devices, total(): mine = lax.all_gather(mine, PLANE, axis=0, tiled=True)  164 us
    ppermute x39, waiting for transfers between devices, swap(): return lax.ppermute(x, axis, SWAP)  126 us
    all_gather x5, blocking collectives, total(): mine = lax.all_gather(mine, PLANE, axis=0, tiled=True)  94.5 us
    ppermute x39, starting transfers between devices, swap(): return lax.ppermute(x, axis, SWAP)  79.6 us
    reduce_scatter x2, waiting for transfers between devices, total(): mine = lax.psum_scatter(mine, PLANE, scatter_dimension=0, tiled=True)  42.5 us
    pallas_call x2, Pallas kernels, run_mixer_backward(): pl.pallas_call(mixer_backward, in_specs=[SMEM] + [WHOLE] * (len(args) - 1...  36.4 us
    pallas_call x2, Pallas kernels, run_ff_backward(): pl.pallas_call(functools.partial(ff_backward, joined), grid=(FH // FC,),...  28.2 us
  transfers between devices with their start and end apart: 52, of which 26 were waited for; matrix products, arithmetic and copies ran while one was open for 12% of the time, Pallas kernels for 5%

profile of v1, /device:TPU:1, one launch (start us, length us, event | category | flops | bytes accessed | tf_op | source)
XLA Modules:
  0.0 1071.7 jit_solution(11686943363109633220)
XLA Ops:
  9.6 4.5 collective-permute-start.1
  14.2 2.9 collective-permute-start.6
  23.7 2.0 fusion.76
  27.8 2.1 fusion.80
  29.9 2.2 fusion.81
  39.0 5.6 filter_spectrum.1
  44.6 4.0 fusion.65
  48.6 2.1 slice_bitcast_fusion.4
  50.8 2.5 slice_bitcast_fusion.1
  59.1 11.0 %mixer_forward.2 = (f32[512,1152]{1,0:T(8,128)}, f32[4,256,384]{2,1,0:T(8,128)}, f32[512,384]{1,0:T(8,128)}, bf16[512,768]{1,0:T(8,128)(2,1)}) custom-call(f32[512,768]{1,0:T(8,128)} %bitcast.224, f32[8,768]{1,0:T(8,128)} %pad.45.refs_1_.vec_ref.refs_4_.refs_8_, bf16[3,768,384]{2,1,0:T(8,128)(2,1)} %get-tuple-element.208.refs_2_.inw_ref, ...), custom_call_target="tpu_custom_call" | custom-call | flops 6000000000 | bytes 12000000 | tf_op jit(solution)/shard_map/mixer_forward/pallas_call | solution.py:484
  71.4 2.5 slice_bitcast_fusion
  74.0 15.3 %collective-permute-done.2.other_ref = bf16[512,768]{1,0:T(8,128)(2,1)S(1)} collective-permute-done((bf16[512,768]{1,0:T(8,128)(2,1)}, bf16[512,768]{1,0:T(8,128)(2,1)S(1)}, u32[]{:S(2)}, u32[]{:S(2)}) %collective-permute-start.2) | collective-permute-done | bytes 786464 | tf_op jit(solution)/shard_map/ppermute | solution.py:607
  90.2 9.7 ff_forward.2
  101.5 16.7 %collective-permute-done.3.refs_3_ = bf16[512,768]{1,0:T(8,128)(2,1)S(1)} collective-permute-done((bf16[512,768]{1,0:T(8,128)(2,1)}, bf16[512,768]{1,0:T(8,128)(2,1)S(1)}, u32[]{:S(2)}, u32[]{:S(2)}) %collective-permute-start.3) | collective-permute-done | bytes 786464 | tf_op jit(solution)/shard_map/ppermute | solution.py:607
  119.1 12.3 %mixer_forward.3 = (f32[512,768]{1,0:T(8,128)}, f32[512,1152]{1,0:T(8,128)}, f32[4,256,384]{2,1,0:T(8,128)}, f32[512,384]{1,0:T(8,128)}, bf16[512,768]{1,0:T(8,128)(2,1)}) custom-call(s32[1]{0:T(128)} %copy.148.len_ref.refs_0_, f32[512,768]{1,0:T(8,128)} %get-tuple-element.69.refs_1_.refs_6_.x1_ref, bf16[512,768]{1,0:T(8,128)(2,1)} %get-tuple-element.70.refs_2_, ...), custom_call_target="tpu_custom_call" | custom-call | flops 6000000000 | bytes 12000000 | tf_op jit(solution)/shard_map/mixer_forward/pallas_call | solution.py:484
  134.7 14.2 %collective-permute-done.4.other_ref = bf16[512,768]{1,0:T(8,128)(2,1)} collective-permute-done((bf16[512,768]{1,0:T(8,128)(2,1)}, bf16[512,768]{1,0:T(8,128)(2,1)}, u32[]{:S(2)}, u32[]{:S(2)}) %collective-permute-start.4) | collective-permute-done | bytes 786464 | tf_op jit(solution)/shard_map/ppermute | solution.py:607
  148.9 9.6 ff_forward.3
  158.5 12.7 %ff_backward.2 = (bf16[768,1536]{1,0:T(8,128)(2,1)}, bf16[1536,768]{1,0:T(8,128)(2,1)}, f32[1,1536]{1,0:T(1,128)}, f32[1,768]{1,0:T(1,128)}, bf16[512,768]{1,0:T(8,128)(2,1)}) custom-call(s32[1]{0:T(128)} %copy.148.len_ref.refs_0_, bf16[512,768]{1,0:T(8,128)(2,1)} %bitcast.238, f32[512,768]{1,0:T(8,128)} %get-tuple-element.73.refs_2_.x1_ref, ...), custom_call_target="tpu_custom_call" | custom-call | flops 10000000000 | bytes 20000000 | tf_op jit(solution)/shard_map/ff_backward/pallas_call | solution.py:544
  172.5 4.4 collective-permute-start.36
  179.8 2.4 constant_dynamic-slice_fusion.1
  183.8 2.6 add_convert_fusion
  186.5 11.8 %collective-permute-done.7.other_ref = bf16[512,768]{1,0:T(8,128)(2,1)} collective-permute-done((bf16[512,768]{1,0:T(8,128)(2,1)}, bf16[512,768]{1,0:T(8,128)(2,1)}, u32[]{:S(2)}, u32[]{:S(2)}) %collective-permute-start.7) | collective-permute-done | bytes 786464 | tf_op jit(solution)/shard_map/ppermute | solution.py:607
  198.3 18.2 %mixer_backward.2 = (f32[512,768]{1,0:T(8,128)}, f32[2,768]{1,0:T(2,128)}, bf16[384,768]{1,0:T(8,128)(2,1)}, f32[1,768]{1,0:T(1,128)}, bf16[3,768,384]{2,1,0:T(8...) custom-call(s32[1]{0:T(128)} %copy.148.len_ref.refs_0_, ...), custom_call_target="tpu_custom_call" | custom-call | flops 10000000000 | bytes 20000000 | tf_op jit(solution)/shard_map/mixer_backward/pallas_call | solution.py:563
  219.7 2.8 fusion.87
  226.5 13.3 %collective-permute-done.8.refs_3_ = bf16[512,768]{1,0:T(8,128)(2,1)S(1)} collective-permute-done((bf16[512,768]{1,0:T(8,128)(2,1)}, bf16[512,768]{1,0:T(8,128)(2,1)S(1)}, u32[]{:S(2)}, u32[]{:S(2)}) %collective-permute-start.8) | collective-permute-done | bytes 786464 | tf_op jit(solution)/shard_map/ppermute | solution.py:607
  240.6 15.5 %ff_backward.3 = (f32[512,768]{1,0:T(8,128)}, f32[2,768]{1,0:T(2,128)}, bf16[768,1536]{1,0:T(8,128)(2,1)}, bf16[1536,768]{1,0:T(8,128)(2,1)}, f32[1,1536]{1,0:T(...) custom-call(s32[1]{0:T(128)} %copy.148.len_ref.refs_0_, f32[512,768]{1,0:T(8,128)} %get-tuple-element.80.refs_1_, ...), custom_call_target="tpu_custom_call" | custom-call | flops 10000000000 | bytes 20000000 | tf_op jit(solution)/shard_map/ff_backward/pallas_call | solution.py:544
  257.0 2.6 add_convert_fusion.2
  264.0 12.2 %collective-permute-done.9.other_ref = bf16[512,768]{1,0:T(8,128)(2,1)} collective-permute-done((bf16[512,768]{1,0:T(8,128)(2,1)}, bf16[512,768]{1,0:T(8,128)(2,1)}, u32[]{:S(2)}, u32[]{:S(2)}) %collective-permute-start.9) | collective-permute-done | bytes 786464 | tf_op jit(solution)/shard_map/ppermute | solution.py:607
  276.1 18.2 %mixer_backward.3 = (f32[512,768]{1,0:T(8,128)}, f32[2,768]{1,0:T(2,128)}, bf16[384,768]{1,0:T(8,128)(2,1)}, f32[1,768]{1,0:T(1,128)}, bf16[3,768,384]{2,1,0:T(8...) custom-call(s32[1]{0:T(128)} %copy.148.len_ref.refs_0_, ...), custom_call_target="tpu_custom_call" | custom-call | flops 10000000000 | bytes 20000000 | tf_op jit(solution)/shard_map/mixer_backward/pallas_call | solution.py:563
  300.6 2.4 add_convert_fusion.4
  311.1 16.4 %collective-permute-done.10 = bf16[512,768]{1,0:T(8,128)(2,1)} collective-permute-done((bf16[512,768]{1,0:T(8,128)(2,1)}, bf16[512,768]{1,0:T(8,128)(2,1)}, u32[]{:S(2)}, u32[]{:S(2)}) %collective-permute-start.10) | collective-permute-done | bytes 786464 | tf_op jit(solution)/shard_map/ppermute | solution.py:607
  327.5 3.9 fusion.1
  331.4 3.8 concatenate.120
  338.5 3.1 add_convert_fusion.3
  342.2 2.1 collective-permute-done.14
  347.5 2.5 collective-permute-done.33
  353.2 2.1 collective-permute-done.37
  358.2 14.3 %collective-permute-done.25 = bf16[24,384]{1,0:T(8,128)(2,1)S(1)} collective-permute-done((bf16[24,384]{1,0:T(8,128)(2,1)}, bf16[24,384]{1,0:T(8,128)(2,1)S(1)}, u32[]{:S(2)}, u32[]{:S(2)}) %collective-permute-start.25) | collective-permute-done | bytes 18464 | tf_op jit(solution)/shard_map/ppermute | solution.py:607
  373.3 21.1 %all_gather.31 = bf16[384,384]{1,0:T(8,128)(2,1)} all-gather(bf16[24,384]{1,0:T(8,128)(2,1)S(1)} %add_convert_fusion.15), channel_id=1, replica_groups=mesh['zl'=2,'y'=4,'x'=4,'c'=2,'zh'=2] {'y','x'}, dimensions={0}, use_global_device_ids=true | all-gather | bytes 313344 | tf_op jit(solution)/shard_map/all_gather | solution.py:622
  394.4 6.3 collective-permute-start.26
  405.3 4.2 reduce-scatter.35.cloned.1.call-done
  414.4 69.2 %reduce-scatter.29.cloned.1.call-done = bf16[24,384]{1,0:T(8,128)(2,1)} async-done(((bf16[384,384]{1,0:T(8,128)(2,1)}), bf16[24,384]{1,0:T(8,128)(2,1)}) %reduce-scatter.29.cloned.1.call-update) | async-done | bytes 18448
  487.2 71.3 %reduce-scatter.27.cloned.1.call-done = bf16[72,384]{1,0:T(8,128)(2,1)} async-done(((bf16[1152,384]{1,0:T(8,128)(2,1)}), bf16[72,384]{1,0:T(8,128)(2,1)}) %reduce-scatter.27.cloned.1.call-update) | async-done | bytes 55312
  559.7 17.1 %all_gather.30 = bf16[384,384]{1,0:T(8,128)(2,1)S(1)} all-gather(bf16[24,384]{1,0:T(8,128)(2,1)S(1)} %add_convert_fusion.16), channel_id=1, replica_groups=mesh['zl'=2,'y'=4,'x'=4,'c'=2,'zh'=2] {'y','x'}, dimensions={0}, use_global_device_ids=true | all-gather | bytes 313344 | tf_op jit(solution)/shard_map/all_gather | solution.py:622
  576.8 8.7 collective-permute-start.23
  586.3 58.7 %all-reduce.23.cloned.1.call-done = f32[128,384]{1,0:T(8,128)} async-done(((f32[128,384]{1,0:T(8,128)}), f32[128,384]{1,0:T(8,128)}) %all-reduce.23.cloned.1.call-update) | async-done | bytes 196624
  647.0 18.1 %all_gather.29 = bf16[1152,384]{1,0:T(8,128)(2,1)S(1)} all-gather(bf16[72,384]{1,0:T(8,128)(2,1)S(1)} %add_convert_fusion.13), channel_id=1, replica_groups=mesh['zl'=2,'y'=4,'x'=4,'c'=2,'zh'=2] {'y','x'}, dimensions={0}, use_global_device_ids=true | all-gather | bytes 940032 | tf_op jit(solution)/shard_map/all_gather | solution.py:622
  665.1 8.1 collective-permute-start.19
  673.9 17.5 %all_gather.27 = f32[128,384]{1,0:T(8,128)S(1)} all-gather(f32[8,384]{1,0:T(8,128)S(1)} %fusion.110), channel_id=1, replica_groups=mesh['zl'=2,'y'=4,'x'=4,'c'=2,'zh'=2] {'y','x'}, dimensions={0}, use_global_device_ids=true | all-gather | bytes 208896 | tf_op jit(solution)/shard_map/all_gather | solution.py:622
  691.4 4.7 collective-permute-start.13
  697.8 22.7 %reduce-scatter.33.cloned.1.call-done = bf16[24,1536]{1,0:T(8,128)(2,1)} async-done(((bf16[384,1536]{1,0:T(8,128)(2,1)}), bf16[24,1536]{1,0:T(8,128)(2,1)}) %reduce-scatter.33.cloned.1.call-update) | async-done | bytes 73744
  721.7 2.1 collective-permute-done.28
  725.5 3.0 collective-permute-start.20
  734.6 61.4 %reduce-scatter.25.cloned.1.call-done = bf16[72,384]{1,0:T(8,128)(2,1)} async-done(((bf16[1152,384]{1,0:T(8,128)(2,1)}), bf16[72,384]{1,0:T(8,128)(2,1)}) %reduce-scatter.25.cloned.1.call-update) | async-done | bytes 55312
  800.6 20.7 %all_gather.28 = bf16[1152,384]{1,0:T(8,128)(2,1)} all-gather(bf16[72,384]{1,0:T(8,128)(2,1)S(1)} %add_convert_fusion.14), channel_id=1, replica_groups=mesh['zl'=2,'y'=4,'x'=4,'c'=2,'zh'=2] {'y','x'}, dimensions={0}, use_global_device_ids=true | all-gather | bytes 940032 | tf_op jit(solution)/shard_map/all_gather | solution.py:622
  821.3 8.4 collective-permute-start.16
  829.7 42.5 %reduce-scatter.21.cloned.1.call-done = bf16[48,768]{1,0:T(8,128)(2,1)} async-done(((bf16[768,768]{1,0:T(8,128)(2,1)}), bf16[48,768]{1,0:T(8,128)(2,1)}) %reduce-scatter.21.cloned.1.call-update) | async-done | bytes 73744 | tf_op jit(solution)/shard_map/reduce_scatter | solution.py:620
  876.5 40.8 %all-gather.11.cloned.1.call-done = bf16[768,768]{1,0:T(8,128)(2,1)} async-done(((bf16[48,768]{1,0:T(8,128)(2,1)}), bf16[768,768]{1,0:T(8,128)(2,1)}) %all-gather.11.cloned.1.call-update) | async-done | bytes 1179664 | tf_op jit(solution)/shard_map/all_gather | solution.py:622
  918.9 43.0 %all-gather.7.cloned.1.call-done = bf16[384,1536]{1,0:T(8,128)(2,1)} async-done(((bf16[24,1536]{1,0:T(8,128)(2,1)}), bf16[384,1536]{1,0:T(8,128)(2,1)}) %all-gather.7.cloned.1.call-update) | async-done | bytes 1179664 | tf_op jit(solution)/shard_map/all_gather | solution.py:622
  965.2 41.6 %all-gather.5.cloned.1.call-done = bf16[384,1536]{1,0:T(8,128)(2,1)} async-done(((bf16[24,1536]{1,0:T(8,128)(2,1)}), bf16[384,1536]{1,0:T(8,128)(2,1)}) %all-gather.5.cloned.1.call-update) | async-done | bytes 1179664 | tf_op jit(solution)/shard_map/all_gather | solution.py:622
  1008.4 3.4 convert_bitcast_fusion
  1013.5 38.4 %all-gather.9.cloned.1.call-done = bf16[768,768]{1,0:T(8,128)(2,1)} async-done(((bf16[48,768]{1,0:T(8,128)(2,1)}), bf16[768,768]{1,0:T(8,128)(2,1)}) %all-gather.9.cloned.1.call-update) | async-done | bytes 1179664 | tf_op jit(solution)/shard_map/all_gather | solution.py:622
  1056.4 4.1 maximum_convert_fusion
  1060.6 4.1 maximum_convert_fusion.1
  (437 shorter events, 127.3 us)
Async XLA Ops:
  7.2 27.6 %copy-start.50 = (f32[512]{0:T(512)S(1)}, f32[512]{0:T(512)}, u32[]{:S(2)}) copy-start(f32[512]{0:T(512)} %constant.109) | copy-start | bytes 6148
  7.2 24.9 %copy-start.44 = (f32[2,2,64,64]{3,2,1,0:T(8,128)S(1)}, f32[2,2,64,64]{3,2,1,0:T(8,128)}, u32[]{:S(2)}) copy-start(f32[2,2,64,64]{3,2,1,0:T(8,128)} %param.35) | copy-start | bytes 196612
  7.2 27.6 %copy-start.34 = (f32[2,64,384]{2,1,0:T(8,128)S(1)}, f32[2,64,384]{2,1,0:T(8,128)}, u32[]{:S(2)}) copy-start(f32[2,64,384]{2,1,0:T(8,128)} %param.37) | copy-start | bytes 589828
  7.2 344.2 %reduce-scatter.23.cloned.1.call-start = ((), (), s32[]{:S(2)}) async-start(), calls=%async_computation.12 | async-start | bytes 1253376 | tf_op jit(solution)/shard_map/reduce_scatter | solution.py:620
  9.6 44.9 %collective-permute-start.1 = (f32[12,384]{1,0:T(8,128)S(1)}, f32[12,384]{1,0:T(8,128)S(1)}, u32[]{:S(2)}, u32[]{:S(2)}) collective-permute-start(f32[12,384]{1,0:T(8,128)S(1)} %concatenate.115), channel_id=1, source_target_pairs={{0,1},{1,0},{2,3},{3,2},{4,5},{5,4},{6,7},{7,6},{8,9},{9,8},{10,11... | collective-permute-start | bytes 55304 | tf_op jit(solution)/shard_map/ppermute | solution.py:607
  14.1 41.7 %collective-permute-start = (bf16[512,384]{1,0:T(8,128)(2,1)}, bf16[512,384]{1,0:T(8,128)(2,1)S(1)}, u32[]{:S(2)}, u32[]{:S(2)}) collective-permute-start(bf16[512,384]{1,0:T(8,128)(2,1)} %param.26), channel_id=1, source_target_pairs={{0,1},{1,0},{2,3},{3,2},{4,5},{5,4},{6,7},{7,6},{8,9},{9,8},{10,11... | collective-permute-start | bytes 1179656 | tf_op jit(solution)/shard_map/ppermute | solution.py:607
  14.2 41.7 %collective-permute-start.6 = (bf16[512,384]{1,0:T(8,128)(2,1)}, bf16[512,384]{1,0:T(8,128)(2,1)S(1)}, u32[]{:S(2)}, u32[]{:S(2)}) collective-permute-start(bf16[512,384]{1,0:T(8,128)(2,1)} %param.45), channel_id=1, source_target_pairs={{0,1},{1,0},{2,3},{3,2},{4,5},{5,4},{6,7},{7,6},{8,9},{9,8},{10,11... | collective-permute-start | bytes 1179656 | tf_op jit(solution)/shard_map/ppermute | solution.py:607
  70.1 19.2 %collective-permute-start.2 = (bf16[512,768]{1,0:T(8,128)(2,1)}, bf16[512,768]{1,0:T(8,128)(2,1)S(1)}, u32[]{:S(2)}, u32[]{:S(2)}) collective-permute-start(bf16[512,768]{1,0:T(8,128)(2,1)} %get-tuple-element.68.own_ref), channel_id=1, source_target_pairs={{0,1},{1,0},{2,3},{3,2},{4,5},{5,4},{6,7},{7,6},{8,9},{9,8},{10,11... | collective-permute-start | bytes 2359304 | tf_op jit(solution)/shard_map/ppermute | solution.py:607
  99.9 18.3 %collective-permute-start.3 = (bf16[512,768]{1,0:T(8,128)(2,1)}, bf16[512,768]{1,0:T(8,128)(2,1)S(1)}, u32[]{:S(2)}, u32[]{:S(2)}) collective-permute-start(bf16[512,768]{1,0:T(8,128)(2,1)} %get-tuple-element.70.refs_2_), channel_id=1, source_target_pairs={{0,1},{1,0},{2,3},{3,2},{4,5},{5,4},{6,7},{7,6},{8,9},{9,8},{10,11... | collective-permute-start | bytes 2359304 | tf_op jit(solution)/shard_map/ppermute | solution.py:607
  131.4 17.5 %collective-permute-start.4 = (bf16[512,768]{1,0:T(8,128)(2,1)}, bf16[512,768]{1,0:T(8,128)(2,1)}, u32[]{:S(2)}, u32[]{:S(2)}) collective-permute-start(bf16[512,768]{1,0:T(8,128)(2,1)} %get-tuple-element.72.own_ref), channel_id=1, source_target_pairs={{0,1},{1,0},{2,3},{3,2},{4,5},{5,4},{6,7},{7,6},{8,9},{9,8},{10,11... | collective-permute-start | bytes 2359304 | tf_op jit(solution)/shard_map/ppermute | solution.py:607
  172.5 11.2 %collective-permute-start.36 = (bf16[768,768]{1,0:T(8,128)(2,1)S(1)}, bf16[768,768]{1,0:T(8,128)(2,1)}, u32[]{:S(2)}, u32[]{:S(2)}) collective-permute-start(bf16[768,768]{1,0:T(8,128)(2,1)S(1)} %constant_dynamic-slice_fusion.16), channel_id=1, source_target_pairs={{0,2},{2,0},{1,3},{3,1},{4,6},{6,4},{5,7},{7,5},{8,10},{10,8},{9,1... | collective-permute-start | bytes 3538952 | tf_op jit(solution)/shard_map/ppermute | solution.py:607
  177.2 21.1 %collective-permute-start.7 = (bf16[512,768]{1,0:T(8,128)(2,1)}, bf16[512,768]{1,0:T(8,128)(2,1)}, u32[]{:S(2)}, u32[]{:S(2)}) collective-permute-start(bf16[512,768]{1,0:T(8,128)(2,1)} %get-tuple-element.76.own_ref), channel_id=1, source_target_pairs={{0,1},{1,0},{2,3},{3,2},{4,5},{5,4},{6,7},{7,6},{8,9},{9,8},{10,11... | collective-permute-start | bytes 2359304 | tf_op jit(solution)/shard_map/ppermute | solution.py:607
  182.3 74.7 %collective-permute-start.30 = (bf16[384,1536]{1,0:T(8,128)(2,1)}, bf16[384,1536]{1,0:T(8,128)(2,1)}, u32[]{:S(2)}, u32[]{:S(2)}) collective-permute-start(bf16[384,1536]{1,0:T(8,128)(2,1)} %constant_dynamic-slice_fusion.1), channel_id=1, source_target_pairs={{0,2},{2,0},{1,3},{3,1},{4,6},{6,4},{5,7},{7,5},{8,10},{10,8},{9,1... | collective-permute-start | bytes 3538952 | tf_op jit(solution)/shard_map/ppermute | solution.py:607
  186.4 166.8 %reduce-scatter.31.cloned.1.call-start = ((), (), s32[]{:S(2)}) async-start(), calls=%async_computation.18 | async-start | bytes 313344
  198.3 21.4 %copy-start.43 = (f32[512,64]{0,1:T(8,128)S(1)}, f32[512,64]{0,1:T(8,128)}, u32[]{:S(2)}) copy-start(f32[512,64]{0,1:T(8,128)} %get-tuple-element.271) | copy-start | bytes 393220
  217.7 7.8 collective-permute-start.24
  218.6 21.1 %collective-permute-start.8 = (bf16[512,768]{1,0:T(8,128)(2,1)}, bf16[512,768]{1,0:T(8,128)(2,1)S(1)}, u32[]{:S(2)}, u32[]{:S(2)}) collective-permute-start(bf16[512,768]{1,0:T(8,128)(2,1)} %get-tuple-element.81.refs_2_), channel_id=1, source_target_pairs={{0,1},{1,0},{2,3},{3,2},{4,5},{5,4},{6,7},{7,6},{8,9},{9,8},{10,11... | collective-permute-start | bytes 2359304 | tf_op jit(solution)/shard_map/ppermute | solution.py:607
  226.4 183.0 %reduce-scatter.35.cloned.1.call-start = ((), (), s32[]{:S(2)}) async-start(), calls=%async_computation.20 | async-start | bytes 1253376
  256.1 20.0 %collective-permute-start.9 = (bf16[512,768]{1,0:T(8,128)(2,1)}, bf16[512,768]{1,0:T(8,128)(2,1)}, u32[]{:S(2)}, u32[]{:S(2)}) collective-permute-start(bf16[512,768]{1,0:T(8,128)(2,1)} %get-tuple-element.84.own_ref), channel_id=1, source_target_pairs={{0,1},{1,0},{2,3},{3,2},{4,5},{5,4},{6,7},{7,6},{8,9},{9,8},{10,11... | collective-permute-start | bytes 2359304 | tf_op jit(solution)/shard_map/ppermute | solution.py:607
  259.6 224.0 %reduce-scatter.29.cloned.1.call-start = ((), (), s32[]{:S(2)}) async-start(), calls=%async_computation.17 | async-start | bytes 313344
  260.7 39.9 %collective-permute-start.17 = (bf16[1152,384]{1,0:T(8,128)(2,1)}, bf16[1152,384]{1,0:T(8,128)(2,1)}, u32[]{:S(2)}, u32[]{:S(2)}) collective-permute-start(bf16[1152,384]{1,0:T(8,128)(2,1)} %constant_dynamic-slice_fusion.5), channel_id=1, source_target_pairs={{0,2},{2,0},{1,3},{3,1},{4,6},{6,4},{5,7},{7,5},{8,10},{10,8},{9,1... | collective-permute-start | bytes 2654216 | tf_op jit(solution)/shard_map/ppermute | solution.py:607
  295.5 3.7 collective-permute-start.21
  298.5 40.0 %collective-permute-start.27 = (bf16[384,1536]{1,0:T(8,128)(2,1)}, bf16[384,1536]{1,0:T(8,128)(2,1)}, u32[]{:S(2)}, u32[]{:S(2)}) collective-permute-start(bf16[384,1536]{1,0:T(8,128)(2,1)} %constant_dynamic-slice_fusion.2), channel_id=1, source_target_pairs={{0,2},{2,0},{1,3},{3,1},{4,6},{6,4},{5,7},{7,5},{8,10},{10,8},{9,1... | collective-permute-start | bytes 3538952 | tf_op jit(solution)/shard_map/ppermute | solution.py:607
  300.0 258.5 %reduce-scatter.27.cloned.1.call-start = ((), (), s32[]{:S(2)}) async-start(), calls=%async_computation.16 | async-start | bytes 940032
  303.1 342.0 %all-reduce.23.cloned.1.call-start = ((), (), s32[]{:S(2)}) async-start(), calls=%async_computation.14 | async-start | bytes 393216
  305.2 22.3 %copy-start = (f32[256,2,768]{2,0,1:T(8,128)S(1)}, f32[256,2,768]{2,0,1:T(8,128)}, u32[]{:S(2)}) copy-start(f32[256,2,768]{2,0,1:T(8,128)} %copy.90) | copy-start | bytes 4718596
  305.2 22.3 %copy-start.58 = (f32[512]{0:T(512)S(1)}, f32[512]{0:T(512)}, u32[]{:S(2)}) copy-start(f32[512]{0:T(512)} %add_rsqrt_fusion) | copy-start | bytes 6148
  305.2 22.3 %copy-start.61 = (f32[1,2,2,128]{3,1,2,0:T(2,128)S(1)}, f32[1,2,2,128]{3,1,2,0:T(2,128)}, u32[]{:S(2)}) copy-start(f32[1,2,2,128]{3,1,2,0:T(2,128)} %copy-done.60) | copy-start | bytes 6148
  306.9 20.5 %collective-permute-start.10 = (bf16[512,768]{1,0:T(8,128)(2,1)}, bf16[512,768]{1,0:T(8,128)(2,1)}, u32[]{:S(2)}, u32[]{:S(2)}) collective-permute-start(bf16[512,768]{1,0:T(8,128)(2,1)} %get-tuple-element.89), channel_id=1, source_target_pairs={{0,1},{1,0},{2,3},{3,2},{4,5},{5,4},{6,7},{7,6},{8,9},{9,8},{10,11... | collective-permute-start | bytes 2359304 | tf_op jit(solution)/shard_map/ppermute | solution.py:607
  335.2 2.5 collective-permute-start.11
  338.5 381.9 %reduce-scatter.33.cloned.1.call-start = ((), (), s32[]{:S(2)}) async-start(), calls=%async_computation.19 | async-start | bytes 1253376
  341.6 454.4 %reduce-scatter.25.cloned.1.call-start = ((), (), s32[]{:S(2)}) async-start(), calls=%async_computation.15 | async-start | bytes 940032
  341.8 2.5 collective-permute-start.14
  345.5 526.8 %reduce-scatter.21.cloned.1.call-start = ((), (), s32[]{:S(2)}) async-start(), calls=%async_computation.10 | async-start | bytes 1253376 | tf_op jit(solution)/shard_map/reduce_scatter | solution.py:620
  347.1 2.9 collective-permute-start.33
  351.3 49.4 %copy-start.69 = (f32[2,384]{1,0:T(2,128)S(1)}, f32[2,384]{1,0:T(2,128)}, u32[]{:S(2)}) copy-start(f32[2,384]{1,0:T(2,128)} %param.44) | copy-start | bytes 9220
  351.3 49.4 %copy-start.46 = (f32[512,768]{1,0:T(8,128)S(1)}, f32[512,768]{1,0:T(8,128)}, u32[]{:S(2)}) copy-start(f32[512,768]{1,0:T(8,128)} %get-tuple-element.73.refs_2_.x1_ref) | copy-start | bytes 4718596
  351.3 566.0 %all-gather.11.cloned.1.call-start = ((), (), s32[]{:S(2)}) async-start(), calls=%async_computation.13 | async-start | bytes 1253376 | tf_op jit(solution)/shard_map/all_gather | solution.py:622
  351.4 3.9 collective-permute-start.37
  352.3 48.4 %collective-permute-start.5 = (bf16[512,768]{1,0:T(8,128)(2,1)}, bf16[512,768]{1,0:T(8,128)(2,1)}, u32[]{:S(2)}, u32[]{:S(2)}) collective-permute-start(bf16[512,768]{1,0:T(8,128)(2,1)} %get-tuple-element.74), channel_id=1, source_target_pairs={{0,1},{1,0},{2,3},{3,2},{4,5},{5,4},{6,7},{7,6},{8,9},{9,8},{10,11... | collective-permute-start | bytes 2359304 | tf_op jit(solution)/shard_map/ppermute | solution.py:607
  353.2 19.3 %collective-permute-start.25 = (bf16[24,384]{1,0:T(8,128)(2,1)}, bf16[24,384]{1,0:T(8,128)(2,1)S(1)}, u32[]{:S(2)}, u32[]{:S(2)}) collective-permute-start(bf16[24,384]{1,0:T(8,128)(2,1)} %reduce-scatter.31.cloned.1.call-done), channel_id=1, source_target_pairs={{0,64},{64,0},{1,65},{65,1},{2,66},{66,2},{3,67},{67,3},{4,68},{68... | collective-permute-start | bytes 55304 | tf_op jit(solution)/shard_map/ppermute | solution.py:607
  356.9 605.0 %all-gather.7.cloned.1.call-start = ((), (), s32[]{:S(2)}) async-start(), calls=%async_computation.9 | async-start | bytes 1253376 | tf_op jit(solution)/shard_map/all_gather | solution.py:622
  394.4 9.0 collective-permute-start.26
  409.5 75.5 %collective-permute-start.31 = (bf16[24,1536]{1,0:T(8,128)(2,1)}, bf16[24,1536]{1,0:T(8,128)(2,1)S(1)}, u32[]{:S(2)}, u32[]{:S(2)}) collective-permute-start(bf16[24,1536]{1,0:T(8,128)(2,1)} %reduce-scatter.35.cloned.1.call-done), channel_id=1, source_target_pairs={{0,64},{64,0},{1,65},{65,1},{2,66},{66,2},{3,67},{67,3},{4,68},{68... | collective-permute-start | bytes 221192 | tf_op jit(solution)/shard_map/ppermute | solution.py:607
  412.4 72.5 %copy-start.51 = (bf16[24,1536]{1,0:T(8,128)(2,1)S(1)}, bf16[24,1536]{1,0:T(8,128)(2,1)}, u32[]{:S(2)}) copy-start(bf16[24,1536]{1,0:T(8,128)(2,1)} %reduce-scatter.35.cloned.1.call-done) | copy-start | bytes 221188
  414.4 281.8 %copy-start.16 = (bf16[1,384,384]{2,1,0:T(8,128)(2,1)S(1)}, bf16[1,384,384]{2,1,0:T(8,128)(2,1)}, u32[]{:S(2)}) copy-start(bf16[1,384,384]{2,1,0:T(8,128)(2,1)} %get-tuple-element.232) | copy-start | bytes 884740
  483.6 2.8 collective-permute-start.22
  485.6 521.2 %all-gather.5.cloned.1.call-start = ((), (), s32[]{:S(2)}) async-start(), calls=%async_computation.8 | async-start | bytes 1253376 | tf_op jit(solution)/shard_map/all_gather | solution.py:622
  558.4 27.0 %collective-permute-start.18 = (bf16[72,384]{1,0:T(8,128)(2,1)}, bf16[72,384]{1,0:T(8,128)(2,1)S(1)}, u32[]{:S(2)}, u32[]{:S(2)}) collective-permute-start(bf16[72,384]{1,0:T(8,128)(2,1)} %reduce-scatter.27.cloned.1.call-done), channel_id=1, source_target_pairs={{0,64},{64,0},{1,65},{65,1},{2,66},{66,2},{3,67},{67,3},{4,68},{68... | collective-permute-start | bytes 165896 | tf_op jit(solution)/shard_map/ppermute | solution.py:607
  576.8 119.3 %collective-permute-start.23 = (bf16[384,384]{1,0:T(8,128)(2,1)S(1)}, bf16[384,384]{1,0:T(8,128)(2,1)S(1)}, u32[]{:S(2)}, u32[]{:S(2)}) collective-permute-start(bf16[384,384]{1,0:T(8,128)(2,1)S(1)} %all_gather.30), channel_id=1, source_target_pairs={{0,2},{2,0},{1,3},{3,1},{4,6},{6,4},{5,7},{7,5},{8,10},{10,8},{9,1... | collective-permute-start | bytes 884744 | tf_op jit(solution)/shard_map/ppermute | solution.py:607
  645.7 27.5 %collective-permute-start.12 = (f32[8,384]{1,0:T(8,128)S(1)}, f32[8,384]{1,0:T(8,128)S(1)}, u32[]{:S(2)}, u32[]{:S(2)}) collective-permute-start(f32[8,384]{1,0:T(8,128)S(1)} %constant_dynamic-slice_fusion.17), channel_id=1, source_target_pairs={{0,64},{64,0},{1,65},{65,1},{2,66},{66,2},{3,67},{67,3},{4,68},{68... | collective-permute-start | bytes 36872 | tf_op jit(solution)/shard_map/ppermute | solution.py:607
  665.1 208.4 %collective-permute-start.19 = (bf16[1152,384]{1,0:T(8,128)(2,1)S(1)}, bf16[1152,384]{1,0:T(8,128)(2,1)}, u32[]{:S(2)}, u32[]{:S(2)}) collective-permute-start(bf16[1152,384]{1,0:T(8,128)(2,1)S(1)} %all_gather.29), channel_id=1, source_target_pairs={{0,2},{2,0},{1,3},{3,1},{4,6},{6,4},{5,7},{7,5},{8,10},{10,8},{9,1... | collective-permute-start | bytes 2654216 | tf_op jit(solution)/shard_map/ppermute | solution.py:607
  691.4 30.3 %collective-permute-start.13 = (f32[128,384]{1,0:T(8,128)S(1)}, f32[128,384]{1,0:T(8,128)S(1)}, u32[]{:S(2)}, u32[]{:S(2)}) collective-permute-start(f32[128,384]{1,0:T(8,128)S(1)} %all_gather.27), channel_id=1, source_target_pairs={{0,2},{2,0},{1,3},{3,1},{4,6},{6,4},{5,7},{7,5},{8,10},{10,8},{9,1... | collective-permute-start | bytes 589832 | tf_op jit(solution)/shard_map/ppermute | solution.py:607
  720.4 3.4 collective-permute-start.28
  725.4 326.5 %all-gather.9.cloned.1.call-start = ((), (), s32[]{:S(2)}) async-start(), calls=%async_computation.11 | async-start | bytes 1253376 | tf_op jit(solution)/shard_map/all_gather | solution.py:622
  725.5 71.7 %collective-permute-start.20 = (f32[55,384]{1,0:T(8,128)S(1)}, f32[55,384]{1,0:T(8,128)S(1)}, u32[]{:S(2)}, u32[]{:S(2)}) collective-permute-start(f32[55,384]{1,0:T(8,128)S(1)} %slice.293), channel_id=1, source_target_pairs={{0,1},{1,0},{2,3},{3,2},{4,5},{5,4},{6,7},{7,6},{8,9},{9,8},{10,11... | collective-permute-start | bytes 253448 | tf_op jit(solution)/shard_map/ppermute | solution.py:607
  796.0 3.8 collective-permute-start.15
  821.3 142.2 %collective-permute-start.16 = (bf16[1152,384]{1,0:T(8,128)(2,1)}, bf16[1152,384]{1,0:T(8,128)(2,1)}, u32[]{:S(2)}, u32[]{:S(2)}) collective-permute-start(bf16[1152,384]{1,0:T(8,128)(2,1)} %all_gather.28), channel_id=1, source_target_pairs={{0,2},{2,0},{1,3},{3,1},{4,6},{6,4},{5,7},{7,5},{8,10},{10,8},{9,1... | collective-permute-start | bytes 2654216 | tf_op jit(solution)/shard_map/ppermute | solution.py:607
  872.2 3.4 collective-permute-start.34
  917.3 136.1 %collective-permute-start.38 = (bf16[768,768]{1,0:T(8,128)(2,1)}, bf16[768,768]{1,0:T(8,128)(2,1)}, u32[]{:S(2)}, u32[]{:S(2)}) collective-permute-start(bf16[768,768]{1,0:T(8,128)(2,1)} %all-gather.11.cloned.1.call-done), channel_id=1, source_target_pairs={{0,2},{2,0},{1,3},{3,1},{4,6},{6,4},{5,7},{7,5},{8,10},{10,8},{9,1... | collective-permute-start | bytes 3538952 | tf_op jit(solution)/shard_map/ppermute | solution.py:607
  961.9 49.9 %collective-permute-start.32 = (bf16[384,1536]{1,0:T(8,128)(2,1)}, bf16[384,1536]{1,0:T(8,128)(2,1)}, u32[]{:S(2)}, u32[]{:S(2)}) collective-permute-start(bf16[384,1536]{1,0:T(8,128)(2,1)} %all-gather.7.cloned.1.call-done), channel_id=1, source_target_pairs={{0,2},{2,0},{1,3},{3,1},{4,6},{6,4},{5,7},{7,5},{8,10},{10,8},{9,1... | collective-permute-start | bytes 3538952 | tf_op jit(solution)/shard_map/ppermute | solution.py:607
  1006.8 48.1 %collective-permute-start.29 = (bf16[384,1536]{1,0:T(8,128)(2,1)}, bf16[384,1536]{1,0:T(8,128)(2,1)}, u32[]{:S(2)}, u32[]{:S(2)}) collective-permute-start(bf16[384,1536]{1,0:T(8,128)(2,1)} %all-gather.5.cloned.1.call-done), channel_id=1, source_target_pairs={{0,2},{2,0},{1,3},{3,1},{4,6},{6,4},{5,7},{7,5},{8,10},{10,8},{9,1... | collective-permute-start | bytes 3538952 | tf_op jit(solution)/shard_map/ppermute | solution.py:607
  1011.8 41.7 %copy-start.12 = (bf16[768,768]{1,0:T(8,128)(2,1)S(1)}, bf16[768,768]{1,0:T(8,128)(2,1)}, u32[]{:S(2)}) copy-start(bf16[768,768]{1,0:T(8,128)(2,1)} %all-gather.11.cloned.1.call-done) | copy-start | bytes 3538948
  1051.9 8.6 collective-permute-start.35
  (78 other events, 512.7 us)
Sparse Core Ops, SparseCore 0:
  186.5 72.1 reduce-scatter.22
  262.5 70.8 reduce-scatter.30
  337.0 72.4 reduce-scatter.34
  412.8 70.7 reduce-scatter.28
  486.7 71.7 reduce-scatter.26
  562.1 82.8 all-reduce.22
  648.2 72.1 reduce-scatter.32
  724.2 71.7 reduce-scatter.24
  799.8 72.4 reduce-scatter.20
  874.2 43.0 all-gather.10
  919.5 42.3 all-gather.6
  964.4 42.3 all-gather.4
  1009.5 42.3 all-gather.8

commit v2 on v1

v2 whole, which is shorter than its diff:
```python
import functools
import math

import jax
import jax.numpy as jnp
import ml_dtypes
import numpy as np
from jax import lax
from jax.experimental import pallas as pl
from jax.experimental.pallas import tpu as pltpu
from jax.sharding import Mesh
from jax.sharding import PartitionSpec as P

D = 768
T = 512
H = T // 2
C = 384
FH = 1536
NET = 64
EMB = 33
BANDS = 16
PIECE = 96
EPSILON = 1e-05
HIGH = lax.Precision.HIGHEST
F32 = jnp.float32
BF = jnp.bfloat16
VMEM_LIMIT = 56 * 2**20

ORDER = np.concatenate([np.arange(0, T, 2), np.arange(1, T, 2)])


def split_table(t):
    hi = t.astype(ml_dtypes.bfloat16)
    lo = (t - hi.astype(np.float64)).astype(ml_dtypes.bfloat16)
    return hi, lo


def wave_tables():
    n = np.arange(H)
    even = 2 * math.pi * (np.outer(n, 2 * n) % (2 * T)) / (2 * T)
    odd = 2 * math.pi * (np.outer(n, 2 * n + 1) % (2 * T)) / (2 * T)
    alt = np.where(n % 2 == 0, 1.0, -1.0)
    out = []
    for ang in (even, odd):
        co, si = np.cos(ang), np.sin(ang)
        si[0] = alt
        hi, lo = split_table(np.concatenate([co, si], 0))
        out.append(np.concatenate([hi, lo, hi], 1))
        hi, lo = split_table(np.concatenate([co.T, si.T], 1))
        out.append(np.concatenate([hi, lo, hi], 1))
    fe, ie, fo, io = out
    return fe, fo, ie, io


FE, FO, IE, IO = wave_tables()


def slot_features():
    slots = ORDER.astype(np.float64)
    freqs = 0.0001 + (BANDS - 1 - 0.0001) * np.arange(BANDS) / (BANDS - 1)
    angle = 2 * math.pi * slots[:, None] * freqs[None, :] / T
    times = (slots / (T - 1))[:, None]
    feats = np.concatenate([times, np.cos(angle), -np.sin(angle), np.zeros((T, 128 - EMB))], 1)
    return feats.astype(np.float32), np.broadcast_to(times, (T, 128)).astype(np.float32)


FEATS, TIMES = slot_features()


def dot(a, b):
    return lax.dot_general(a, b, (((1,), (0,)), ((), ())), preferred_element_type=F32)


def dot_nt(a, b):
    return lax.dot_general(a, b, (((1,), (1,)), ((), ())), preferred_element_type=F32)


def dot_tn(a, b):
    return lax.dot_general(a, b, (((0,), (0,)), ((), ())), preferred_element_type=F32)


def normalize(x):
    mean = jnp.mean(x, -1, keepdims=True)
    scale = lax.rsqrt(jnp.mean(x * x, -1, keepdims=True) - mean * mean + EPSILON)
    return (x - mean) * scale, scale


def norm_pull(dn, x, gain):
    xhat, scale = normalize(x)
    ds = dn * gain
    first = jnp.mean(ds, -1, keepdims=True)
    second = jnp.mean(ds * xhat, -1, keepdims=True)
    return scale * (ds - first - xhat * second), dn * xhat


def row_mask(start, rows, length):
    r = start + lax.broadcasted_iota(jnp.int32, (rows, 1), 0)
    slot = jnp.where(r < H, 2 * r, 2 * (r - H) + 1)
    return (slot < length).astype(F32)


def down_one(x):
    r = lax.broadcasted_iota(jnp.int32, x.shape, 0)
    return jnp.where(r == 0, 0.0, pltpu.roll(x, 1, 0))


def up_one(x):
    r = lax.broadcasted_iota(jnp.int32, x.shape, 0)
    return jnp.where(r == x.shape[0] - 1, 0.0, pltpu.roll(x, x.shape[0] - 1, 0))


def put_split(ref, value, rows, lanes):
    hi = value.astype(BF)
    lo = (value - hi.astype(F32)).astype(BF)
    step = ref.shape[0] // 3
    ref[pl.ds(rows, value.shape[0]), lanes] = hi
    ref[pl.ds(step + rows, value.shape[0]), lanes] = hi
    ref[pl.ds(2 * step + rows, value.shape[0]), lanes] = lo


def top_row(shape):
    return lax.broadcasted_iota(jnp.int32, shape, 0) == 0


def butterfly(even, odd, lanes):
    ce, se = even[pl.ds(0, H), lanes], even[pl.ds(H, H), lanes]
    co, so = odd[pl.ds(0, H), lanes], odd[pl.ds(H, H), lanes]
    top = top_row(ce.shape)
    return ce + co, ce - co, jnp.where(top, se, se + so), jnp.where(top, so, se - so)


def spectrum_product(a, k, conj):
    a1, a2, b1, b2 = a
    k1, k2, l1, l2 = k
    top = top_row(a1.shape)
    aa, bb, cc, dd = a1 * k1, b1 * l1, a2 * k2, b2 * l2
    if conj:
        y1 = jnp.where(top, aa, aa + bb)
        y2 = jnp.where(top, cc, cc + dd)
        m1 = jnp.where(top, bb + dd, b1 * k1 - a1 * l1)
        m2 = jnp.where(top, b2 * l1 - b1 * l2, b2 * k2 - a2 * l2)
    else:
        y1 = jnp.where(top, aa, aa - bb)
        y2 = jnp.where(top, cc, cc - dd)
        m1 = jnp.where(top, bb - dd, a1 * l1 + b1 * k1)
        m2 = jnp.where(top, b1 * l2 + b2 * l1, a2 * l2 + b2 * k2)
    return y1, y2, m1, m2


def put_inverse(rhs_e, rhs_o, y, lanes):
    y1, y2, m1, m2 = y
    top = top_row(y1.shape)
    unit = 1.0 / T
    w = jnp.where(top, 0.5 * unit, unit)
    put_split(rhs_e, (y1 + y2) * w, 0, lanes)
    put_split(rhs_o, (y1 - y2) * w, 0, lanes)
    put_split(rhs_e, jnp.where(top, m1, m1 + m2) * unit, H, lanes)
    put_split(rhs_o, jnp.where(top, m2, m1 - m2) * unit, H, lanes)


def lanes_of(block):
    return pl.ds(block * 128, 128)


def short_conv(u_ref, sw_ref, sb_ref, block):
    out = []
    for s in range(3):
        at = lanes_of(s * (C // 128) + block)
        ue, uo = u_ref[pl.ds(0, H), at], u_ref[pl.ds(H, H), at]
        t0, t1, t2 = (sw_ref[j : j + 1, at] for j in range(3))
        bias = sb_ref[0:1, at]
        uo_d = down_one(uo)
        we = t2 * ue + t1 * uo_d + t0 * down_one(ue) + bias
        wo = t2 * uo + t1 * ue + t0 * uo_d + bias
        out.append((we, wo))
    return out


def hdot(a, b, dims=(1, 0)):
    return lax.dot_general(
        a, b, (((dims[0],), (dims[1],)), ((), ())), precision=HIGH, preferred_element_type=F32
    )


def decay_of(half_at, times_ref):
    slow = math.log(0.01) / 1.5
    fast = math.log(0.01) / 0.3
    channel = (half_at * C + lax.broadcasted_iota(jnp.int32, (1, C), 1)).astype(F32)
    rates = jnp.abs(slow + (fast - slow) * channel / (D - 1))
    return jnp.exp(-times_ref[:, 0:1] * rates) + 0.05


def sin_cos(x):
    k = jnp.floor(x * (2 / math.pi) + 0.5)
    r = ((x - k * 1.5703125) - k * 4.837512969970703125e-4) - k * 7.54978995489188e-8
    rr = r * r
    sine = r + r * rr * (-1.6666654611e-1 + rr * (8.3321608736e-3 + rr * -1.9515295891e-4))
    cosine = 1.0 - 0.5 * rr + rr * rr * (
        4.166664568298827e-2 + rr * (-1.388731625493765e-3 + rr * 2.443315711809948e-5)
    )
    quarter = k - 4.0 * jnp.floor(k * 0.25)
    odd = (quarter == 1.0) | (quarter == 3.0)
    s = jnp.where(odd, cosine, sine)
    c = jnp.where(odd, sine, cosine)
    return jnp.where(quarter >= 2.0, -s, s), jnp.where((quarter == 1.0) | (quarter == 2.0), -c, c)


def filter_forward(
    at_ref, feats_ref, times_ref, first_ref, inner_ref, bias_ref, out_ref, fe_ref, fo_ref,
    ks_ref, sin_ref, cos_ref, both_ref, wide_ref, first_s, bias_s, k_s, rhs_e, rhs_o, se, so,
):
    for ref in (both_ref, wide_ref, first_s, bias_s):
        ref[...] = jnp.zeros_like(ref)
    for l in range(2):
        at = pl.ds(l * NET, NET)
        first_s[0:EMB, at] = first_ref[l]
        bias_s[0:3, at] = bias_ref[l]
        wide_ref[l, at, :] = out_ref[l]
        for i in range(2):
            both_ref[i, at, at] = inner_ref[l, i]
    low = feats_ref[...]
    for i in range(3):
        weight = first_s[...] if i == 0 else both_ref[i - 1]
        low, cosine = sin_cos(hdot(low, weight) + bias_s[i : i + 1, :])
        sin_ref[i] = low
        cos_ref[i] = cosine
    decay = decay_of(at_ref[0], times_ref)
    for l in range(2):
        k_s[...] = hdot(sin_ref[2], wide_ref[l]) * decay
        for b in range(C // 128):
            at = lanes_of(b)
            put_split(rhs_e, k_s[pl.ds(0, H), at], 0, at)
            put_split(rhs_o, k_s[pl.ds(H, H), at], 0, at)
        se[...] = dot(fe_ref[...], rhs_e[...])
        so[...] = dot(fo_ref[...], rhs_o[...])
        for b in range(C // 128):
            at = lanes_of(b)
            for i, v in enumerate(butterfly(se, so, at)):
                ks_ref[l, i, :, at] = v


def filter_backward(at_ref, feats_ref, times_ref, inner_ref, out_ref, sin_ref, cos_ref, dk0_ref, dk1_ref, gout_ref, gnet_ref):
    decay = decay_of(at_ref[0], times_ref)
    ds = jnp.zeros((T, 128), F32)
    for l, dk_ref in enumerate((dk0_ref, dk1_ref)):
        dk = dk_ref[...] * decay
        gout_ref[l] = hdot(sin_ref[2], dk, (0, 0))[l * NET : (l + 1) * NET]
        ds += hdot(dk, out_ref[l], (1, 1))
    lane = lax.broadcasted_iota(jnp.int32, (NET, 128), 1)
    gnet_ref[...] = jnp.zeros_like(gnet_ref)
    for i in (2, 1, 0):
        da = ds * cos_ref[i]
        gnet_ref[40 + i : 41 + i, pl.ds(256, 128)] = jnp.sum(da, 0, keepdims=True)
        if i > 0:
            block = hdot(sin_ref[i - 1], da, (0, 0))
            gnet_ref[:, pl.ds((i - 1) * 128, 128)] = jnp.where(lane < NET, block[:NET], block[NET:])
            ds = hdot(da, inner_ref[i - 1], (1, 1))
        else:
            gnet_ref[0:40, pl.ds(256, 128)] = hdot(feats_ref[...], da, (0, 0))[0:40]


def arrange(at_ref, own_ref, other_ref, out_ref, tmp):
    for half, first in ((0, own_ref), (1, other_ref)):
        for b in range(C // 128):
            tmp[b] = first[:, lanes_of(b)].astype(F32)

        def put(first_lane):
            for b in range(C // 128):
                to = pl.ds(first_lane + b * 128, 128)
                out_ref[pl.ds(0, H), to] = tmp[b, pl.ds(0, H, stride=2), :]
                out_ref[pl.ds(H, H), to] = tmp[b, pl.ds(1, H, stride=2), :]

        pl.when(at_ref[0] == half)(functools.partial(put, 0))
        pl.when(at_ref[0] != half)(functools.partial(put, C))


def by_slot(at_ref, src_ref, out_ref, tmp):
    def put(first_lane):
        for b in range(C // 128):
            lanes = pl.ds(first_lane + b * 128, 128)
            tmp[b, pl.ds(0, H, stride=2), :] = src_ref[pl.ds(0, H), lanes]
            tmp[b, pl.ds(1, H, stride=2), :] = src_ref[pl.ds(H, H), lanes]

    pl.when(at_ref[0] == 0)(functools.partial(put, 0))
    pl.when(at_ref[0] != 0)(functools.partial(put, C))
    for b in range(C // 128):
        out_ref[:, lanes_of(b)] = tmp[b].astype(out_ref.dtype)


def finish_result(at_ref, x_ref, own_ref, other_ref, vec_ref, out_ref, x_s, tmp):
    def body(start, c):
        x_s[pl.ds(start, RB), :] = add_branch(x_ref, own_ref, other_ref, vec_ref.at[0], 5, at_ref[1], start, RB)
        return c

    row_loop(body)
    by_slot(at_ref, x_s, out_ref, tmp)


def finish_grad(at_ref, g_ref, own_ref, other_ref, x_ref, vec_ref, out_ref, x_s, tmp):
    def body(start, c):
        at = pl.ds(start, RB)
        dn = own_ref[at, :].astype(F32) + other_ref[at, :].astype(F32)
        x_s[at, :] = g_ref[at, :] + norm_pull(dn, x_ref[at, :], vec_ref[0, 0:1, :])[0]
        return c

    row_loop(body)
    by_slot(at_ref, x_s, out_ref, tmp)


def add_branch(x_ref, own_ref, other_ref, vec_ref, row, length, start, rows):
    at = pl.ds(start, rows)
    y = own_ref[at, :].astype(F32) + other_ref[at, :].astype(F32) + vec_ref[row : row + 1, :]
    return x_ref[at, :] + row_mask(start, rows, length) * y


RB = 128


def row_loop(body, init=0):
    def step(i, c):
        return body(pl.multiple_of(i * RB, RB), c)

    return lax.fori_loop(0, T // RB, step, init)


def mixer_forward(joined, *refs):
    at_ref, x_ref = refs[:2]
    refs = refs[2:]
    if joined:
        own_ref, other_ref, prev_ref = refs[:3]
        refs = refs[3:]
    (vec_ref, inw_ref, inb_ref, sw_ref, sb_ref, ks_ref, skip_ref, fe_ref, fo_ref, ie_ref, io_ref, outw_ref) = refs[:12]
    refs = refs[12:]
    if joined:
        xo_ref = refs[0]
        refs = refs[1:]
    u_ref, qs_ref, g_ref, p_ref, a_s, w0_s, q_s, rhs_e, rhs_o, se, so, rhs2_e, rhs2_o, z_s = refs

    def first(start, c):
        at = pl.ds(start, RB)
        if joined:
            x = add_branch(x_ref, own_ref, other_ref, prev_ref.at[0], 5, at_ref[1], start, RB)
            xo_ref[at, :] = x
        else:
            x = x_ref[at, :]
        xhat, _ = normalize(x)
        a_s[at, :] = (xhat * vec_ref[0, 0:1, :] + vec_ref[0, 1:2, :]).astype(BF)
        return c

    row_loop(first)
    for s in range(3):
        at = pl.ds(s * C, C)
        u_ref[:, at] = dot(a_s[...], inw_ref[0, s]) + inb_ref[0, 0:1, at]
    for b in range(C // 128):
        at = lanes_of(b)
        (w0e, w0o), (w1e, w1o), (w2e, w2o) = short_conv(u_ref, sw_ref.at[0], sb_ref.at[0], b)
        w0_s[pl.ds(0, H), at] = w0e
        w0_s[pl.ds(H, H), at] = w0o
        qe, qo = w2e * w1e, w2o * w1o
        q_s[pl.ds(0, H), at] = qe
        q_s[pl.ds(H, H), at] = qo
        put_split(rhs_e, qe, 0, at)
        put_split(rhs_o, qo, 0, at)
    se[...] = dot(fe_ref[...], rhs_e[...])
    so[...] = dot(fo_ref[...], rhs_o[...])
    for b in range(C // 128):
        at = lanes_of(b)
        spec = butterfly(se, so, at)
        for i, v in enumerate(spec):
            qs_ref[i, :, at] = v
        y = spectrum_product(spec, [ks_ref[0, i, :, at] for i in range(4)], False)
        put_inverse(rhs2_e, rhs2_o, y, at)
    se[pl.ds(0, H), :] = dot(ie_ref[...], rhs2_e[...])
    se[pl.ds(H, H), :] = dot(io_ref[...], rhs2_o[...])

    def last(start, c):
        at = pl.ds(start, RB)
        g = se[at, :] + skip_ref[0, 0:1, :] * q_s[at, :]
        g_ref[at, :] = g
        z_s[at, :] = (g * w0_s[at, :]).astype(BF)
        return c

    row_loop(last)
    p_ref[...] = dot(z_s[...], outw_ref[0]).astype(BF)


def gelu_parts(h):
    c0 = math.sqrt(2 / math.pi)
    hh = h * h
    t = jnp.tanh(c0 * (h + 0.044715 * (hh * h)))
    half = 0.5 * (1.0 + t)
    return half, t, hh, c0


def collect(j, acc, part):
    @pl.when(j == 0)
    def _():
        acc[...] = part

    @pl.when(j > 0)
    def _():
        acc[...] += part


def ff_forward(at_ref, x_ref, own_ref, other_ref, vec_ref, up_ref, upb_ref, dn_ref, xo_ref, h_ref, p_ref, b_s, acc):
    j = pl.program_id(0)

    @pl.when(j == 0)
    def _():
        def first(start, c):
            at = pl.ds(start, RB)
            x = add_branch(x_ref, own_ref, other_ref, vec_ref.at[0], 4, at_ref[1], start, RB)
            xo_ref[at, :] = x
            xhat, _ = normalize(x)
            b_s[at, :] = (xhat * vec_ref[0, 2:3, :] + vec_ref[0, 3:4, :]).astype(BF)
            return c

        row_loop(first)

    h = dot(b_s[...], up_ref[0]) + upb_ref[0]
    h_ref[...] = h
    half, _, _, _ = gelu_parts(h)
    collect(j, acc, dot((h * half).astype(BF), dn_ref[0]))

    @pl.when(j == pl.num_programs(0) - 1)
    def _():
        p_ref[...] = acc[...].astype(BF)


def ff_backward(joined, *refs):
    at_ref, g_ref = refs[:2]
    refs = refs[2:]
    if joined:
        own_ref, other_ref, xn_ref, nvec_ref = refs[:4]
        refs = refs[4:]
    x_ref, h_ref, vec_ref, up_ref, dn_ref = refs[:5]
    refs = refs[5:]
    if joined:
        go_ref, ngrad_ref = refs[:2]
        refs = refs[2:]
    e_ref, dh_ref, dm_ref, b_ref, gupb_ref, gdnb_ref, p_ref, acc = refs
    j = pl.program_id(0)

    @pl.when(j == 0)
    def _():
        def first(start, c):
            at = pl.ds(start, RB)
            g = g_ref[at, :]
            sums, s1, s2 = c
            if joined:
                dn = own_ref[at, :].astype(F32) + other_ref[at, :].astype(F32)
                dx, dg = norm_pull(dn, xn_ref[at, :], nvec_ref[0, 0:1, :])
                g = g + dx
                go_ref[at, :] = g
                s1 = s1 + jnp.sum(dg, 0, keepdims=True)
                s2 = s2 + jnp.sum(dn, 0, keepdims=True)
            dm = (row_mask(start, RB, at_ref[1]) * g).astype(BF)
            dm_ref[at, :] = dm
            xhat, _ = normalize(x_ref[at, :])
            b_ref[at, :] = (xhat * vec_ref[0, 2:3, :] + vec_ref[0, 3:4, :]).astype(BF)
            return sums + jnp.sum(dm.astype(F32), 0, keepdims=True), s1, s2

        zero = jnp.zeros((1, D), F32)
        sums, s1, s2 = row_loop(first, (zero, zero, zero))
        gdnb_ref[...] = sums
        if joined:
            ngrad_ref[0:1, :] = s1
            ngrad_ref[1:2, :] = s2

    h = h_ref[...]
    half, t, hh, c0 = gelu_parts(h)
    e_ref[...] = (h * half).astype(BF)
    slope = half + 0.5 * c0 * h * (1.0 - t * t) * (1.0 + 3 * 0.044715 * hh)
    dh = (dot_nt(dm_ref[...], dn_ref[0]) * slope).astype(BF)
    dh_ref[...] = dh
    gupb_ref[...] = jnp.sum(dh.astype(F32), 0, keepdims=True)
    collect(j, acc, dot_nt(dh, up_ref[0]))

    @pl.when(j == pl.num_programs(0) - 1)
    def _():
        p_ref[...] = acc[...].astype(BF)


FIRST, SECOND = 5, 6


def put_pieces(at_ref, ref, first, value):
    for n in range(value.shape[0] // PIECE):
        block = first + n // 4
        at = lax.rem(block - at_ref[FIRST] + 4, 4), lax.rem(n % 4 - at_ref[SECOND] + 4, 4), pl.ds(0, PIECE)
        ref[at] = value[n * PIECE : (n + 1) * PIECE]


def put_halves(at_ref, keep_ref, give_ref, first, low, high):
    @pl.when(at_ref[4] == 0)
    def _():
        put_pieces(at_ref, keep_ref, first, low)
        put_pieces(Swapped(at_ref), give_ref, first, high)

    @pl.when(at_ref[4] != 0)
    def _():
        put_pieces(at_ref, keep_ref, first, high)
        put_pieces(Swapped(at_ref), give_ref, first, low)


class Swapped:
    def __init__(self, at_ref):
        self.at_ref = at_ref

    def __getitem__(self, i):
        return self.at_ref[{FIRST: SECOND, SECOND: FIRST}.get(i, i)]


def ff_weights(at_ref, e_ref, dm_ref, b_ref, dh_ref, keep_ref, give_ref):
    j = pl.program_id(0)
    down = dot_tn(e_ref[...], dm_ref[...]).astype(BF)
    up = dot_tn(dh_ref[...], b_ref[...]).astype(BF)
    put_halves(at_ref, keep_ref, give_ref, 2 * j, down, up)


def mixer_backward(
    last, at_ref, g_in_ref, own_ref, other_ref, x1_ref, x0_ref, u_ref, qs_ref, g_ref, ks_ref, vec_ref, inw_ref, outw_ref,
    sw_ref, sb_ref, skip_ref, fe_ref, fo_ref, ie_ref, io_ref,
    go_ref, ngrad_ref, goutb_ref, ginb_ref, gsw_ref, gsb_ref, gskip_ref, dk_ref, p_ref, dy_ref, a_ref, z_ref, du_ref,
    nown_ref, dz_s, dg_s, w1_s, w2_s, dw0_s, rhs_e, rhs_o, se, so, rhs2_e, rhs2_o, inv_s,
):
    def first(start, c):
        at = pl.ds(start, RB)
        sums, s1, s2 = c
        dn = own_ref[at, :].astype(F32) + other_ref[at, :].astype(F32)
        dx, dg = norm_pull(dn, x1_ref[at, :], vec_ref[0, 2:3, :])
        g = g_in_ref[at, :] + dx
        go_ref[at, :] = g
        dy = (row_mask(start, RB, at_ref[1]) * g).astype(BF)
        dy_ref[at, :] = dy
        xhat, _ = normalize(x0_ref[at, :])
        a_ref[at, :] = (xhat * vec_ref[0, 0:1, :] + vec_ref[0, 1:2, :]).astype(BF)
        return (
            sums + jnp.sum(dy.astype(F32), 0, keepdims=True),
            s1 + jnp.sum(dg, 0, keepdims=True),
            s2 + jnp.sum(dn, 0, keepdims=True),
        )

    zero = jnp.zeros((1, D), F32)
    sums, s1, s2 = row_loop(first, (zero, zero, zero))
    goutb_ref[...] = sums
    ngrad_ref[0:1, :] = s1
    ngrad_ref[1:2, :] = s2
    dz_s[...] = dot_nt(dy_ref[...], outw_ref[0])
    halves = (pl.ds(0, H), pl.ds(H, H))
    for b in range(C // 128):
        at = lanes_of(b)
        w0, w1, w2 = short_conv(u_ref, sw_ref.at[0], sb_ref.at[0], b)
        dskip = 0.0
        for i, (rows, rhs) in enumerate(zip(halves, (rhs_e, rhs_o))):
            dz, g = dz_s[rows, at], g_ref[rows, at]
            z_ref[rows, at] = (g * w0[i]).astype(BF)
            dw0_s[rows, at] = dz * g
            dg = dz * w0[i]
            dg_s[rows, at] = dg
            dskip = dskip + jnp.sum(dg * (w2[i] * w1[i]), 0, keepdims=True)
            w1_s[rows, at] = w1[i]
            w2_s[rows, at] = w2[i]
            put_split(rhs, dg, 0, at)
        gskip_ref[0:1, at] = dskip
    se[...] = dot(fe_ref[...], rhs_e[...])
    so[...] = dot(fo_ref[...], rhs_o[...])
    for b in range(C // 128):
        at = lanes_of(b)
        spec = butterfly(se, so, at)
        put_inverse(rhs2_e, rhs2_o, spectrum_product(spec, [ks_ref[0, i, :, at] for i in range(4)], True), at)
        put_inverse(
            rhs2_e, rhs2_o, spectrum_product(spec, [qs_ref[i, :, at] for i in range(4)], True), pl.ds(C + b * 128, 128)
        )
    inv_s[pl.ds(0, H), :] = dot(ie_ref[...], rhs2_e[...])
    inv_s[pl.ds(H, H), :] = dot(io_ref[...], rhs2_o[...])
    dk_ref[...] = inv_s[:, pl.ds(C, C)]
    for b in range(C // 128):
        at = lanes_of(b)
        dw = [[dw0_s[rows, at] for rows in halves], [], []]
        for rows in halves:
            dq = inv_s[rows, at] + skip_ref[0, 0:1, at] * dg_s[rows, at]
            dw[1].append(dq * w2_s[rows, at])
            dw[2].append(dq * w1_s[rows, at])
        for s in range(3):
            to = lanes_of(s * (C // 128) + b)
            ue, uo = u_ref[halves[0], to], u_ref[halves[1], to]
            t0, t1, t2 = (sw_ref[0, j : j + 1, to] for j in range(3))
            de, do = dw[s]
            de_u, do_u = up_one(de), up_one(do)
            due = (t2 * de + t1 * do + t0 * de_u).astype(BF)
            duo = (t2 * do + t1 * de_u + t0 * do_u).astype(BF)
            du_ref[halves[0], to] = due
            du_ref[halves[1], to] = duo
            uo_d = down_one(uo)
            gsw_ref[0:1, to] = jnp.sum(de * down_one(ue) + do * uo_d, 0, keepdims=True)
            gsw_ref[1:2, to] = jnp.sum(de * uo_d + do * ue, 0, keepdims=True)
            gsw_ref[2:3, to] = jnp.sum(de * ue + do * uo, 0, keepdims=True)
            gsb_ref[0:1, to] = jnp.sum(de + do, 0, keepdims=True)
            ginb_ref[0:1, to] = jnp.sum(due.astype(F32) + duo.astype(F32), 0, keepdims=True)
    part = dot_nt(du_ref[:, pl.ds(0, C)], inw_ref[0, 0])
    for s in range(1, 3):
        part += dot_nt(du_ref[:, pl.ds(s * C, C)], inw_ref[0, s])
    p_ref[...] = part.astype(BF)
    nown_ref[...] = jnp.zeros_like(nown_ref)
    if last:

        def terms(start, c):
            at = pl.ds(start, RB)
            dn = p_ref[at, :].astype(F32)
            xhat, _ = normalize(x0_ref[at, :])
            return c[0] + jnp.sum(dn * xhat, 0, keepdims=True), c[1] + jnp.sum(dn, 0, keepdims=True)

        s1, s2 = row_loop(terms, (zero, zero))
        nown_ref[0:1, :] = s1
        nown_ref[1:2, :] = s2


def put_split_rows(value):
    hi = value.astype(BF).astype(F32)
    return jnp.concatenate([hi, value - hi], 0).astype(BF)


def put_pack(at_ref, ref, rows, half):
    for n in range(16):
        at = lax.rem(n // 4 - at_ref[FIRST] + 4, 4), lax.rem(n % 4 - at_ref[SECOND] + 4, 4), pl.ds(PIECE, 16)
        first = half * (PACK // 2) + n * 8
        ref[at] = put_split_rows(rows[first : first + 8, :])


def mixer_weights(packed, at_ref, *refs):
    if packed:
        pack_ref, refs = refs[0], refs[1:]
    a_ref, du_ref, z_ref, dy_ref, keep_ref, give_ref = refs
    for n in range(2):
        low = dot_tn(a_ref[...], du_ref[:, pl.ds(n * C, C)]).astype(BF)
        if n == 0:
            high = dot_tn(a_ref[...], du_ref[:, pl.ds(2 * C, C)]).astype(BF)
        else:
            high = dot_tn(dy_ref[...], z_ref[...]).astype(BF)
        put_halves(at_ref, keep_ref, give_ref, 2 * n, low, high)
    if packed:

        @pl.when(at_ref[4] == 0)
        def _():
            put_pack(at_ref, keep_ref, pack_ref, 0)
            put_pack(Swapped(at_ref), give_ref, pack_ref, 1)

        @pl.when(at_ref[4] != 0)
        def _():
            put_pack(at_ref, keep_ref, pack_ref, 1)
            put_pack(Swapped(at_ref), give_ref, pack_ref, 0)


def add_parts(count, sides, *refs):
    ins, outs = refs[:count], refs[count:]
    lane = 0
    for side in range(sides):
        some = ins[side * count // sides : (side + 1) * count // sides]
        lanes = slice(lane, lane + some[0].shape[-1])
        lane = lanes.stop
        for i, out in enumerate(outs):
            total = functools.reduce(jnp.add, [(r[i] if len(outs) > 1 else r[...]).astype(F32) for r in some])
            rows = (slice(None),) * (total.ndim - 2)
            out[rows + (slice(0, PIECE), lanes)] = total[rows + (slice(0, PIECE),)].astype(BF)
            if total.shape[-2] > PIECE:
                for n in range(total.shape[0] if total.ndim > 2 else 1):
                    value = total[n] if total.ndim > 2 else total
                    value = value[PIECE : PIECE + 8] + value[PIECE + 8 : PIECE + 16]
                    to = (n, slice(PIECE, PIECE + 16)) if total.ndim > 2 else slice(PIECE, PIECE + 16)
                    out[to] = put_split_rows(value)


def gather_block(at_ref, ref, block, tmp, first_lane, pack_ref=None, first=0):
    width = tmp.shape[-1]
    lanes = slice(first_lane, first_lane + width)
    for m in range(4):
        if len(ref.shape) == 5:
            by_x = (at_ref[4] == 0) != isinstance(at_ref, Swapped)
            at = 0, jnp.where(by_x, m, block), jnp.where(by_x, block, m)
        else:
            at = lax.rem(at_ref[FIRST] - block + 4, 4), lax.rem(at_ref[SECOND] - m + 4, 4)
        tmp[pl.ds(m * PIECE, PIECE), :] = ref[at + (slice(0, PIECE), lanes)].astype(F32)
        if pack_ref is not None:
            extra = ref[at + (slice(PIECE, PIECE + 16),)].astype(F32)
            pack_ref[pl.ds(pl.multiple_of(first + m * 8, 8), 8), :] = extra[:8] + extra[8:]


def gather_half(at_ref, half, refs, *args):
    own = at_ref[4] == half
    pl.when(own)(lambda: gather_block(at_ref, refs[0], *args))
    pl.when(jnp.logical_not(own))(lambda: gather_block(Swapped(at_ref), refs[1], *args))


def place_ff(at_ref, *refs):
    ins, (gup_ref, gdn_ref, tmp) = refs[:2], refs[-3:]
    block = pl.program_id(0)
    gather_half(at_ref, 0, ins, block, tmp, 0)
    gdn_ref[0] = tmp[...]
    gather_half(at_ref, 1, ins, block, tmp, 0)
    gup_ref[0] = tmp[...].T


def place_mixer(packed, lane, at_ref, *refs):
    ins, outs, tmp = refs[:2], refs[2:-1], refs[-1]
    gin_ref, gout_ref = outs[:2]
    step = pl.program_id(0)
    args = ins, lax.rem(step, 4), tmp, lane, outs[2] if packed else None, step * 32
    gather_half(at_ref, step // 4, *args)

    @pl.when(step < 6)
    def _():
        gin_ref[0, 0] = tmp[...]

    @pl.when(step >= 6)
    def _():
        gout_ref[0] = tmp[...].T


PACK = 256
SHARED = 72
LAYER_ROWS = 92


def pack_small(at_ref, gnet_ref, gout_ref, nown_ref, *refs):
    out_ref = refs[-1]
    out_ref[...] = jnp.zeros_like(out_ref)
    out_ref[0:NET, :] = gnet_ref[...]
    for j in range(2):
        for i in range(2):
            row = NET + 2 * j + i
            out_ref[row : row + 1, :] = nown_ref[j : j + 1, i * C : (i + 1) * C]
    for l in range(2):
        n0, n1, gdnb, goutb, gupb, ginb, gsw, gsb, gskip = refs[9 * l : 9 * l + 9]
        row = SHARED + LAYER_ROWS * l

        def put(value):
            nonlocal row
            out_ref[row : row + value.shape[0], :] = value
            row += value.shape[0]

        for ref in (n0, n1, gdnb, goutb):
            put(jnp.where(at_ref[0] == 0, ref[:, :C], ref[:, C:]))
        for ref in (gupb, ginb, gsw, gsb):
            for j in range(ref.shape[0]):
                for i in range(ref.shape[1] // C):
                    put(ref[j : j + 1, i * C : (i + 1) * C])
        put(gskip[...])
        put(gout_ref[l])


def sds(shape, dtype=F32):
    return jax.ShapeDtypeStruct(shape, dtype)


def params(us):
    return dict(
        compiler_params=pltpu.CompilerParams(vmem_limit_bytes=VMEM_LIMIT),
        cost_estimate=pl.CostEstimate(flops=int(us * 1e9), bytes_accessed=10000, transcendentals=0),
    )


SMEM = pl.BlockSpec(memory_space=pltpu.SMEM)
WHOLE = pl.BlockSpec(memory_space=pltpu.VMEM)
ANY = pl.BlockSpec(memory_space=pl.ANY)
SLOTS = pltpu.VMEM((C // 128, T, 128), F32)


def layer_of(x, l):
    rest = x.ndim - 1
    return pl.BlockSpec((1,) + x.shape[1:], lambda *_: (l,) + (0,) * rest, pipeline_mode=pl.Buffered(1))


def fixed(shape):
    return pl.BlockSpec(shape, lambda *_: (0,) * len(shape))


def spectrum_scratch():
    return [pltpu.VMEM((3 * H, C), BF)] * 2 + [pltpu.VMEM((T, C), F32)] * 2


def run_filter_forward(at, first, inner, bias, out):
    layers = out.shape[0]
    return pl.pallas_call(
        filter_forward,
        in_specs=[SMEM] + [WHOLE] * 8,
        out_specs=[WHOLE] * 5,
        out_shape=[
            sds((layers, 4, H, C)), sds((3, T, 128)), sds((3, T, 128)), sds((2, 128, 128)), sds((layers, 128, C)),
        ],
        scratch_shapes=[pltpu.VMEM((128, 128), F32), pltpu.VMEM((8, 128), F32), pltpu.VMEM((T, C), F32)]
        + spectrum_scratch(),
        name="filter_forward",
        **params(12),
    )(at, FEATS, TIMES, first, inner, bias, out, FE, FO)


def run_filter_backward(at, inner, out, sines, cosines, dks):
    return pl.pallas_call(
        filter_backward,
        in_specs=[SMEM] + [WHOLE] * 8,
        out_specs=[WHOLE] * 2,
        out_shape=[sds((2, NET, C)), sds((NET, C))],
        name="filter_backward",
        **params(8),
    )(at, FEATS, TIMES, inner, out, sines, cosines, *dks)


def run_arrange(at, own, other):
    return pl.pallas_call(
        arrange,
        in_specs=[SMEM, WHOLE, WHOLE],
        out_specs=WHOLE,
        out_shape=sds((T, D)),
        scratch_shapes=[SLOTS],
        name="arrange",
        **params(2),
    )(at, own, other)


def run_finish_result(at, x, own, other, vec, l):
    return pl.pallas_call(
        finish_result,
        grid=(1,),
        in_specs=[SMEM, WHOLE, WHOLE, WHOLE, layer_of(vec, l)],
        out_specs=WHOLE,
        out_shape=sds((T, C), BF),
        scratch_shapes=[pltpu.VMEM((T, D), F32), SLOTS],
        name="finish_result",
        **params(3),
    )(at, x, own, other, vec)


def run_finish_grad(at, g, own, other, x, vec, l, after):
    return pl.pallas_call(
        functools.partial(body_without, finish_grad, 6, len(after)),
        grid=(1,),
        in_specs=[SMEM, WHOLE, WHOLE, WHOLE, WHOLE, layer_of(vec, l)] + [ANY] * len(after),
        out_specs=WHOLE,
        out_shape=sds((T, C)),
        scratch_shapes=[pltpu.VMEM((T, D), F32), SLOTS],
        name="finish_grad",
        **params(4),
    )(at, g, own, other, x, vec, *after)


def run_mixer_forward(l, joint, at, x, vec, inw, inb, sw, sb, ks, skip, outw, after):
    joined = joint is not None
    args = [at, x] + (list(joint) + [vec] if joined else [])
    specs = [SMEM] + [WHOLE] * 3 + [layer_of(vec, l - 1)] if joined else [SMEM, WHOLE]
    args += [vec, inw, inb, sw, sb, ks, skip, FE, FO, IE, IO, outw]
    specs += [layer_of(m, l) for m in (vec, inw, inb, sw, sb, ks, skip)] + [WHOLE] * 4 + [layer_of(outw, l)]
    outs = ([sds((T, D))] if joined else []) + [sds((T, 3 * C)), sds((4, H, C)), sds((T, C)), sds((T, D), BF)]
    return pl.pallas_call(
        functools.partial(body_without, functools.partial(mixer_forward, joined), len(args), len(after)),
        grid=(1,),
        in_specs=specs + [ANY] * len(after),
        out_specs=[WHOLE] * len(outs),
        out_shape=outs,
        scratch_shapes=[pltpu.VMEM((T, D), BF), pltpu.VMEM((T, C), F32), pltpu.VMEM((T, C), F32)]
        + spectrum_scratch()
        + [pltpu.VMEM((6 * H, C), BF)] * 2
        + [pltpu.VMEM((T, C), BF)],
        name="mixer_forward",
        **params(11),
    )(*args, *after)


FC = 512


def up_spec(l):
    return pl.BlockSpec((1, D, FC), lambda j: (l, 0, j))


def down_spec(l):
    return pl.BlockSpec((1, FC, D), lambda j: (l, j, 0))


def hidden_spec(rows, width=FC):
    return pl.BlockSpec((rows, width), lambda j: (0, j))


def run_ff_forward(l, at, x, own, other, vec, up, upb, dn, after):
    return pl.pallas_call(
        functools.partial(body_without, ff_forward, 8, len(after)),
        grid=(FH // FC,),
        in_specs=[
            SMEM, fixed((T, D)), fixed((T, D)), fixed((T, D)), layer_of(vec, l),
            up_spec(l), pl.BlockSpec((1, 1, FC), lambda j: (l, 0, j)), down_spec(l),
        ] + [ANY] * len(after),
        out_specs=[fixed((T, D)), hidden_spec(T), fixed((T, D))],
        out_shape=[sds((T, D)), sds((T, FH)), sds((T, D), BF)],
        scratch_shapes=[pltpu.VMEM((T, D), BF), pltpu.VMEM((T, D), F32)],
        name="ff_forward",
        **params(10),
    )(at, x, own, other, vec, up, upb, dn, *after)


def run_ff_backward(l, at, g, joint, x, h, vec, up, dn, after):
    joined = joint is not None
    args = [at, g] + (list(joint) + [vec] if joined else []) + [x, h, vec, up, dn]
    specs = [SMEM, fixed((T, D))]
    if joined:
        specs += [fixed((T, D))] * 3 + [layer_of(vec, l + 1)]
    specs += [fixed((T, D)), hidden_spec(T), layer_of(vec, l), up_spec(l), down_spec(l)]
    out_specs = [fixed((T, D)), fixed((2, D))] if joined else []
    outs = [sds((T, D)), sds((2, D))] if joined else []
    out_specs += [hidden_spec(T), hidden_spec(T), fixed((T, D)), fixed((T, D)), hidden_spec(1), fixed((1, D)), fixed((T, D))]
    outs += [
        sds((T, FH), BF), sds((T, FH), BF), sds((T, D), BF), sds((T, D), BF), sds((1, FH)), sds((1, D)), sds((T, D), BF),
    ]
    return pl.pallas_call(
        functools.partial(body_without, functools.partial(ff_backward, joined), len(args), len(after)),
        grid=(FH // FC,),
        in_specs=specs + [ANY] * len(after),
        out_specs=out_specs,
        out_shape=outs,
        scratch_shapes=[pltpu.VMEM((T, D), F32)],
        name="ff_backward",
        **params(10),
    )(*args, *after)


def run_ff_weights(at, e, dm, b, dh):
    wide = FH // 2
    return pl.pallas_call(
        ff_weights,
        grid=(2,),
        in_specs=[SMEM, hidden_spec(T, wide), fixed((T, D)), fixed((T, D)), hidden_spec(T, wide)],
        out_specs=[fixed((4, 4, PIECE, D))] * 2,
        out_shape=[sds((4, 4, PIECE, D), BF)] * 2,
        name="ff_weights",
        **params(7),
    )(at, e, dm, b, dh)


def run_mixer_backward(l, last, at, g_in, own, other, x1, x0, u, qs, g, ks, vec, inw, outw, sw, sb, skip, after):
    args = [at, g_in, own, other, x1, x0, u, qs, g, ks, vec, inw, outw, sw, sb, skip, FE, FO, IE, IO]
    specs = [SMEM] + [WHOLE] * 8 + [layer_of(m, l) for m in (ks, vec, inw, outw, sw, sb, skip)] + [WHOLE] * 4
    outs = [
        sds((T, D)), sds((2, D)), sds((1, D)), sds((1, 3 * C)), sds((3, 3 * C)), sds((1, 3 * C)), sds((1, C)),
        sds((T, C)), sds((T, D), BF), sds((T, D), BF), sds((T, D), BF), sds((T, C), BF), sds((T, 3 * C), BF), sds((2, D)),
    ]
    tc = pltpu.VMEM((T, C), F32)
    return pl.pallas_call(
        functools.partial(body_without, functools.partial(mixer_backward, last), len(args), len(after)),
        grid=(1,),
        in_specs=specs + [ANY] * len(after),
        out_specs=[WHOLE] * len(outs),
        out_shape=outs,
        scratch_shapes=[
            tc, tc, tc, tc, tc, *spectrum_scratch(),
            pltpu.VMEM((6 * H, 2 * C), BF), pltpu.VMEM((6 * H, 2 * C), BF), pltpu.VMEM((T, 2 * C), F32),
        ],
        name="mixer_backward",
        **params(15),
    )(*args, *after)


def run_mixer_weights(at, a, du, z, dy, pack=None):
    packed = [] if pack is None else [pack]
    rows = PIECE + 16 * len(packed)
    return pl.pallas_call(
        functools.partial(mixer_weights, bool(packed)),
        in_specs=[SMEM] + [WHOLE] * (4 + len(packed)),
        out_specs=[WHOLE] * 2,
        out_shape=[sds((4, 4, rows, C), BF)] * 2,
        name="mixer_weights",
        **params(5),
    )(at, *packed, a, du, z, dy)


def run_add(parts, count, after=(), sides=1):
    shape = parts[0].shape[1:] if count > 1 else parts[0].shape
    width = sum(p.shape[-1] for p in parts[:: len(parts) // sides])
    made = pl.pallas_call(
        functools.partial(body_without, functools.partial(add_parts, len(parts), sides), len(parts), len(after)),
        in_specs=[WHOLE] * len(parts) + [ANY] * len(after),
        out_specs=[WHOLE] * count,
        out_shape=[sds(shape[:-1] + (width,), BF)] * count,
        name="add_parts",
        **params(1),
    )(*parts, *after)
    return list(made)


def copy(ref, out_ref):
    out_ref[...] = ref[...]


def run_copy_after(x, after):
    return pl.pallas_call(
        functools.partial(body_without, copy, 1, len(after)),
        in_specs=[WHOLE] + [ANY] * len(after),
        out_specs=WHOLE,
        out_shape=sds(x.shape, x.dtype),
        name="copy_after",
        **params(1),
    )(x, *after)


def run_place(body, at, ins, into, shapes, out_specs, steps, width, name):
    aliases = {} if into is None else {3: 0, 4: 1}
    into = [] if into is None else list(into)
    return pl.pallas_call(
        functools.partial(body_without, body, 3, len(into)),
        grid=(steps,),
        in_specs=[SMEM] + [fixed(m.shape) for m in ins] + [ANY] * len(into),
        out_specs=out_specs,
        out_shape=[sds(s) for s in shapes],
        scratch_shapes=[pltpu.VMEM((4 * PIECE, width), F32)],
        input_output_aliases=aliases,
        name=name,
        **params(6),
    )(at, *ins, *into)


def body_without(body, first, count, *refs):
    body(*refs[:first], *refs[first + count :])


def run_place_ff(l, layers, at, ins, into):
    specs = [
        pl.BlockSpec((1, D, 4 * PIECE), lambda p: (l, 0, p)),
        pl.BlockSpec((1, 4 * PIECE, D), lambda p: (l, p, 0)),
    ]
    return run_place(place_ff, at, ins, into, [(layers, D, FH), (layers, FH, D)], specs, 4, D, "place_ff")


def run_place_mixer(l, layers, at, ins, into, lane):
    packed = ins[0].shape[-2] > PIECE
    specs = [
        pl.BlockSpec((1, 1, C, C), lambda n: (l, jnp.minimum(n, 5) // 2, jnp.minimum(n, 5) % 2, 0)),
        pl.BlockSpec((1, C, C), lambda n: (l, 0, jnp.maximum(n - 6, 0))),
    ] + [fixed((PACK, C))] * packed
    shapes = [(layers, 3, D, C), (layers, C, D)] + [(PACK, C)] * packed
    body = functools.partial(place_mixer, packed, lane)
    return run_place(body, at, ins, into, shapes, specs, 8, C, "place_mixer")


SWAP = [(0, 1), (1, 0)]


def swap(x, axis):
    return lax.ppermute(x, axis, SWAP)


def shift(x, axis, k):
    pairs = []
    for y, x_at, c in np.ndindex(4, 4, 2):
        along_x = (axis == FIRST) == (c == 0)
        to = (y, (x_at + k) % 4) if along_x else ((y + k) % 4, x_at)
        pairs.append(((y * 4 + x_at) * 2 + c, (to[0] * 4 + to[1]) * 2 + c))
    return lax.ppermute(x, ("y", "x", "c"), pairs)


def spread_sum(*halves):
    after = yield [h for pair in halves for h in pair]
    parts = [part for keep, give in halves for part in (keep, swap(give, "c"))]
    blocks = run_add(parts, 4, after, len(halves))
    after = yield blocks
    pieces = run_add([blocks[0]] + [shift(blocks[k], FIRST, k) for k in range(1, 4)], 4, after)
    after = yield pieces
    [piece] = run_add([pieces[0]] + [shift(pieces[m], SECOND, m) for m in range(1, 4)], 1, after)
    yield run_add([piece, swap(piece, "zl")], 1)


def gather_near(piece):
    row = jnp.stack([piece] + [shift(piece, SECOND, m) for m in range(1, 4)])
    mine = jnp.stack([row] + [shift(row, FIRST, k) for k in range(1, 4)])
    return [mine, swap(mine, "c")]


def gather_plane(piece):
    mine = lax.all_gather(piece, ("y", "x"), axis=0, tiled=False)
    mine = mine.reshape(1, 4, 4, *piece.shape)
    return [mine, swap(mine, "c")]


def run_pack_small(at, gnet, gout, nown, small):
    return pl.pallas_call(
        pack_small,
        in_specs=[SMEM] + [WHOLE] * (3 + len(small)),
        out_specs=WHOLE,
        out_shape=sds((PACK, C)),
        name="pack_small",
        **params(2),
    )(at, gnet, gout, nown, *small)


def shards(
    tokens, lengths, norm_gain, norm_bias, in_weight, in_bias, short_weight, short_bias, filter_first, filter_inner,
    filter_biases, filter_out, filter_skip, out_weight, out_bias, up_weight, up_bias, down_weight, down_bias, cotangent,
):
    layers = norm_gain.shape[0]
    half_at = lax.axis_index("zh")
    core = lax.axis_index("c")
    x_at, y_at = lax.axis_index("x"), lax.axis_index("y")
    order = jnp.where(core == 0, x_at, y_at), jnp.where(core == 0, y_at, x_at)
    at = jnp.stack([half_at, lengths[0], x_at, y_at, core, *order]).astype(jnp.int32)

    tokens_other = swap(tokens, "zh")
    rows = jnp.stack(
        [norm_gain[:, 0], norm_bias[:, 0], norm_gain[:, 1], norm_bias[:, 1], out_bias, down_bias, out_bias, out_bias], 1
    )
    other = swap(rows, "zh")
    low = half_at == 0
    vec = jnp.concatenate([jnp.where(low, rows, other), jnp.where(low, other, rows)], 2)

    ks, sines, cosines, inner, fout = run_filter_forward(at, filter_first, filter_inner, filter_biases, filter_out)

    x = run_arrange(at, tokens, tokens_other)
    inw = in_weight.transpose(0, 2, 1, 3)
    inb = in_bias.reshape(layers, 1, 3 * C)
    sw = short_weight.reshape(layers, 3, 3 * C)
    sb = short_bias.reshape(layers, 1, 3 * C)
    skip = filter_skip.reshape(layers, 1, C)
    upb = up_bias.reshape(layers, 1, FH)

    cot = run_copy_after(cotangent, [x])
    grad = run_arrange(at, cotangent, swap(cot, "zh"))
    saved = []
    joint = None
    for l in range(layers):
        after = [cot] if l == 0 else []
        made = run_mixer_forward(l, joint, at, x, vec, inw, inb, sw, sb, ks, skip, out_weight, after)
        if joint is not None:
            x, made = made[0], made[1:]
        u, qs, g, p = made
        after = [grad] if l == 0 else []
        x1, h, p2 = run_ff_forward(l, at, x, p, swap(p, "zh"), vec, up_weight, upb, down_weight, after)
        saved.append((x, u, qs, g, x1, h))
        joint = (p2, swap(p2, "zh")) if l < layers - 1 else p2
        x = x1

    joint = None
    sums = []
    small = [None] * layers
    norms = {}

    def advance(after):
        made = []
        for entry in sums:
            try:
                entry[1] = entry[0].send(after) if entry[1] else next(entry[0])
            except StopIteration:
                pass
            made += entry[1]
        return made

    def begin(*halves):
        sums.append([spread_sum(*halves), []])

    result = None
    waits = []
    for l in reversed(range(layers)):
        x0, u, qs, g, x1, h = saved[l]
        made = run_ff_backward(l, at, grad, joint, x1, h, vec, up_weight, down_weight, waits)
        if joint is not None:
            grad, norms[l + 1] = made[:2]
            made = made[2:]
        e, dh, dm, b, gupb, gdnb, p = made
        p_other = swap(p, "zh")
        halves = run_ff_weights(at, e, dm, b, dh)
        if l == 0:
            begin(halves)
        waits = advance([p]) if l == 0 else list(halves)
        if l == layers - 1:
            p2 = run_copy_after(p2, [p_other])
            waits.append(p2)
        made = run_mixer_backward(
            l, l == 0, at, grad, p, p_other, x1, x0, u, qs, g, ks, vec, inw, out_weight, sw, sb, skip, waits
        )
        grad, norm1, goutb, ginb, gsw, gsb, gskip, dk, p, dy, a, z, du, nown = made
        joint = (p, swap(p, "zh"), x0)
        small[l] = (norm1, gdnb, goutb, gupb, ginb, gsw, gsb, gskip, dk)
        pack = None
        if l == 0:
            norms[0] = jnp.zeros_like(nown)
            gfout, gnet = run_filter_backward(at, inner, fout, sines, cosines, [s[-1] for s in small])
            pack = run_pack_small(at, gnet, gfout, nown, [m for l in range(layers) for m in (norms[l], *small[l][:-1])])
        mixer_halves = run_mixer_weights(at, a, du, z, dy, pack)
        if l == 0:
            begin(mixer_halves)
        else:
            begin(halves, mixer_halves)
        waits = advance([p])
        if l == layers - 1:
            result = run_finish_result(at, saved[l][4], p2, swap(p2, "zh"), vec, l)
            waits.append(result)

    grad = run_finish_grad(at, grad, *joint, vec, 0, waits)
    for _ in range(4):
        advance([])
    later, ff, mixer = (entry[1][0] for entry in sums)
    later = gather_plane(later)
    ff_out = run_place_ff(1, layers, at, later, None)
    mixer_out = run_place_mixer(1, layers, at, later, None, D)
    ff_out = run_place_ff(0, layers, at, gather_near(ff), ff_out)
    *mixer_out, pack = run_place_mixer(0, layers, at, gather_near(mixer), mixer_out, 0)

    net = pack[:SHARED]
    net = net + swap(net, "zh")
    pack = pack[SHARED:].reshape(layers, -1, C)
    first_norm = jnp.where(low, net[NET : NET + 4 : 2], net[NET + 1 : NET + 4 : 2])
    norm_rows = jnp.stack([jnp.concatenate([first_norm, pack[0, 2:4]]), pack[1, :4]])

    def apart(a):
        return jnp.stack([a[..., :NET], a[..., NET:]])

    return (
        result,
        grad,
        norm_rows[:, 0:4:2],
        norm_rows[:, 1:4:2],
        mixer_out[0].transpose(0, 2, 1, 3),
        pack[:, 10:13],
        pack[:, 13:22].reshape(short_weight.shape),
        pack[:, 22:25],
        apart(net[:EMB, 256:]),
        jnp.stack([apart(net[:NET, :128]), apart(net[:NET, 128:256])], 1),
        apart(net[40:43, 256:]),
        pack[:, 26:90],
        pack[:, 25],
        mixer_out[1],
        pack[:, 5],
        ff_out[0],
        pack[:, 6:10].reshape(layers, FH),
        ff_out[1],
        pack[:, 4],
    )


def solution(mesh):
    names = ("zl", "y", "x", "c", "zh")
    fine = Mesh(mesh.devices.reshape(2, 4, 4, 2, 2), names)
    dp = ("zl", "y", "x", "c")
    rows = P(dp, "zh")
    third, fourth = P(None, None, "zh"), P(None, None, None, "zh")
    second, middle = P(None, "zh"), P(None, "zh", None)
    placed = (
        rows, P(dp), third, third, fourth, third, fourth, third, P(), P(), P(), third, second, middle, second, third,
        second, middle, second, rows,
    )
    return jax.shard_map(
        shards,
        mesh=fine,
        in_specs=placed,
        out_specs=(
            rows, rows, third, third, fourth, third, fourth, third, P(), P(), P(), third, second, middle, second, third,
            second, middle, second,
        ),
        check_vma=False,
    )
```

time: 1080 us -> 524 us (0.49)
  waiting for transfers between devices: 620 us -> 147 us
  Pallas kernels: 113 us -> 221 us
  blocking collectives: 94.5 us -> 0 us
  other arithmetic: 58.4 us -> 2.29 us
  local copies, waits for them, and re-layouts: 66.3 us -> 36.6 us
  matrix products: 22.8 us -> 0 us
  starting transfers between devices: 80.3 us -> 92.4 us
    unnamed x20 -> x1, waiting for transfers between devices: 288 us -> 0.02 us
    all_gather x4 -> x1, waiting for transfers between devices: 164 us -> 31.5 us  [gather_plane(): mine = lax.all_gather(piece, ('y', 'x'), axis=0, tiled=False)]
    pallas_call x9 -> x37, Pallas kernels: 113 us -> 221 us  [the longest x2 34.8 us: run_mixer_backward(): pl.pallas_call(functools.partial(body_without, functools.partial(mixer_ba...]
    all_gather x5 -> x0, blocking collectives: 94.5 us -> none  [total(): mine = lax.all_gather(mine, PLANE, axis=0, tiled=True)]
    ppermute x39 -> x22, waiting for transfers between devices: 126 us -> 75.1 us  [swap(): return lax.ppermute(x, axis, SWAP)]
    reduce_scatter x2 -> x0, waiting for transfers between devices: 42.5 us -> none  [total(): mine = lax.psum_scatter(mine, PLANE, scatter_dimension=0, tiled=True)]
    ppermute x0 -> x30, waiting for transfers between devices: none -> 40 us  [shift(): return lax.ppermute(x, ('y', 'x', 'c'), pairs)]
    ppermute x0 -> x30, starting transfers between devices: none -> 36.5 us  [shift(): return lax.ppermute(x, ('y', 'x', 'c'), pairs)]
  transfers between devices with their start and end apart: 52 -> 53, of which waited for: 26 -> 19; matrix products, arithmetic and copies ran while one was open for 12% -> 3% of each run, Pallas kernels for 5% -> 30%
where the time goes in v2:
time: 524 us; the launch traced here: 514 us
  Pallas kernels  221 us (42%)
  waiting for transfers between devices  147 us (28%)
  starting transfers between devices  92.4 us (18%)
  local copies, waits for them, and re-layouts  36.6 us (7%)
  between operations  15.3 us (3%)
    ppermute x22, waiting for transfers between devices, swap(): return lax.ppermute(x, axis, SWAP)  75.1 us
    ppermute x22, starting transfers between devices, swap(): return lax.ppermute(x, axis, SWAP)  55.9 us
    ppermute x30, waiting for transfers between devices, shift(): return lax.ppermute(x, ('y', 'x', 'c'), pairs)  40 us
    ppermute x30, starting transfers between devices, shift(): return lax.ppermute(x, ('y', 'x', 'c'), pairs)  36.5 us
    pallas_call x2, Pallas kernels, run_mixer_backward(): pl.pallas_call(functools.partial(body_without, functools.partial(mixer_ba...  34.8 us
    all_gather x1, waiting for transfers between devices, gather_plane(): mine = lax.all_gather(piece, ('y', 'x'), axis=0, tiled=False)  31.5 us
    pallas_call x12, Pallas kernels, run_add(): pl.pallas_call(functools.partial(body_without, functools.partial(add_part...  30.6 us
    pallas_call x4, Pallas kernels, run_place(): pl.pallas_call(functools.partial(body_without, body, 3, len(into)), grid=...  27.8 us
  transfers between devices with their start and end apart: 53, of which 19 were waited for; matrix products, arithmetic and copies ran while one was open for 3% of the time, Pallas kernels for 30%

profile of v2, /device:TPU:1, one launch (start us, length us, event | category | flops | bytes accessed | tf_op | source)
XLA Modules:
  0.0 514.4 jit_solution(4599518259075374271)
XLA Ops:
  9.5 4.5 collective-permute-start.1
  18.0 9.3 %filter_forward.1 = (f32[2,4,256,384]{3,2,1,0:T(8,128)}, f32[3,512,128]{2,1,0:T(8,128)}, f32[3,512,128]{2,1,0:T(8,128)}, f32[2,128,128]{2,1,0:T(8,128)}, f32[2,128,384]{2,1,0:T(8,128)}) custom-call(s32[7]{0:T(128)} %stack.149.at_ref.refs_0_, f32[512,128]{1,0:T(8,128)} %constant.31.clone.feats_ref, f32[512,128]{1,0:T(8,128)} %constant.32.clone.times_ref, ...), custom_call_target="tpu_custom_call" | custom-call | flops 12000000000 | bytes 10000 | tf_op jit(solution)/shard_map/filter_forward/pallas_call | solution.py:784
  31.1 2.5 arrange.2.refs_1_.refs_5_.refs_4_
  35.4 10.9 %mixer_forward.2 = (f32[512,1152]{1,0:T(8,128)}, f32[4,256,384]{2,1,0:T(8,128)}, f32[512,384]{1,0:T(8,128)}, bf16[512,768]{1,0:T(8,128)(2,1)}) custom-call(s32[7]{0:T(128)} %stack.149.at_ref.refs_0_, f32[512,768]{1,0:T(8,128)} %arrange.2.refs_1_.refs_5_.refs_4_, f32[2,8,768]{2,1,0:T(8,128)} %pad_maximum_fusion.5.refs_2_.refs_4_.refs_5_.vec_ref.refs_10_.refs_8_, ...), custom_call_target="tpu_custom_call" | custom-call | flops 11000000512 | bytes 10000 | tf_op jit(solution)/shard_map/mixer_forward/pallas_call | solution.py:854
  46.3 2.9 collective-permute-start.2
  49.9 24.6 %collective-permute-done.3.other_ref = bf16[512,384]{1,0:T(8,128)(2,1)S(1)} collective-permute-done((bf16[512,384]{1,0:T(8,128)(2,1)S(1)}, bf16[512,384]{1,0:T(8,128)(2,1)S(1)}, u32[]{:S(2)}, u32[]{:S(2)}) %collective-permute-start.3) | collective-permute-done | bytes 393248 | tf_op jit(solution)/shard_map/ppermute | solution.py:1046
  75.2 2.7 arrange.3.refs_8_.refs_1_
  78.9 9.6 %ff_forward.2 = (f32[512,768]{1,0:T(8,128)}, f32[512,1536]{1,0:T(8,128)}, bf16[512,768]{1,0:T(8,128)(2,1)}) custom-call(s32[7]{0:T(128)} %stack.149.at_ref.refs_0_, f32[512,768]{1,0:T(8,128)} %arrange.2.refs_1_.refs_5_.refs_4_, bf16[512,768]{1,0:T(8,128)(2,1)} %get-tuple-element.126.refs_2_, bf16[512,768]{1,0:T(8,128)(2,1)} %copy-done.22, ...), custom_call_target="tpu_custom_call" | custom-call | flops 10000000000 | bytes 10000 | tf_op jit(solution)/shard_map/ff_forward/pallas_call | solution.py:885
  88.5 2.7 collective-permute-start.4
  91.2 16.3 %collective-permute-done.4.refs_3_ = bf16[512,768]{1,0:T(8,128)(2,1)S(1)} collective-permute-done((bf16[512,768]{1,0:T(8,128)(2,1)}, bf16[512,768]{1,0:T(8,128)(2,1)S(1)}, u32[]{:S(2)}, u32[]{:S(2)}) %collective-permute-start.4) | collective-permute-done | bytes 786464 | tf_op jit(solution)/shard_map/ppermute | solution.py:1046
  108.3 12.2 %mixer_forward.3 = (f32[512,768]{1,0:T(8,128)}, f32[512,1152]{1,0:T(8,128)}, f32[4,256,384]{2,1,0:T(8,128)}, f32[512,384]{1,0:T(8,128)}, bf16[512,768]{1,0:T(8,128)(2,1)}) custom-call(s32[7]{0:T(128)} %stack.149.at_ref.refs_0_, f32[512,768]{1,0:T(8,128)} %get-tuple-element.127.refs_1_.refs_6_.refs_4_, bf16[512,768]{1,0:T(8,128)(2,1)} %get-tuple-element.128.refs_2_, ...), custom_call_target="tpu_custom_call" | custom-call | flops 11000000512 | bytes 10000 | tf_op jit(solution)/shard_map/mixer_forward/pallas_call | solution.py:854
  120.6 2.3 collective-permute-start.5
  122.9 15.7 %collective-permute-done.5.refs_3_ = bf16[512,768]{1,0:T(8,128)(2,1)S(1)} collective-permute-done((bf16[512,768]{1,0:T(8,128)(2,1)}, bf16[512,768]{1,0:T(8,128)(2,1)S(1)}, u32[]{:S(2)}, u32[]{:S(2)}) %collective-permute-start.5) | collective-permute-done | bytes 786464 | tf_op jit(solution)/shard_map/ppermute | solution.py:1046
  139.5 9.6 %ff_forward.3 = (f32[512,768]{1,0:T(8,128)}, f32[512,1536]{1,0:T(8,128)}, bf16[512,768]{1,0:T(8,128)(2,1)}) custom-call(s32[7]{0:T(128)} %stack.149.at_ref.refs_0_, f32[512,768]{1,0:T(8,128)} %get-tuple-element.129.refs_1_.refs_5_.refs_4_, bf16[512,768]{1,0:T(8,128)(2,1)} %get-tuple-element.130.refs_2_, bf16[512,768]{1,0:T(8,128)(2,1)} %copy-done.24, ...), custom_call_target="tpu_custom_call" | custom-call | flops 10000000000 | bytes 10000 | tf_op jit(solution)/shard_map/ff_forward/pallas_call | solution.py:885
  149.1 11.0 %ff_backward.2 = (bf16[512,1536]{1,0:T(8,128)(2,1)}, bf16[512,1536]{1,0:T(8,128)(2,1)}, bf16[512,768]{1,0:T(8,128)(2,1)}, bf16[512,768]{1,0:T(8,128)(2,1)}, f32[...) custom-call(s32[7]{0:T(128)} %stack.149.at_ref.refs_0_, f32[512,768]{1,0:T(8,128)} %arrange.3.refs_8_.refs_1_, ...), custom_call_target="tpu_custom_call" | custom-call | flops 10000000000 | bytes 10000 | tf_op jit(solution)/shard_map/ff_backward/pallas_call | solution.py:913
  160.1 2.5 collective-permute-start.6
  162.6 7.4 %ff_weights.2 = (bf16[4,4,96,768]{3,2,1,0:T(8,128)(2,1)}, bf16[4,4,96,768]{3,2,1,0:T(8,128)(2,1)}) custom-call(s32[7]{0:T(128)} %stack.149.at_ref.refs_0_, bf16[512,1536]{1,0:T(8,128)(2,1)} %get-tuple-element.138.e_ref, bf16[512,768]{1,0:T(8,128)(2,1)} %get-tuple-element.139.dm_ref, bf16[512,768]{1,0:T(8,128)(2,1)} %get-tuple-element.140.b_ref, ...), custom_call_target="tpu_custom_call" | custom-call | flops 7000000000 | bytes 10000 | tf_op jit(solution)/shard_map/ff_weights/pallas_call | solution.py:927
  170.1 7.6 %collective-permute-done.6.refs_1_.refs_3_ = bf16[512,768]{1,0:T(8,128)(2,1)S(1)} collective-permute-done((bf16[512,768]{1,0:T(8,128)(2,1)}, bf16[512,768]{1,0:T(8,128)(2,1)S(1)}, u32[]{:S(2)}, u32[]{:S(2)}) %collective-permute-start.6) | collective-permute-done | bytes 786464 | tf_op jit(solution)/shard_map/ppermute | solution.py:1046
  178.5 2.1 copy_after.3.own_ref.refs_22_
  182.3 16.2 %mixer_backward.2 = (f32[512,768]{1,0:T(8,128)}, f32[2,768]{1,0:T(2,128)}, f32[1,768]{1,0:T(1,128)}, f32[1,1152]{1,0:T(1,128)}, f32[3,1152]{1,0:T(4,128)}, /*ind...) custom-call(s32[7]{0:T(128)} %stack.149.at_ref.refs_0_, ...), custom_call_target="tpu_custom_call" | custom-call | flops 15000000512 | bytes 10000 | tf_op jit(solution)/shard_map/mixer_backward/pallas_call | solution.py:946
  199.9 5.2 %collective-permute-start.10 = (bf16[4,4,96,768]{3,2,1,0:T(8,128)(2,1)S(1)}, bf16[4,4,96,768]{3,2,1,0:T(8,128)(2,1)S(1)}, u32[]{:S(2)}, u32[]{:S(2)}) collective-permute-start(bf16[4,4,96,768]{3,2,1,0:T(8,128)(2,1)S(1)} %copy-done.16), channel_id=1, source_target_pairs={{0,2},{2,0},{1,3},{3,1},{4,6},{6,4},{5,7},{7,5},{8,10},{10,8},{9,1... | collective-permute-start | bytes 7077896 | tf_op jit(solution)/shard_map/ppermute | solution.py:1046
  205.1 5.5 %mixer_weights.2 = (bf16[4,4,96,384]{3,2,1,0:T(8,128)(2,1)}, bf16[4,4,96,384]{3,2,1,0:T(8,128)(2,1)}) custom-call(s32[7]{0:T(128)} %stack.149.at_ref.refs_0_, bf16[512,768]{1,0:T(8,128)(2,1)} %get-tuple-element.147.refs_0_, bf16[512,1152]{1,0:T(8,128)(2,1)} %get-tuple-element.148.refs_1_, bf16[512,384]{1,0:T(8,128)(2,1)} %get-tuple-element.149.refs_2_, ...), custom_call_target="tpu_custom_call" | custom-call | flops 5000000000 | bytes 10000 | tf_op jit(solution)/shard_map/mixer_weights/pallas_call | solution.py:964
  211.6 3.3 finish_result.1.refs_15_
  215.8 13.4 %ff_backward.3 = (f32[512,768]{1,0:T(8,128)}, f32[2,768]{1,0:T(2,128)}, bf16[512,1536]{1,0:T(8,128)(2,1)}, bf16[512,1536]{1,0:T(8,128)(2,1)}, bf16[512,768]{1,0:...) custom-call(s32[7]{0:T(128)} %stack.149.at_ref.refs_0_, ...), custom_call_target="tpu_custom_call" | custom-call | flops 10000000000 | bytes 10000 | tf_op jit(solution)/shard_map/ff_backward/pallas_call | solution.py:913
  229.2 2.1 collective-permute-start.9
  231.3 7.3 %ff_weights.3 = (bf16[4,4,96,768]{3,2,1,0:T(8,128)(2,1)}, bf16[4,4,96,768]{3,2,1,0:T(8,128)(2,1)}) custom-call(s32[7]{0:T(128)} %stack.149.at_ref.refs_0_, bf16[512,1536]{1,0:T(8,128)(2,1)} %get-tuple-element.162.e_ref, bf16[512,768]{1,0:T(8,128)(2,1)} %get-tuple-element.163.dm_ref, bf16[512,768]{1,0:T(8,128)(2,1)} %get-tuple-element.164.b_ref, ...), custom_call_target="tpu_custom_call" | custom-call | flops 7000000000 | bytes 10000 | tf_op jit(solution)/shard_map/ff_weights/pallas_call | solution.py:927
  241.1 5.3 %add_parts.12 = (bf16[4,96,1152]{2,1,0:T(8,128)(2,1)}, bf16[4,96,1152]{2,1,0:T(8,128)(2,1)}, bf16[4,96,1152]{2,1,0:T(8,128)(2,1)}, bf16[4,96,1152]{2,1,0:T(8,128)(2,1)}) custom-call(bf16[4,4,96,768]{3,2,1,0:T(8,128)(2,1)} %get-tuple-element.142.refs_20_.refs_11_.refs_0_, bf16[4,4,96,768]{3,2,1,0:T(8,128)(2,1)} %copy-done.3, ...), custom_call_target="tpu_custom_call" | custom-call | flops 1000000000 | bytes 10000 | tf_op jit(solution)/shard_map/add_parts/pallas_call | solution.py:977
  247.7 2.6 collective-permute-start.14
  252.3 18.6 %mixer_backward.3 = (f32[512,768]{1,0:T(8,128)}, f32[2,768]{1,0:T(2,128)}, f32[1,768]{1,0:T(1,128)}, f32[1,1152]{1,0:T(1,128)}, f32[3,1152]{1,0:T(4,128)}, /*ind...) custom-call(s32[7]{0:T(128)} %stack.149.at_ref.refs_0_, ...), custom_call_target="tpu_custom_call" | custom-call | flops 15000000512 | bytes 10000 | tf_op jit(solution)/shard_map/mixer_backward/pallas_call | solution.py:946
  272.3 3.1 add_parts.13
  276.6 2.5 collective-permute-start.33
  281.6 3.3 collective-permute-done.33.refs_2_
  285.7 2.1 add_parts.19.refs_0_
  288.5 4.3 collective-permute-done.35.refs_1_
  295.3 8.6 %collective-permute-start.16 = (bf16[4,4,96,768]{3,2,1,0:T(8,128)(2,1)}, bf16[4,4,96,768]{3,2,1,0:T(8,128)(2,1)S(1)}, u32[]{:S(2)}, u32[]{:S(2)}) collective-permute-start(bf16[4,4,96,768]{3,2,1,0:T(8,128)(2,1)} %get-tuple-element.167.refs_25_), channel_id=1, source_target_pairs={{0,2},{2,0},{1,3},{3,1},{4,6},{6,4},{5,7},{7,5},{8,10},{10,8},{9,1... | collective-permute-start | bytes 7077896 | tf_op jit(solution)/shard_map/ppermute | solution.py:1046
  303.9 7.1 %filter_backward.1 = (f32[2,64,384]{2,1,0:T(8,128)}, f32[64,384]{1,0:T(8,128)}) custom-call(s32[7]{0:T(128)} %stack.149.at_ref.refs_0_, f32[512,128]{1,0:T(8,128)} %constant.31.clone.feats_ref, f32[512,128]{1,0:T(8,128)} %constant.32.clone.times_ref, f32[2,128,128]{2,1,0:T(8,128)} %get-tuple-element.178.inner_ref, ...), custom_call_target="tpu_custom_call" | custom-call | flops 8000000000 | bytes 10000 | tf_op jit(solution)/shard_map/filter_backward/pallas_call | solution.py:799
  311.6 2.0 pack_small.1.refs_0_
  313.6 5.9 %mixer_weights.3 = (bf16[4,4,112,384]{3,2,1,0:T(8,128)(2,1)}, bf16[4,4,112,384]{3,2,1,0:T(8,128)(2,1)}) custom-call(s32[7]{0:T(128)} %stack.149.at_ref.refs_0_, f32[256,384]{1,0:T(8,128)} %pack_small.1.refs_0_, bf16[512,768]{1,0:T(8,128)(2,1)} %get-tuple-element.204.refs_1_, bf16[512,1152]{1,0:T(8,128)(2,1)} %get-tuple-element.205.refs_2_, ...), custom_call_target="tpu_custom_call" | custom-call | flops 5000000000 | bytes 10000 | tf_op jit(solution)/shard_map/mixer_weights/pallas_call | solution.py:964
  319.4 31.5 %all-gather.3.cloned.1.call-done = bf16[1536,1152]{1,0:T(8,128)(2,1)} async-done(((bf16[96,1152]{1,0:T(8,128)(2,1)}), bf16[1536,1152]{1,0:T(8,128)(2,1)}) %all-gather.3.cloned.1.call-update) | async-done | bytes 3538960 | tf_op jit(solution)/shard_map/all_gather | solution.py:1076
  352.0 2.9 add_parts.15
  355.4 2.4 collective-permute-start.19
  360.4 3.9 add_parts.14
  368.1 2.1 add_parts.16
  370.7 11.8 %collective-permute-done.21.refs_1_ = bf16[112,384]{1,0:T(8,128)(2,1)S(1)} collective-permute-done((bf16[112,384]{1,0:T(8,128)(2,1)}, bf16[112,384]{1,0:T(8,128)(2,1)S(1)}, u32[]{:S(2)}, u32[]{:S(2)}) %collective-permute-start.21) | collective-permute-done | bytes 86048 | tf_op jit(solution)/shard_map/ppermute | solution.py:1055
  382.5 5.3 %collective-permute-done.22.refs_2_ = bf16[112,384]{1,0:T(8,128)(2,1)S(1)} collective-permute-done((bf16[112,384]{1,0:T(8,128)(2,1)}, bf16[112,384]{1,0:T(8,128)(2,1)S(1)}, u32[]{:S(2)}, u32[]{:S(2)}) %collective-permute-start.22) | collective-permute-done | bytes 86048 | tf_op jit(solution)/shard_map/ppermute | solution.py:1055
  387.8 3.8 collective-permute-done.23.refs_3_
  396.6 2.5 add_parts.21
  399.2 2.1 collective-permute-start.42
  401.9 2.7 collective-permute-start.12
  406.8 2.1 collective-permute-start.26
  416.3 6.7 %collective-permute-done.44.refs_1_ = bf16[96,768]{1,0:T(8,128)(2,1)S(1)} collective-permute-done((bf16[96,768]{1,0:T(8,128)(2,1)}, bf16[96,768]{1,0:T(8,128)(2,1)S(1)}, u32[]{:S(2)}, u32[]{:S(2)}) %collective-permute-start.44) | collective-permute-done | bytes 147488 | tf_op jit(solution)/shard_map/ppermute | solution.py:1046
  423.0 2.2 collective-permute-start.30
  426.9 3.9 collective-permute-start.46
  431.8 2.0 collective-permute-done.47
  433.8 3.1 collective-permute-start.31
  437.0 2.7 collective-permute-start.49
  439.8 2.6 collective-permute-start.50
  442.4 4.4 finish_grad.1
  448.8 6.3 %collective-permute-done.48 = bf16[4,96,768]{2,1,0:T(8,128)(2,1)S(1)} collective-permute-done((bf16[4,96,768]{2,1,0:T(8,128)(2,1)S(1)}, bf16[4,96,768]{2,1,0:T(8,128)(2,1)S(1)}, u32[]{:S(2)}, u32[]{:S(2)}) %collective-permute-start.48) | collective-permute-done | bytes 589856 | tf_op jit(solution)/shard_map/ppermute | solution.py:1055
  455.4 12.9 %collective-permute-start.51 = (bf16[4,4,96,768]{3,2,1,0:T(8,128)(2,1)S(1)}, bf16[4,4,96,768]{3,2,1,0:T(8,128)(2,1)}, u32[]{:S(2)}, u32[]{:S(2)}) collective-permute-start(bf16[4,4,96,768]{3,2,1,0:T(8,128)(2,1)S(1)} %pad_maximum_fusion.refs_1_), channel_id=1, source_target_pairs={{0,2},{2,0},{1,3},{3,1},{4,6},{6,4},{5,7},{7,5},{8,10},{10,8},{9,1... | collective-permute-start | bytes 7077896 | tf_op jit(solution)/shard_map/ppermute | solution.py:1046
  468.3 7.6 %place_mixer.2 = (f32[2,3,768,384]{3,2,1,0:T(8,128)}, f32[2,384,768]{2,1,0:T(8,128)}) custom-call(s32[7]{0:T(128)} %stack.149.at_ref.refs_0_, bf16[1,4,4,96,1152]{4,3,2,1,0:T(8,128)(2,1)} %bitcast.94, bf16[1,4,4,96,1152]{4,3,2,1,0:T(8,128)(2,1)} %collective-permute-done.36.refs_2_), custom_call_target="tpu_custom_call" | custom-call | flops 6000000000 | bytes 10000 | tf_op jit(solution)/shard_map/place_mixer/pallas_call | solution.py:1006
  475.8 6.5 %place_mixer.3 = (f32[2,3,768,384]{3,2,1,0:T(8,128)}, f32[2,384,768]{2,1,0:T(8,128)}, f32[256,384]{1,0:T(8,128)}) custom-call(s32[7]{0:T(128)} %stack.149.at_ref.refs_0_, bf16[4,4,112,384]{3,2,1,0:T(8,128)(2,1)} %copy-done.4, bf16[4,4,112,384]{3,2,1,0:T(8,128)(2,1)} %collective-permute-done.31.refs_2_, ...), custom_call_target="tpu_custom_call", output_to_operand_aliasing={{0}: (3, {}), {1}: (4, {})} | custom-call | flops 6000000000 | bytes 10000 | tf_op jit(solution)/shard_map/place_mixer/pallas_call | solution.py:1006
  484.4 7.2 %place_ff.2 = (f32[2,768,1536]{2,1,0:T(8,128)}, f32[2,1536,768]{2,1,0:T(8,128)}) custom-call(s32[7]{0:T(128)} %stack.149.at_ref.refs_0_, bf16[1,4,4,96,1152]{4,3,2,1,0:T(8,128)(2,1)} %bitcast.95, bf16[1,4,4,96,1152]{4,3,2,1,0:T(8,128)(2,1)} %collective-permute-done.36.refs_2_), custom_call_target="tpu_custom_call" | custom-call | flops 6000000000 | bytes 10000 | tf_op jit(solution)/shard_map/place_ff/pallas_call | solution.py:1006
  491.6 6.5 %place_ff.3 = (f32[2,768,1536]{2,1,0:T(8,128)}, f32[2,1536,768]{2,1,0:T(8,128)}) custom-call(s32[7]{0:T(128)} %stack.149.at_ref.refs_0_, bf16[4,4,96,768]{3,2,1,0:T(8,128)(2,1)} %copy-done, bf16[4,4,96,768]{3,2,1,0:T(8,128)(2,1)} %collective-permute-done.51.refs_2_, ...), custom_call_target="tpu_custom_call", output_to_operand_aliasing={{0}: (3, {}), {1}: (4, {})} | custom-call | flops 6000000000 | bytes 10000 | tf_op jit(solution)/shard_map/place_ff/pallas_call | solution.py:1006
  (227 shorter events, 76.7 us)
Async XLA Ops:
  7.2 343.7 %all-gather.3.cloned.1.call-start = ((), (), s32[]{:S(2)}) async-start(), calls=%async_computation | async-start | bytes 3760128 | tf_op jit(solution)/shard_map/all_gather | solution.py:1076
  9.5 20.3 %collective-permute-start.1 = (f32[2,8,384]{2,1,0:T(8,128)S(1)}, f32[2,8,384]{2,1,0:T(8,128)S(1)}, u32[]{:S(2)}, u32[]{:S(2)}) collective-permute-start(f32[2,8,384]{2,1,0:T(8,128)S(1)} %stack.152), channel_id=1, source_target_pairs={{0,1},{1,0},{2,3},{3,2},{4,5},{5,4},{6,7},{7,6},{8,9},{9,8},{10,11... | collective-permute-start | bytes 73736 | tf_op jit(solution)/shard_map/ppermute | solution.py:1046
  14.0 16.4 %collective-permute-start = (bf16[512,384]{1,0:T(8,128)(2,1)}, bf16[512,384]{1,0:T(8,128)(2,1)S(1)}, u32[]{:S(2)}, u32[]{:S(2)}) collective-permute-start(bf16[512,384]{1,0:T(8,128)(2,1)} %own_ref.2), channel_id=1, source_target_pairs={{0,1},{1,0},{2,3},{3,2},{4,5},{5,4},{6,7},{7,6},{8,9},{9,8},{10,11... | collective-permute-start | bytes 1179656 | tf_op jit(solution)/shard_map/ppermute | solution.py:1046
  18.0 9.3 %copy-start.15 = (f32[2,384]{1,0:T(2,128)S(1)}, f32[2,384]{1,0:T(2,128)}, u32[]{:S(2)}) copy-start(f32[2,384]{1,0:T(2,128)} %param.38) | copy-start | bytes 9220
  18.0 9.9 %copy-start.13 = (f32[2,3,384]{2,0,1:T(2,128)S(1)}, f32[2,3,384]{2,0,1:T(2,128)}, u32[]{:S(2)}) copy-start(f32[2,3,384]{2,0,1:T(2,128)} %param.33) | copy-start | bytes 27652
  18.0 10.5 %copy-start.14 = (f32[2,3,384]{2,0,1:T(2,128)S(1)}, f32[2,3,384]{2,0,1:T(2,128)}, u32[]{:S(2)}) copy-start(f32[2,3,384]{2,0,1:T(2,128)} %param.31) | copy-start | bytes 27652
  18.0 11.1 %copy-start.11 = (f32[2,3,3,384]{3,0,2,1:T(2,128)S(1)}, f32[2,3,3,384]{3,0,2,1:T(2,128)}, u32[]{:S(2)}) copy-start(f32[2,3,3,384]{3,0,2,1:T(2,128)} %param.32) | copy-start | bytes 82948
  35.4 13.8 %copy-start.29 = (bf16[512,384]{1,0:T(8,128)(2,1)S(1)}, bf16[512,384]{1,0:T(8,128)(2,1)}, u32[]{:S(2)}) copy-start(bf16[512,384]{1,0:T(8,128)(2,1)} %copy_after.2.refs_14_) | copy-start | bytes 1179652
  35.4 13.9 %copy-start.12 = (f32[2,1536]{1,0:T(2,128)S(1)}, f32[2,1536]{1,0:T(2,128)}, u32[]{:S(2)}) copy-start(f32[2,1536]{1,0:T(2,128)} %param.42) | copy-start | bytes 36868
  46.3 31.7 %collective-permute-start.2 = (bf16[512,768]{1,0:T(8,128)(2,1)}, bf16[512,768]{1,0:T(8,128)(2,1)S(1)}, u32[]{:S(2)}, u32[]{:S(2)}) collective-permute-start(bf16[512,768]{1,0:T(8,128)(2,1)} %get-tuple-element.126.refs_2_), channel_id=1, source_target_pairs={{0,1},{1,0},{2,3},{3,2},{4,5},{5,4},{6,7},{7,6},{8,9},{9,8},{10,11... | collective-permute-start | bytes 2359304 | tf_op jit(solution)/shard_map/ppermute | solution.py:1046
  49.2 25.3 %collective-permute-start.3 = (bf16[512,384]{1,0:T(8,128)(2,1)S(1)}, bf16[512,384]{1,0:T(8,128)(2,1)S(1)}, u32[]{:S(2)}, u32[]{:S(2)}) collective-permute-start(bf16[512,384]{1,0:T(8,128)(2,1)S(1)} %copy-done.29), channel_id=1, source_target_pairs={{0,1},{1,0},{2,3},{3,2},{4,5},{5,4},{6,7},{7,6},{8,9},{9,8},{10,11... | collective-permute-start | bytes 1179656 | tf_op jit(solution)/shard_map/ppermute | solution.py:1046
  88.5 19.0 %collective-permute-start.4 = (bf16[512,768]{1,0:T(8,128)(2,1)}, bf16[512,768]{1,0:T(8,128)(2,1)S(1)}, u32[]{:S(2)}, u32[]{:S(2)}) collective-permute-start(bf16[512,768]{1,0:T(8,128)(2,1)} %get-tuple-element.128.refs_2_), channel_id=1, source_target_pairs={{0,1},{1,0},{2,3},{3,2},{4,5},{5,4},{6,7},{7,6},{8,9},{9,8},{10,11... | collective-permute-start | bytes 2359304 | tf_op jit(solution)/shard_map/ppermute | solution.py:1046
  120.6 18.0 %collective-permute-start.5 = (bf16[512,768]{1,0:T(8,128)(2,1)}, bf16[512,768]{1,0:T(8,128)(2,1)S(1)}, u32[]{:S(2)}, u32[]{:S(2)}) collective-permute-start(bf16[512,768]{1,0:T(8,128)(2,1)} %get-tuple-element.130.refs_2_), channel_id=1, source_target_pairs={{0,1},{1,0},{2,3},{3,2},{4,5},{5,4},{6,7},{7,6},{8,9},{9,8},{10,11... | collective-permute-start | bytes 2359304 | tf_op jit(solution)/shard_map/ppermute | solution.py:1046
  160.1 17.5 %collective-permute-start.6 = (bf16[512,768]{1,0:T(8,128)(2,1)}, bf16[512,768]{1,0:T(8,128)(2,1)S(1)}, u32[]{:S(2)}, u32[]{:S(2)}) collective-permute-start(bf16[512,768]{1,0:T(8,128)(2,1)} %get-tuple-element.134.refs_2_), channel_id=1, source_target_pairs={{0,1},{1,0},{2,3},{3,2},{4,5},{5,4},{6,7},{7,6},{8,9},{9,8},{10,11... | collective-permute-start | bytes 2359304 | tf_op jit(solution)/shard_map/ppermute | solution.py:1046
  180.6 30.0 %collective-permute-start.7 = (bf16[512,768]{1,0:T(8,128)(2,1)}, bf16[512,768]{1,0:T(8,128)(2,1)S(1)}, u32[]{:S(2)}, u32[]{:S(2)}) collective-permute-start(bf16[512,768]{1,0:T(8,128)(2,1)} %copy_after.3.own_ref.refs_22_), channel_id=1, source_target_pairs={{0,1},{1,0},{2,3},{3,2},{4,5},{5,4},{6,7},{7,6},{8,9},{9,8},{10,11... | collective-permute-start | bytes 2359304 | tf_op jit(solution)/shard_map/ppermute | solution.py:1046
  182.3 17.5 %copy-start.16 = (bf16[4,4,96,768]{3,2,1,0:T(8,128)(2,1)S(1)}, bf16[4,4,96,768]{3,2,1,0:T(8,128)(2,1)}, u32[]{:S(2)}) copy-start(bf16[4,4,96,768]{3,2,1,0:T(8,128)(2,1)} %get-tuple-element.143.refs_21_.refs_12_) | copy-start | bytes 7077892
  198.5 16.3 %collective-permute-start.8 = (bf16[512,768]{1,0:T(8,128)(2,1)}, bf16[512,768]{1,0:T(8,128)(2,1)S(1)}, u32[]{:S(2)}, u32[]{:S(2)}) collective-permute-start(bf16[512,768]{1,0:T(8,128)(2,1)} %get-tuple-element.145.refs_2_), channel_id=1, source_target_pairs={{0,1},{1,0},{2,3},{3,2},{4,5},{5,4},{6,7},{7,6},{8,9},{9,8},{10,11... | collective-permute-start | bytes 2359304 | tf_op jit(solution)/shard_map/ppermute | solution.py:1046
  199.9 38.8 %collective-permute-start.10 = (bf16[4,4,96,768]{3,2,1,0:T(8,128)(2,1)S(1)}, bf16[4,4,96,768]{3,2,1,0:T(8,128)(2,1)S(1)}, u32[]{:S(2)}, u32[]{:S(2)}) collective-permute-start(bf16[4,4,96,768]{3,2,1,0:T(8,128)(2,1)S(1)} %copy-done.16), channel_id=1, source_target_pairs={{0,2},{2,0},{1,3},{3,1},{4,6},{6,4},{5,7},{7,5},{8,10},{10,8},{9,1... | collective-permute-start | bytes 7077896 | tf_op jit(solution)/shard_map/ppermute | solution.py:1046
  210.6 28.0 %collective-permute-start.11 = (bf16[4,4,96,384]{3,2,1,0:T(8,128)(2,1)}, bf16[4,4,96,384]{3,2,1,0:T(8,128)(2,1)S(1)}, u32[]{:S(2)}, u32[]{:S(2)}) collective-permute-start(bf16[4,4,96,384]{3,2,1,0:T(8,128)(2,1)} %get-tuple-element.152.refs_14_), channel_id=1, source_target_pairs={{0,2},{2,0},{1,3},{3,1},{4,6},{6,4},{5,7},{7,5},{8,10},{10,8},{9,1... | collective-permute-start | bytes 3538952 | tf_op jit(solution)/shard_map/ppermute | solution.py:1046
  229.2 22.2 %collective-permute-start.9 = (bf16[512,768]{1,0:T(8,128)(2,1)}, bf16[512,768]{1,0:T(8,128)(2,1)S(1)}, u32[]{:S(2)}, u32[]{:S(2)}) collective-permute-start(bf16[512,768]{1,0:T(8,128)(2,1)} %get-tuple-element.154.refs_4_.refs_2_), channel_id=1, source_target_pairs={{0,1},{1,0},{2,3},{3,2},{4,5},{5,4},{6,7},{7,6},{8,9},{9,8},{10,11... | collective-permute-start | bytes 2359304 | tf_op jit(solution)/shard_map/ppermute | solution.py:1046
  246.4 24.5 %collective-permute-start.13 = (bf16[4,96,1152]{2,1,0:T(8,128)(2,1)}, bf16[4,96,1152]{2,1,0:T(8,128)(2,1)S(1)}, u32[]{:S(2)}, u32[]{:S(2)}) collective-permute-start(bf16[4,96,1152]{2,1,0:T(8,128)(2,1)} %get-tuple-element.159.refs_21_), channel_id=1, source_target_pairs={{0,4},{2,18},{4,8},{6,22},{8,12},{10,26},{12,0},{14,30},{16,20},{1... | collective-permute-start | bytes 2654216 | tf_op jit(solution)/shard_map/ppermute | solution.py:1055
  247.7 23.2 %collective-permute-start.14 = (bf16[4,96,1152]{2,1,0:T(8,128)(2,1)}, bf16[4,96,1152]{2,1,0:T(8,128)(2,1)S(1)}, u32[]{:S(2)}, u32[]{:S(2)}) collective-permute-start(bf16[4,96,1152]{2,1,0:T(8,128)(2,1)} %get-tuple-element.160.refs_22_), channel_id=1, source_target_pairs={{0,8},{2,34},{4,12},{6,38},{8,0},{10,42},{12,4},{14,46},{16,24},{1... | collective-permute-start | bytes 2654216 | tf_op jit(solution)/shard_map/ppermute | solution.py:1055
  250.3 20.6 %collective-permute-start.15 = (bf16[4,96,1152]{2,1,0:T(8,128)(2,1)}, bf16[4,96,1152]{2,1,0:T(8,128)(2,1)S(1)}, u32[]{:S(2)}, u32[]{:S(2)}) collective-permute-start(bf16[4,96,1152]{2,1,0:T(8,128)(2,1)} %get-tuple-element.161.refs_23_), channel_id=1, source_target_pairs={{0,12},{2,50},{4,0},{6,54},{8,4},{10,58},{12,8},{14,62},{16,28},{1... | collective-permute-start | bytes 2654216 | tf_op jit(solution)/shard_map/ppermute | solution.py:1055
  275.4 6.2 %collective-permute-start.32 = (bf16[96,1152]{1,0:T(8,128)(2,1)}, bf16[96,1152]{1,0:T(8,128)(2,1)S(1)}, u32[]{:S(2)}, u32[]{:S(2)}) collective-permute-start(bf16[96,1152]{1,0:T(8,128)(2,1)} %get-tuple-element.171.refs_7_), channel_id=1, source_target_pairs={{0,16},{2,6},{4,20},{6,10},{8,24},{10,14},{12,28},{14,2},{16,32},{... | collective-permute-start | bytes 663560 | tf_op jit(solution)/shard_map/ppermute | solution.py:1055
  276.6 8.4 %collective-permute-start.33 = (bf16[96,1152]{1,0:T(8,128)(2,1)}, bf16[96,1152]{1,0:T(8,128)(2,1)S(1)}, u32[]{:S(2)}, u32[]{:S(2)}) collective-permute-start(bf16[96,1152]{1,0:T(8,128)(2,1)} %get-tuple-element.172.refs_8_), channel_id=1, source_target_pairs={{0,32},{2,10},{4,36},{6,14},{8,40},{10,2},{12,44},{14,6},{16,48},{... | collective-permute-start | bytes 663560 | tf_op jit(solution)/shard_map/ppermute | solution.py:1055
  279.1 5.9 %collective-permute-start.34 = (bf16[96,1152]{1,0:T(8,128)(2,1)}, bf16[96,1152]{1,0:T(8,128)(2,1)S(1)}, u32[]{:S(2)}, u32[]{:S(2)}) collective-permute-start(bf16[96,1152]{1,0:T(8,128)(2,1)} %get-tuple-element.173.refs_9_), channel_id=1, source_target_pairs={{0,48},{2,14},{4,52},{6,2},{8,56},{10,6},{12,60},{14,10},{16,0},{1... | collective-permute-start | bytes 663560 | tf_op jit(solution)/shard_map/ppermute | solution.py:1055
  287.8 5.0 collective-permute-start.35
  295.3 63.7 %collective-permute-start.16 = (bf16[4,4,96,768]{3,2,1,0:T(8,128)(2,1)}, bf16[4,4,96,768]{3,2,1,0:T(8,128)(2,1)S(1)}, u32[]{:S(2)}, u32[]{:S(2)}) collective-permute-start(bf16[4,4,96,768]{3,2,1,0:T(8,128)(2,1)} %get-tuple-element.167.refs_25_), channel_id=1, source_target_pairs={{0,2},{2,0},{1,3},{3,1},{4,6},{6,4},{5,7},{7,5},{8,10},{10,8},{9,1... | collective-permute-start | bytes 7077896 | tf_op jit(solution)/shard_map/ppermute | solution.py:1046
  319.4 32.5 %collective-permute-start.17 = (bf16[4,4,112,384]{3,2,1,0:T(8,128)(2,1)}, bf16[4,4,112,384]{3,2,1,0:T(8,128)(2,1)}, u32[]{:S(2)}, u32[]{:S(2)}) collective-permute-start(bf16[4,4,112,384]{3,2,1,0:T(8,128)(2,1)} %get-tuple-element.209.refs_15_), channel_id=1, source_target_pairs={{0,2},{2,0},{1,3},{3,1},{4,6},{6,4},{5,7},{7,5},{8,10},{10,8},{9,1... | collective-permute-start | bytes 4128776 | tf_op jit(solution)/shard_map/ppermute | solution.py:1046
  350.9 117.3 %collective-permute-start.36 = (bf16[1,4,4,96,1152]{4,3,2,1,0:T(8,128)(2,1)}, bf16[1,4,4,96,1152]{4,3,2,1,0:T(8,128)(2,1)}, u32[]{:S(2)}, u32[]{:S(2)}) collective-permute-start(bf16[1,4,4,96,1152]{4,3,2,1,0:T(8,128)(2,1)} %bitcast.93), channel_id=1, source_target_pairs={{0,2},{2,0},{1,3},{3,1},{4,6},{6,4},{5,7},{7,5},{8,10},{10,8},{9,1... | collective-permute-start | bytes 10616840 | tf_op jit(solution)/shard_map/ppermute | solution.py:1046
  354.9 9.7 %collective-permute-start.18 = (bf16[4,112,384]{2,1,0:T(8,128)(2,1)}, bf16[4,112,384]{2,1,0:T(8,128)(2,1)S(1)}, u32[]{:S(2)}, u32[]{:S(2)}) collective-permute-start(bf16[4,112,384]{2,1,0:T(8,128)(2,1)} %get-tuple-element.211), channel_id=1, source_target_pairs={{0,4},{2,18},{4,8},{6,22},{8,12},{10,26},{12,0},{14,30},{16,20},{1... | collective-permute-start | bytes 1032200 | tf_op jit(solution)/shard_map/ppermute | solution.py:1055
  355.4 11.3 %collective-permute-start.19 = (bf16[4,112,384]{2,1,0:T(8,128)(2,1)}, bf16[4,112,384]{2,1,0:T(8,128)(2,1)S(1)}, u32[]{:S(2)}, u32[]{:S(2)}) collective-permute-start(bf16[4,112,384]{2,1,0:T(8,128)(2,1)} %get-tuple-element.212), channel_id=1, source_target_pairs={{0,8},{2,34},{4,12},{6,38},{8,0},{10,42},{12,4},{14,46},{16,24},{1... | collective-permute-start | bytes 1032200 | tf_op jit(solution)/shard_map/ppermute | solution.py:1055
  357.8 9.5 %collective-permute-start.20 = (bf16[4,112,384]{2,1,0:T(8,128)(2,1)}, bf16[4,112,384]{2,1,0:T(8,128)(2,1)S(1)}, u32[]{:S(2)}, u32[]{:S(2)}) collective-permute-start(bf16[4,112,384]{2,1,0:T(8,128)(2,1)} %get-tuple-element.213), channel_id=1, source_target_pairs={{0,12},{2,50},{4,0},{6,54},{8,4},{10,58},{12,8},{14,62},{16,28},{1... | collective-permute-start | bytes 1032200 | tf_op jit(solution)/shard_map/ppermute | solution.py:1055
  364.3 31.1 %collective-permute-start.38 = (bf16[4,96,768]{2,1,0:T(8,128)(2,1)}, bf16[4,96,768]{2,1,0:T(8,128)(2,1)S(1)}, u32[]{:S(2)}, u32[]{:S(2)}) collective-permute-start(bf16[4,96,768]{2,1,0:T(8,128)(2,1)} %get-tuple-element.175.refs_11_), channel_id=1, source_target_pairs={{0,4},{2,18},{4,8},{6,22},{8,12},{10,26},{12,0},{14,30},{16,20},{1... | collective-permute-start | bytes 1769480 | tf_op jit(solution)/shard_map/ppermute | solution.py:1055
  364.6 30.8 %collective-permute-start.39 = (bf16[4,96,768]{2,1,0:T(8,128)(2,1)}, bf16[4,96,768]{2,1,0:T(8,128)(2,1)S(1)}, u32[]{:S(2)}, u32[]{:S(2)}) collective-permute-start(bf16[4,96,768]{2,1,0:T(8,128)(2,1)} %get-tuple-element.176.refs_12_), channel_id=1, source_target_pairs={{0,8},{2,34},{4,12},{6,38},{8,0},{10,42},{12,4},{14,46},{16,24},{1... | collective-permute-start | bytes 1769480 | tf_op jit(solution)/shard_map/ppermute | solution.py:1055
  366.7 28.8 %collective-permute-start.40 = (bf16[4,96,768]{2,1,0:T(8,128)(2,1)}, bf16[4,96,768]{2,1,0:T(8,128)(2,1)S(1)}, u32[]{:S(2)}, u32[]{:S(2)}) collective-permute-start(bf16[4,96,768]{2,1,0:T(8,128)(2,1)} %get-tuple-element.177.refs_13_), channel_id=1, source_target_pairs={{0,12},{2,50},{4,0},{6,54},{8,4},{10,58},{12,8},{14,62},{16,28},{1... | collective-permute-start | bytes 1769480 | tf_op jit(solution)/shard_map/ppermute | solution.py:1055
  370.2 12.3 %collective-permute-start.21 = (bf16[112,384]{1,0:T(8,128)(2,1)}, bf16[112,384]{1,0:T(8,128)(2,1)S(1)}, u32[]{:S(2)}, u32[]{:S(2)}) collective-permute-start(bf16[112,384]{1,0:T(8,128)(2,1)} %get-tuple-element.215), channel_id=1, source_target_pairs={{0,16},{2,6},{4,20},{6,10},{8,24},{10,14},{12,28},{14,2},{16,32},{... | collective-permute-start | bytes 258056 | tf_op jit(solution)/shard_map/ppermute | solution.py:1055
  382.5 9.1 %copy-start.43 = (bf16[112,384]{1,0:T(8,128)(2,1)}, bf16[112,384]{1,0:T(8,128)(2,1)S(1)}, u32[]{:S(2)}) copy-start(bf16[112,384]{1,0:T(8,128)(2,1)S(1)} %collective-permute-done.21.refs_1_) | copy-start | bytes 258052
  382.5 5.3 %collective-permute-start.22 = (bf16[112,384]{1,0:T(8,128)(2,1)}, bf16[112,384]{1,0:T(8,128)(2,1)S(1)}, u32[]{:S(2)}, u32[]{:S(2)}) collective-permute-start(bf16[112,384]{1,0:T(8,128)(2,1)} %get-tuple-element.216), channel_id=1, source_target_pairs={{0,32},{2,10},{4,36},{6,14},{8,40},{10,2},{12,44},{14,6},{16,48},{... | collective-permute-start | bytes 258056 | tf_op jit(solution)/shard_map/ppermute | solution.py:1055
  387.8 3.8 collective-permute-start.23
  394.0 7.9 %collective-permute-start.24 = (bf16[112,384]{1,0:T(8,128)(2,1)}, bf16[112,384]{1,0:T(8,128)(2,1)S(1)}, u32[]{:S(2)}, u32[]{:S(2)}) collective-permute-start(bf16[112,384]{1,0:T(8,128)(2,1)} %add_parts.17.refs_0_), channel_id=1, source_target_pairs={{0,64},{64,0},{1,65},{65,1},{2,66},{66,2},{3,67},{67,3},{4,68},{68... | collective-permute-start | bytes 258056 | tf_op jit(solution)/shard_map/ppermute | solution.py:1046
  399.2 7.3 %collective-permute-start.41 = (bf16[96,768]{1,0:T(8,128)(2,1)}, bf16[96,768]{1,0:T(8,128)(2,1)S(1)}, u32[]{:S(2)}, u32[]{:S(2)}) collective-permute-start(bf16[96,768]{1,0:T(8,128)(2,1)} %get-tuple-element.224), channel_id=1, source_target_pairs={{0,16},{2,6},{4,20},{6,10},{8,24},{10,14},{12,28},{14,2},{16,32},{... | collective-permute-start | bytes 442376 | tf_op jit(solution)/shard_map/ppermute | solution.py:1055
  399.2 7.6 %collective-permute-start.42 = (bf16[96,768]{1,0:T(8,128)(2,1)}, bf16[96,768]{1,0:T(8,128)(2,1)S(1)}, u32[]{:S(2)}, u32[]{:S(2)}) collective-permute-start(bf16[96,768]{1,0:T(8,128)(2,1)} %get-tuple-element.225), channel_id=1, source_target_pairs={{0,32},{2,10},{4,36},{6,14},{8,40},{10,2},{12,44},{14,6},{16,48},{... | collective-permute-start | bytes 442376 | tf_op jit(solution)/shard_map/ppermute | solution.py:1055
  401.3 7.6 %collective-permute-start.43 = (bf16[96,768]{1,0:T(8,128)(2,1)}, bf16[96,768]{1,0:T(8,128)(2,1)S(1)}, u32[]{:S(2)}, u32[]{:S(2)}) collective-permute-start(bf16[96,768]{1,0:T(8,128)(2,1)} %get-tuple-element.226), channel_id=1, source_target_pairs={{0,48},{2,14},{4,52},{6,2},{8,56},{10,6},{12,60},{14,10},{16,0},{1... | collective-permute-start | bytes 442376 | tf_op jit(solution)/shard_map/ppermute | solution.py:1055
  401.9 38.0 %collective-permute-start.12 = (bf16[512,768]{1,0:T(8,128)(2,1)S(1)}, bf16[512,768]{1,0:T(8,128)(2,1)S(1)}, u32[]{:S(2)}, u32[]{:S(2)}) collective-permute-start(bf16[512,768]{1,0:T(8,128)(2,1)S(1)} %copy-done.1), channel_id=1, source_target_pairs={{0,1},{1,0},{2,3},{3,2},{4,5},{5,4},{6,7},{7,6},{8,9},{9,8},{10,11... | collective-permute-start | bytes 2359304 | tf_op jit(solution)/shard_map/ppermute | solution.py:1046
  406.5 4.9 collective-permute-start.27
  406.8 5.3 %collective-permute-start.26 = (bf16[112,384]{1,0:T(8,128)(2,1)}, bf16[112,384]{1,0:T(8,128)(2,1)S(1)}, u32[]{:S(2)}, u32[]{:S(2)}) collective-permute-start(bf16[112,384]{1,0:T(8,128)(2,1)} %add_parts.18), channel_id=1, source_target_pairs={{0,32},{2,10},{4,36},{6,14},{8,40},{10,2},{12,44},{14,6},{16,48},{... | collective-permute-start | bytes 258056 | tf_op jit(solution)/shard_map/ppermute | solution.py:1055
  408.9 5.1 collective-permute-start.25
  411.4 11.6 %collective-permute-start.44 = (bf16[96,768]{1,0:T(8,128)(2,1)}, bf16[96,768]{1,0:T(8,128)(2,1)S(1)}, u32[]{:S(2)}, u32[]{:S(2)}) collective-permute-start(bf16[96,768]{1,0:T(8,128)(2,1)} %add_parts.22.refs_0_), channel_id=1, source_target_pairs={{0,64},{64,0},{1,65},{65,1},{2,66},{66,2},{3,67},{67,3},{4,68},{68... | collective-permute-start | bytes 442376 | tf_op jit(solution)/shard_map/ppermute | solution.py:1046
  414.0 12.9 %collective-permute-start.29 = (bf16[4,112,384]{2,1,0:T(8,128)(2,1)S(1)}, bf16[4,112,384]{2,1,0:T(8,128)(2,1)S(1)}, u32[]{:S(2)}, u32[]{:S(2)}) collective-permute-start(bf16[4,112,384]{2,1,0:T(8,128)(2,1)S(1)} %get-tuple-element.272), channel_id=1, source_target_pairs={{0,8},{2,34},{4,12},{6,38},{8,0},{10,42},{12,4},{14,46},{16,24},{1... | collective-permute-start | bytes 1032200 | tf_op jit(solution)/shard_map/ppermute | solution.py:1055
  415.7 11.2 %collective-permute-start.28 = (bf16[4,112,384]{2,1,0:T(8,128)(2,1)S(1)}, bf16[4,112,384]{2,1,0:T(8,128)(2,1)S(1)}, u32[]{:S(2)}, u32[]{:S(2)}) collective-permute-start(bf16[4,112,384]{2,1,0:T(8,128)(2,1)S(1)} %get-tuple-element.272), channel_id=1, source_target_pairs={{0,4},{2,18},{4,8},{6,22},{8,12},{10,26},{12,0},{14,30},{16,20},{1... | collective-permute-start | bytes 1032200 | tf_op jit(solution)/shard_map/ppermute | solution.py:1055
  423.0 7.8 %collective-permute-start.30 = (bf16[4,112,384]{2,1,0:T(8,128)(2,1)S(1)}, bf16[4,112,384]{2,1,0:T(8,128)(2,1)S(1)}, u32[]{:S(2)}, u32[]{:S(2)}) collective-permute-start(bf16[4,112,384]{2,1,0:T(8,128)(2,1)S(1)} %get-tuple-element.272), channel_id=1, source_target_pairs={{0,12},{2,50},{4,0},{6,54},{8,4},{10,58},{12,8},{14,62},{16,28},{1... | collective-permute-start | bytes 1032200 | tf_op jit(solution)/shard_map/ppermute | solution.py:1055
  426.9 10.0 %copy-start.9 = (bf16[96,768]{1,0:T(8,128)(2,1)S(1)}, bf16[96,768]{1,0:T(8,128)(2,1)}, u32[]{:S(2)}) copy-start(bf16[96,768]{1,0:T(8,128)(2,1)} %add_parts.23) | copy-start | bytes 442372
  426.9 6.9 %collective-permute-start.47 = (bf16[96,768]{1,0:T(8,128)(2,1)}, bf16[96,768]{1,0:T(8,128)(2,1)S(1)}, u32[]{:S(2)}, u32[]{:S(2)}) collective-permute-start(bf16[96,768]{1,0:T(8,128)(2,1)} %add_parts.23), channel_id=1, source_target_pairs={{0,48},{2,14},{4,52},{6,2},{8,56},{10,6},{12,60},{14,10},{16,0},{1... | collective-permute-start | bytes 442376 | tf_op jit(solution)/shard_map/ppermute | solution.py:1055
  426.9 9.9 %collective-permute-start.46 = (bf16[96,768]{1,0:T(8,128)(2,1)}, bf16[96,768]{1,0:T(8,128)(2,1)S(1)}, u32[]{:S(2)}, u32[]{:S(2)}) collective-permute-start(bf16[96,768]{1,0:T(8,128)(2,1)} %add_parts.23), channel_id=1, source_target_pairs={{0,32},{2,10},{4,36},{6,14},{8,40},{10,2},{12,44},{14,6},{16,48},{... | collective-permute-start | bytes 442376 | tf_op jit(solution)/shard_map/ppermute | solution.py:1055
  430.9 6.0 %collective-permute-start.45 = (bf16[96,768]{1,0:T(8,128)(2,1)}, bf16[96,768]{1,0:T(8,128)(2,1)S(1)}, u32[]{:S(2)}, u32[]{:S(2)}) collective-permute-start(bf16[96,768]{1,0:T(8,128)(2,1)} %add_parts.23), channel_id=1, source_target_pairs={{0,16},{2,6},{4,20},{6,10},{8,24},{10,14},{12,28},{14,2},{16,32},{... | collective-permute-start | bytes 442376 | tf_op jit(solution)/shard_map/ppermute | solution.py:1055
  431.8 15.0 %copy-start.4 = (bf16[4,4,112,384]{3,2,1,0:T(8,128)(2,1)}, bf16[4,4,112,384]{3,2,1,0:T(8,128)(2,1)S(1)}, u32[]{:S(2)}) copy-start(bf16[4,4,112,384]{3,2,1,0:T(8,128)(2,1)S(1)} %pad_maximum_fusion.1.refs_1_) | copy-start | bytes 4128772
  433.8 42.0 %collective-permute-start.31 = (bf16[4,4,112,384]{3,2,1,0:T(8,128)(2,1)S(1)}, bf16[4,4,112,384]{3,2,1,0:T(8,128)(2,1)}, u32[]{:S(2)}, u32[]{:S(2)}) collective-permute-start(bf16[4,4,112,384]{3,2,1,0:T(8,128)(2,1)S(1)} %pad_maximum_fusion.1.refs_1_), channel_id=1, source_target_pairs={{0,2},{2,0},{1,3},{3,1},{4,6},{6,4},{5,7},{7,5},{8,10},{10,8},{9,1... | collective-permute-start | bytes 4128776 | tf_op jit(solution)/shard_map/ppermute | solution.py:1046
  437.0 11.8 %collective-permute-start.49 = (bf16[4,96,768]{2,1,0:T(8,128)(2,1)S(1)}, bf16[4,96,768]{2,1,0:T(8,128)(2,1)S(1)}, u32[]{:S(2)}, u32[]{:S(2)}) collective-permute-start(bf16[4,96,768]{2,1,0:T(8,128)(2,1)S(1)} %get-tuple-element.270), channel_id=1, source_target_pairs={{0,8},{2,34},{4,12},{6,38},{8,0},{10,42},{12,4},{14,46},{16,24},{1... | collective-permute-start | bytes 1769480 | tf_op jit(solution)/shard_map/ppermute | solution.py:1055
  439.8 15.3 %collective-permute-start.48 = (bf16[4,96,768]{2,1,0:T(8,128)(2,1)S(1)}, bf16[4,96,768]{2,1,0:T(8,128)(2,1)S(1)}, u32[]{:S(2)}, u32[]{:S(2)}) collective-permute-start(bf16[4,96,768]{2,1,0:T(8,128)(2,1)S(1)} %get-tuple-element.270), channel_id=1, source_target_pairs={{0,4},{2,18},{4,8},{6,22},{8,12},{10,26},{12,0},{14,30},{16,20},{1... | collective-permute-start | bytes 1769480 | tf_op jit(solution)/shard_map/ppermute | solution.py:1055
  439.8 15.3 %collective-permute-start.50 = (bf16[4,96,768]{2,1,0:T(8,128)(2,1)S(1)}, bf16[4,96,768]{2,1,0:T(8,128)(2,1)S(1)}, u32[]{:S(2)}, u32[]{:S(2)}) collective-permute-start(bf16[4,96,768]{2,1,0:T(8,128)(2,1)S(1)} %get-tuple-element.270), channel_id=1, source_target_pairs={{0,12},{2,50},{4,0},{6,54},{8,4},{10,58},{12,8},{14,62},{16,28},{1... | collective-permute-start | bytes 1769480 | tf_op jit(solution)/shard_map/ppermute | solution.py:1055
  455.4 20.4 %copy-start = (bf16[4,4,96,768]{3,2,1,0:T(8,128)(2,1)}, bf16[4,4,96,768]{3,2,1,0:T(8,128)(2,1)S(1)}, u32[]{:S(2)}) copy-start(bf16[4,4,96,768]{3,2,1,0:T(8,128)(2,1)S(1)} %pad_maximum_fusion.refs_1_) | copy-start | bytes 7077892
  455.4 36.2 %collective-permute-start.51 = (bf16[4,4,96,768]{3,2,1,0:T(8,128)(2,1)S(1)}, bf16[4,4,96,768]{3,2,1,0:T(8,128)(2,1)}, u32[]{:S(2)}, u32[]{:S(2)}) collective-permute-start(bf16[4,4,96,768]{3,2,1,0:T(8,128)(2,1)S(1)} %pad_maximum_fusion.refs_1_), channel_id=1, source_target_pairs={{0,2},{2,0},{1,3},{3,1},{4,6},{6,4},{5,7},{7,5},{8,10},{10,8},{9,1... | collective-permute-start | bytes 7077896 | tf_op jit(solution)/shard_map/ppermute | solution.py:1046
  484.2 18.8 %collective-permute-start.37 = (f32[72,384]{1,0:T(8,128)S(1)}, f32[72,384]{1,0:T(8,128)S(1)}, u32[]{:S(2)}, u32[]{:S(2)}) collective-permute-start(f32[72,384]{1,0:T(8,128)S(1)} %slice.100), channel_id=1, source_target_pairs={{0,1},{1,0},{2,3},{3,2},{4,5},{5,4},{6,7},{7,6},{8,9},{9,8},{10,11... | collective-permute-start | bytes 331784 | tf_op jit(solution)/shard_map/ppermute | solution.py:1046
  (35 other events, 61.8 us)
Sparse Core Ops, SparseCore 0:
  295.4 55.4 all-gather.2

commit v3 on v2

--- a/solution.py
+++ b/solution.py
@@ -287,13 +287,21 @@
         out_ref[:, lanes_of(b)] = tmp[b].astype(out_ref.dtype)
 
 
-def finish_result(at_ref, x_ref, own_ref, other_ref, vec_ref, out_ref, x_s, tmp):
-    def body(start, c):
-        x_s[pl.ds(start, RB), :] = add_branch(x_ref, own_ref, other_ref, vec_ref.at[0], 5, at_ref[1], start, RB)
-        return c
-
-    row_loop(body)
-    by_slot(at_ref, x_s, out_ref, tmp)
+def finish_result(at_ref, x_ref, own_ref, other_ref, vec_ref, out_ref, y_s, tmp):
+    def put(first_lane):
+        lanes = pl.ds(first_lane, C)
+
+        def body(start, c):
+            rows = pl.ds(start, RB)
+            y = own_ref[rows, :].astype(F32) + other_ref[rows, :].astype(F32) + vec_ref[0, 5:6, lanes]
+            y_s[rows, lanes] = x_ref[rows, lanes] + row_mask(start, RB, at_ref[1]) * y
+            return c
+
+        row_loop(body)
+
+    pl.when(at_ref[0] == 0)(functools.partial(put, 0))
+    pl.when(at_ref[0] != 0)(functools.partial(put, C))
+    by_slot(at_ref, y_s, out_ref, tmp)
 
 
 def finish_grad(at_ref, g_ref, own_ref, other_ref, x_ref, vec_ref, out_ref, x_s, tmp):
@@ -402,7 +410,8 @@
         acc[...] += part
 
 
-def ff_forward(at_ref, x_ref, own_ref, other_ref, vec_ref, up_ref, upb_ref, dn_ref, xo_ref, h_ref, p_ref, b_s, acc):
+def ff_forward(last, at_ref, x_ref, own_ref, other_ref, vec_ref, up_ref, upb_ref, dn_ref, xo_ref, h_ref, *refs):
+    *p_refs, b_s, acc = refs
     j = pl.program_id(0)
 
     @pl.when(j == 0)
@@ -424,7 +433,25 @@
 
     @pl.when(j == pl.num_programs(0) - 1)
     def _():
-        p_ref[...] = acc[...].astype(BF)
+        if not last:
+            p_refs[0][...] = acc[...].astype(BF)
+        else:
+            low, high = acc[:, :C].astype(BF), acc[:, C:].astype(BF)
+            own = at_ref[0] == 0
+            p_refs[0][...] = jnp.where(own, low, high)
+            p_refs[1][...] = jnp.where(own, high, low)
+
+
+def put_by_core(at_ref, keep_ref, give_ref, at, low, high):
+    @pl.when(at_ref[4] == 0)
+    def _():
+        keep_ref[at] = low
+        give_ref[at] = high
+
+    @pl.when(at_ref[4] != 0)
+    def _():
+        keep_ref[at] = high
+        give_ref[at] = low
 
 
 def ff_backward(joined, *refs):
@@ -438,7 +465,7 @@
     if joined:
         go_ref, ngrad_ref = refs[:2]
         refs = refs[2:]
-    e_ref, dh_ref, dm_ref, b_ref, gupb_ref, gdnb_ref, p_ref, acc = refs
+    keep_ref, give_ref, gupb_ref, gdnb_ref, p_ref, dm_s, acc = refs
     j = pl.program_id(0)
 
     @pl.when(j == 0)
@@ -455,9 +482,10 @@
                 s1 = s1 + jnp.sum(dg, 0, keepdims=True)
                 s2 = s2 + jnp.sum(dn, 0, keepdims=True)
             dm = (row_mask(start, RB, at_ref[1]) * g).astype(BF)
-            dm_ref[at, :] = dm
+            dm_s[at, :] = dm
             xhat, _ = normalize(x_ref[at, :])
-            b_ref[at, :] = (xhat * vec_ref[0, 2:3, :] + vec_ref[0, 3:4, :]).astype(BF)
+            b = (xhat * vec_ref[0, 2:3, :] + vec_ref[0, 3:4, :]).astype(BF)
+            put_by_core(at_ref, keep_ref, give_ref, (at, pl.ds(0, D)), dm, b)
             return sums + jnp.sum(dm.astype(F32), 0, keepdims=True), s1, s2
 
         zero = jnp.zeros((1, D), F32)
@@ -469,10 +497,10 @@
 
     h = h_ref[...]
     half, t, hh, c0 = gelu_parts(h)
-    e_ref[...] = (h * half).astype(BF)
+    e = (h * half).astype(BF)
     slope = half + 0.5 * c0 * h * (1.0 - t * t) * (1.0 + 3 * 0.044715 * hh)
-    dh = (dot_nt(dm_ref[...], dn_ref[0]) * slope).astype(BF)
-    dh_ref[...] = dh
+    dh = (dot_nt(dm_s[...], dn_ref[0]) * slope).astype(BF)
+    put_by_core(at_ref, keep_ref, give_ref, (slice(None), pl.ds(pl.multiple_of(D + j * FC, 128), FC)), e, dh)
     gupb_ref[...] = jnp.sum(dh.astype(F32), 0, keepdims=True)
     collect(j, acc, dot_nt(dh, up_ref[0]))
 
@@ -482,25 +510,7 @@
 
 
 FIRST, SECOND = 5, 6
-
-
-def put_pieces(at_ref, ref, first, value):
-    for n in range(value.shape[0] // PIECE):
-        block = first + n // 4
-        at = lax.rem(block - at_ref[FIRST] + 4, 4), lax.rem(n % 4 - at_ref[SECOND] + 4, 4), pl.ds(0, PIECE)
-        ref[at] = value[n * PIECE : (n + 1) * PIECE]
-
-
-def put_halves(at_ref, keep_ref, give_ref, first, low, high):
-    @pl.when(at_ref[4] == 0)
-    def _():
-        put_pieces(at_ref, keep_ref, first, low)
-        put_pieces(Swapped(at_ref), give_ref, first, high)
-
-    @pl.when(at_ref[4] != 0)
-    def _():
-        put_pieces(at_ref, keep_ref, first, high)
-        put_pieces(Swapped(at_ref), give_ref, first, low)
+WIDE = 3 * D
 
 
 class Swapped:
@@ -511,18 +521,24 @@
         return self.at_ref[{FIRST: SECOND, SECOND: FIRST}.get(i, i)]
 
 
-def ff_weights(at_ref, e_ref, dm_ref, b_ref, dh_ref, keep_ref, give_ref):
-    j = pl.program_id(0)
-    down = dot_tn(e_ref[...], dm_ref[...]).astype(BF)
-    up = dot_tn(dh_ref[...], b_ref[...]).astype(BF)
-    put_halves(at_ref, keep_ref, give_ref, 2 * j, down, up)
+def put_pieces(at_ref, ref, value):
+    for n in range(4):
+        ref[lax.rem(n - at_ref[SECOND] + 4, 4), pl.ds(0, PIECE)] = value[n * PIECE : (n + 1) * PIECE]
+
+
+def ff_weights(at_ref, mine_ref, got_ref, *outs):
+    for k, out_ref in enumerate(outs):
+        block = lax.rem(at_ref[FIRST] + k, 4)
+        lanes = pl.ds(pl.multiple_of(D + block * 4 * PIECE, 128), 4 * PIECE)
+        total = sum(dot_tn(ref[:, lanes], ref[:, pl.ds(0, D)]) for ref in (mine_ref, got_ref))
+        put_pieces(at_ref, out_ref, total.astype(BF))
 
 
 def mixer_backward(
     last, at_ref, g_in_ref, own_ref, other_ref, x1_ref, x0_ref, u_ref, qs_ref, g_ref, ks_ref, vec_ref, inw_ref, outw_ref,
     sw_ref, sb_ref, skip_ref, fe_ref, fo_ref, ie_ref, io_ref,
-    go_ref, ngrad_ref, goutb_ref, ginb_ref, gsw_ref, gsb_ref, gskip_ref, dk_ref, p_ref, dy_ref, a_ref, z_ref, du_ref,
-    nown_ref, dz_s, dg_s, w1_s, w2_s, dw0_s, rhs_e, rhs_o, se, so, rhs2_e, rhs2_o, inv_s,
+    go_ref, ngrad_ref, goutb_ref, ginb_ref, gsw_ref, gsb_ref, gskip_ref, dk_ref, p_ref, keep_ref, give_ref,
+    nown_ref, dy_ref, a_ref, z_ref, du_ref, dz_s, dg_s, w1_s, w2_s, dw0_s, rhs_e, rhs_o, se, so, rhs2_e, rhs2_o, inv_s,
 ):
     def first(start, c):
         at = pl.ds(start, RB)
@@ -602,6 +618,18 @@
     for s in range(1, 3):
         part += dot_nt(du_ref[:, pl.ds(s * C, C)], inw_ref[0, s])
     p_ref[...] = part.astype(BF)
+
+    def spread(start, c):
+        rows = pl.ds(start, RB)
+        a, dy, z = a_ref[rows, :], dy_ref[rows, :], z_ref[rows, :]
+        du = [du_ref[rows, pl.ds(s * C, C)] for s in range(3)]
+        lane = 0
+        for low, high in ((a, a), (du[0], du[2]), (a, dy), (du[1], z)):
+            put_by_core(at_ref, keep_ref, give_ref, (rows, pl.ds(lane, low.shape[1])), low, high)
+            lane += low.shape[1]
+        return c
+
+    row_loop(spread)
     nown_ref[...] = jnp.zeros_like(nown_ref)
     if last:
 
@@ -621,35 +649,20 @@
     return jnp.concatenate([hi, value - hi], 0).astype(BF)
 
 
-def put_pack(at_ref, ref, rows, half):
-    for n in range(16):
-        at = lax.rem(n // 4 - at_ref[FIRST] + 4, 4), lax.rem(n % 4 - at_ref[SECOND] + 4, 4), pl.ds(PIECE, 16)
-        first = half * (PACK // 2) + n * 8
-        ref[at] = put_split_rows(rows[first : first + 8, :])
-
-
-def mixer_weights(packed, at_ref, *refs):
+def mixer_weights(packed, at_ref, mine_ref, got_ref, *refs):
     if packed:
-        pack_ref, refs = refs[0], refs[1:]
-    a_ref, du_ref, z_ref, dy_ref, keep_ref, give_ref = refs
-    for n in range(2):
-        low = dot_tn(a_ref[...], du_ref[:, pl.ds(n * C, C)]).astype(BF)
-        if n == 0:
-            high = dot_tn(a_ref[...], du_ref[:, pl.ds(2 * C, C)]).astype(BF)
-        else:
-            high = dot_tn(dy_ref[...], z_ref[...]).astype(BF)
-        put_halves(at_ref, keep_ref, give_ref, 2 * n, low, high)
-    if packed:
-
-        @pl.when(at_ref[4] == 0)
-        def _():
-            put_pack(at_ref, keep_ref, pack_ref, 0)
-            put_pack(Swapped(at_ref), give_ref, pack_ref, 1)
-
-        @pl.when(at_ref[4] != 0)
-        def _():
-            put_pack(at_ref, keep_ref, pack_ref, 1)
-            put_pack(Swapped(at_ref), give_ref, pack_ref, 0)
+        pack_refs, refs = refs[:2], refs[2:]
+    for k, out_ref in enumerate(refs):
+        block = lax.rem(at_ref[FIRST] + k, 4)
+        left = pl.multiple_of(jnp.where(block < 2, block, block + 1) * C, 128)
+        right = pl.multiple_of(jnp.where(block < 2, D, 2 * D + C), 128)
+        total = sum(dot_tn(ref[:, pl.ds(left, C)], ref[:, pl.ds(right, C)]) for ref in (mine_ref, got_ref))
+        put_pieces(at_ref, out_ref, total.astype(BF))
+        if packed:
+            for n in range(4):
+                rows = pl.ds(pl.multiple_of(block * 32 + n * 8, 8), 8)
+                value = pack_refs[0][rows, :] + pack_refs[1][rows, :]
+                out_ref[lax.rem(n - at_ref[SECOND] + 4, 4), pl.ds(PIECE, 16)] = put_split_rows(value)
 
 
 def add_parts(count, sides, *refs):
@@ -723,7 +736,7 @@
 
 
 def pack_small(at_ref, gnet_ref, gout_ref, nown_ref, *refs):
-    out_ref = refs[-1]
+    keep_ref, give_ref, out_ref = refs[-3:]
     out_ref[...] = jnp.zeros_like(out_ref)
     out_ref[0:NET, :] = gnet_ref[...]
     for j in range(2):
@@ -747,6 +760,7 @@
                     put(ref[j : j + 1, i * C : (i + 1) * C])
         put(gskip[...])
         put(gout_ref[l])
+    put_by_core(at_ref, keep_ref, give_ref, slice(None), out_ref[: PACK // 2], out_ref[PACK // 2 :])
 
 
 def sds(shape, dtype=F32):
@@ -881,16 +895,16 @@
     return pl.BlockSpec((rows, width), lambda j: (0, j))
 
 
-def run_ff_forward(l, at, x, own, other, vec, up, upb, dn, after):
-    return pl.pallas_call(
-        functools.partial(body_without, ff_forward, 8, len(after)),
+def run_ff_forward(l, last, at, x, own, other, vec, up, upb, dn, after):
+    return pl.pallas_call(
+        functools.partial(body_without, functools.partial(ff_forward, last), 8, len(after)),
         grid=(FH // FC,),
         in_specs=[
             SMEM, fixed((T, D)), fixed((T, D)), fixed((T, D)), layer_of(vec, l),
             up_spec(l), pl.BlockSpec((1, 1, FC), lambda j: (l, 0, j)), down_spec(l),
         ] + [ANY] * len(after),
-        out_specs=[fixed((T, D)), hidden_spec(T), fixed((T, D))],
-        out_shape=[sds((T, D)), sds((T, FH)), sds((T, D), BF)],
+        out_specs=[fixed((T, D)), hidden_spec(T)] + ([fixed((T, C))] * 2 if last else [fixed((T, D))]),
+        out_shape=[sds((T, D)), sds((T, FH))] + ([sds((T, C), BF)] * 2 if last else [sds((T, D), BF)]),
         scratch_shapes=[pltpu.VMEM((T, D), BF), pltpu.VMEM((T, D), F32)],
         name="ff_forward",
         **params(10),
@@ -906,33 +920,29 @@
     specs += [fixed((T, D)), hidden_spec(T), layer_of(vec, l), up_spec(l), down_spec(l)]
     out_specs = [fixed((T, D)), fixed((2, D))] if joined else []
     outs = [sds((T, D)), sds((2, D))] if joined else []
-    out_specs += [hidden_spec(T), hidden_spec(T), fixed((T, D)), fixed((T, D)), hidden_spec(1), fixed((1, D)), fixed((T, D))]
-    outs += [
-        sds((T, FH), BF), sds((T, FH), BF), sds((T, D), BF), sds((T, D), BF), sds((1, FH)), sds((1, D)), sds((T, D), BF),
-    ]
+    out_specs += [fixed((T, WIDE)), fixed((T, WIDE)), hidden_spec(1), fixed((1, D)), fixed((T, D))]
+    outs += [sds((T, WIDE), BF), sds((T, WIDE), BF), sds((1, FH)), sds((1, D)), sds((T, D), BF)]
     return pl.pallas_call(
         functools.partial(body_without, functools.partial(ff_backward, joined), len(args), len(after)),
         grid=(FH // FC,),
         in_specs=specs + [ANY] * len(after),
         out_specs=out_specs,
         out_shape=outs,
-        scratch_shapes=[pltpu.VMEM((T, D), F32)],
+        scratch_shapes=[pltpu.VMEM((T, D), BF), pltpu.VMEM((T, D), F32)],
         name="ff_backward",
         **params(10),
     )(*args, *after)
 
 
-def run_ff_weights(at, e, dm, b, dh):
-    wide = FH // 2
+def run_ff_weights(at, mine, got):
     return pl.pallas_call(
         ff_weights,
-        grid=(2,),
-        in_specs=[SMEM, hidden_spec(T, wide), fixed((T, D)), fixed((T, D)), hidden_spec(T, wide)],
-        out_specs=[fixed((4, 4, PIECE, D))] * 2,
-        out_shape=[sds((4, 4, PIECE, D), BF)] * 2,
+        in_specs=[SMEM, WHOLE, WHOLE],
+        out_specs=[WHOLE] * 4,
+        out_shape=[sds((4, PIECE, D), BF)] * 4,
         name="ff_weights",
         **params(7),
-    )(at, e, dm, b, dh)
+    )(at, mine, got)
 
 
 def run_mixer_backward(l, last, at, g_in, own, other, x1, x0, u, qs, g, ks, vec, inw, outw, sw, sb, skip, after):
@@ -940,7 +950,7 @@
     specs = [SMEM] + [WHOLE] * 8 + [layer_of(m, l) for m in (ks, vec, inw, outw, sw, sb, skip)] + [WHOLE] * 4
     outs = [
         sds((T, D)), sds((2, D)), sds((1, D)), sds((1, 3 * C)), sds((3, 3 * C)), sds((1, 3 * C)), sds((1, C)),
-        sds((T, C)), sds((T, D), BF), sds((T, D), BF), sds((T, D), BF), sds((T, C), BF), sds((T, 3 * C), BF), sds((2, D)),
+        sds((T, C)), sds((T, D), BF), sds((T, WIDE), BF), sds((T, WIDE), BF), sds((2, D)),
     ]
     tc = pltpu.VMEM((T, C), F32)
     return pl.pallas_call(
@@ -950,6 +960,7 @@
         out_specs=[WHOLE] * len(outs),
         out_shape=outs,
         scratch_shapes=[
+            pltpu.VMEM((T, D), BF), pltpu.VMEM((T, D), BF), pltpu.VMEM((T, C), BF), pltpu.VMEM((T, 3 * C), BF),
             tc, tc, tc, tc, tc, *spectrum_scratch(),
             pltpu.VMEM((6 * H, 2 * C), BF), pltpu.VMEM((6 * H, 2 * C), BF), pltpu.VMEM((T, 2 * C), F32),
         ],
@@ -958,17 +969,16 @@
     )(*args, *after)
 
 
-def run_mixer_weights(at, a, du, z, dy, pack=None):
-    packed = [] if pack is None else [pack]
-    rows = PIECE + 16 * len(packed)
-    return pl.pallas_call(
-        functools.partial(mixer_weights, bool(packed)),
-        in_specs=[SMEM] + [WHOLE] * (4 + len(packed)),
-        out_specs=[WHOLE] * 2,
-        out_shape=[sds((4, 4, rows, C), BF)] * 2,
+def run_mixer_weights(at, mine, got, pack=()):
+    rows = PIECE + (16 if pack else 0)
+    return pl.pallas_call(
+        functools.partial(mixer_weights, bool(pack)),
+        in_specs=[SMEM] + [WHOLE] * (2 + len(pack)),
+        out_specs=[WHOLE] * 4,
+        out_shape=[sds((4, rows, C), BF)] * 4,
         name="mixer_weights",
         **params(5),
-    )(at, *packed, a, du, z, dy)
+    )(at, mine, got, *pack)
 
 
 def run_add(parts, count, after=(), sides=1):
@@ -1000,6 +1010,19 @@
     )(x, *after)
 
 
+def run_behind(arrays, after):
+    count = len(arrays)
+    return pl.pallas_call(
+        lambda *refs: None,
+        in_specs=[ANY] * (count + len(after)),
+        out_specs=[ANY] * count,
+        out_shape=[sds(x.shape, x.dtype) for x in arrays],
+        input_output_aliases={i: i for i in range(count)},
+        name="behind",
+        **params(1),
+    )(*arrays, *after)
+
+
 def run_place(body, at, ins, into, shapes, out_specs, steps, width, name):
     aliases = {} if into is None else {3: 0, 4: 1}
     into = [] if into is None else list(into)
@@ -1055,15 +1078,20 @@
     return lax.ppermute(x, ("y", "x", "c"), pairs)
 
 
-def spread_sum(*halves):
-    after = yield [h for pair in halves for h in pair]
-    parts = [part for keep, give in halves for part in (keep, swap(give, "c"))]
-    blocks = run_add(parts, 4, after, len(halves))
-    after = yield blocks
-    pieces = run_add([blocks[0]] + [shift(blocks[k], FIRST, k) for k in range(1, 4)], 4, after)
-    after = yield pieces
-    [piece] = run_add([pieces[0]] + [shift(pieces[m], SECOND, m) for m in range(1, 4)], 1, after)
-    yield run_add([piece, swap(piece, "zl")], 1)
+def send_first(blocks):
+    return [blocks[0]] + [shift(blocks[k], FIRST, k) for k in range(1, 4)]
+
+
+def sum_first(*gradients, after=()):
+    return run_add([p for came in gradients for p in came], 4, after, len(gradients))
+
+
+def sum_second(pieces, after=()):
+    return run_add([pieces[0]] + [shift(pieces[m], SECOND, m) for m in range(1, 4)], 1, after)[0]
+
+
+def sum_near(piece, after=()):
+    return run_add([piece, swap(piece, "zl")], 1, after)[0]
 
 
 def gather_near(piece):
@@ -1082,8 +1110,9 @@
     return pl.pallas_call(
         pack_small,
         in_specs=[SMEM] + [WHOLE] * (3 + len(small)),
-        out_specs=WHOLE,
-        out_shape=sds((PACK, C)),
+        out_specs=[WHOLE] * 2,
+        out_shape=[sds((PACK // 2, C))] * 2,
+        scratch_shapes=[pltpu.VMEM((PACK, C), F32)],
         name="pack_small",
         **params(2),
     )(at, gnet, gout, nown, *small)
@@ -1119,7 +1148,8 @@
     upb = up_bias.reshape(layers, 1, FH)
 
     cot = run_copy_after(cotangent, [x])
-    grad = run_arrange(at, cotangent, swap(cot, "zh"))
+    cot_other = swap(cot, "zh")
+    grad = run_arrange(at, cotangent, cot_other)
     saved = []
     joint = None
     for l in range(layers):
@@ -1128,72 +1158,57 @@
         if joint is not None:
             x, made = made[0], made[1:]
         u, qs, g, p = made
+        if l == 0:
+            [p] = run_behind([p], [cot_other])
         after = [grad] if l == 0 else []
-        x1, h, p2 = run_ff_forward(l, at, x, p, swap(p, "zh"), vec, up_weight, upb, down_weight, after)
+        last = l == layers - 1
+        x1, h, *p2 = run_ff_forward(l, last, at, x, p, swap(p, "zh"), vec, up_weight, upb, down_weight, after)
         saved.append((x, u, qs, g, x1, h))
-        joint = (p2, swap(p2, "zh")) if l < layers - 1 else p2
+        joint = p2[0], swap(p2[-1], "zh")
         x = x1
+    last_branch = joint
 
     joint = None
-    sums = []
     small = [None] * layers
     norms = {}
-
-    def advance(after):
-        made = []
-        for entry in sums:
-            try:
-                entry[1] = entry[0].send(after) if entry[1] else next(entry[0])
-            except StopIteration:
-                pass
-            made += entry[1]
-        return made
-
-    def begin(*halves):
-        sums.append([spread_sum(*halves), []])
-
-    result = None
     waits = []
+    came = {}
     for l in reversed(range(layers)):
         x0, u, qs, g, x1, h = saved[l]
         made = run_ff_backward(l, at, grad, joint, x1, h, vec, up_weight, down_weight, waits)
         if joint is not None:
             grad, norms[l + 1] = made[:2]
             made = made[2:]
-        e, dh, dm, b, gupb, gdnb, p = made
+        keep, give, gupb, gdnb, p = made
+        p, give = run_behind([p, give], [last_branch[1]] if l == layers - 1 else came["mixer", l + 1][1:])
         p_other = swap(p, "zh")
-        halves = run_ff_weights(at, e, dm, b, dh)
-        if l == 0:
-            begin(halves)
-        waits = advance([p]) if l == 0 else list(halves)
-        if l == layers - 1:
-            p2 = run_copy_after(p2, [p_other])
-            waits.append(p2)
+        halves = run_ff_weights(at, keep, swap(give, "c"))
+        came["ff", l] = send_first(halves)
+        waits = list(halves)
         made = run_mixer_backward(
             l, l == 0, at, grad, p, p_other, x1, x0, u, qs, g, ks, vec, inw, out_weight, sw, sb, skip, waits
         )
-        grad, norm1, goutb, ginb, gsw, gsb, gskip, dk, p, dy, a, z, du, nown = made
+        grad, norm1, goutb, ginb, gsw, gsb, gskip, dk, p, keep, give, nown = made
+        p, give = run_behind([p, give], came["ff", l][1:])
         joint = (p, swap(p, "zh"), x0)
         small[l] = (norm1, gdnb, goutb, gupb, ginb, gsw, gsb, gskip, dk)
-        pack = None
+        pack = ()
         if l == 0:
             norms[0] = jnp.zeros_like(nown)
             gfout, gnet = run_filter_backward(at, inner, fout, sines, cosines, [s[-1] for s in small])
             pack = run_pack_small(at, gnet, gfout, nown, [m for l in range(layers) for m in (norms[l], *small[l][:-1])])
-        mixer_halves = run_mixer_weights(at, a, du, z, dy, pack)
-        if l == 0:
-            begin(mixer_halves)
-        else:
-            begin(halves, mixer_halves)
-        waits = advance([p])
+            pack = pack[0], swap(pack[1], "c")
+        halves = run_mixer_weights(at, keep, swap(give, "c"), pack)
+        came["mixer", l] = send_first(halves)
+        waits = list(halves)
         if l == layers - 1:
-            result = run_finish_result(at, saved[l][4], p2, swap(p2, "zh"), vec, l)
+            result = run_finish_result(at, saved[l][4], *last_branch, vec, l)
             waits.append(result)
 
+    later = sum_near(sum_second(sum_first(came["ff", 1], came["mixer", 1], after=[p])))
+    ff = sum_near(sum_second(sum_first(came["ff", 0])))
+    mixer = sum_near(sum_second(sum_first(came["mixer", 0])))
     grad = run_finish_grad(at, grad, *joint, vec, 0, waits)
-    for _ in range(4):
-        advance([])
-    later, ff, mixer = (entry[1][0] for entry in sums)
     later = gather_plane(later)
     ff_out = run_place_ff(1, layers, at, later, None)
     mixer_out = run_place_mixer(1, layers, at, later, None, D)

time: 524 us -> 520 us (level)
  the two profiles are of different devices: /device:TPU:1 before, /device:TPU:8 now
where the time goes in v3:
time: 520 us; the launch traced here: 511 us
  Pallas kernels  211 us (41%)
  waiting for transfers between devices  155 us (30%)
  starting transfers between devices  85.2 us (16%)
  local copies, waits for them, and re-layouts  40.7 us (8%)
  between operations  15.6 us (3%)
    ppermute x23, waiting for transfers between devices, swap(): return lax.ppermute(x, axis, SWAP)  81.5 us
    ppermute x33, starting transfers between devices, shift(): return lax.ppermute(x, ('y', 'x', 'c'), pairs)  54.6 us
    all_gather x1, waiting for transfers between devices, gather_plane(): mine = lax.all_gather(piece, ('y', 'x'), axis=0, tiled=False)  42.4 us
    pallas_call x2, Pallas kernels, run_mixer_backward(): pl.pallas_call(functools.partial(body_without, functools.partial(mixer_ba...  39.1 us
    ppermute x33, waiting for transfers between devices, shift(): return lax.ppermute(x, ('y', 'x', 'c'), pairs)  31.3 us
    ppermute x23, starting transfers between devices, swap(): return lax.ppermute(x, axis, SWAP)  30.6 us
    unnamed x108, local copies, waits for them, and re-layouts  29.5 us
    pallas_call x4, Pallas kernels, run_place(): pl.pallas_call(functools.partial(body_without, body, 3, len(into)), grid=...  27.8 us
  transfers between devices with their start and end apart: 57, of which 22 were waited for; matrix products, arithmetic and copies ran while one was open for 3% of the time, Pallas kernels for 33%

profile of v3, /device:TPU:8, one launch (start us, length us, event | category | flops | bytes accessed | tf_op | source)
XLA Modules:
  0.0 511.0 jit_solution(5201622828037402564)
XLA Ops:
  9.5 4.0 collective-permute-start.1
  17.5 9.3 %filter_forward.1 = (f32[2,4,256,384]{3,2,1,0:T(8,128)}, f32[3,512,128]{2,1,0:T(8,128)}, f32[3,512,128]{2,1,0:T(8,128)}, f32[2,128,128]{2,1,0:T(8,128)}, f32[2,128,384]{2,1,0:T(8,128)}) custom-call(s32[7]{0:T(128)} %stack.149.at_ref.refs_0_, f32[512,128]{1,0:T(8,128)} %constant.31.clone.feats_ref, f32[512,128]{1,0:T(8,128)} %constant.32.clone.times_ref, ...), custom_call_target="tpu_custom_call" | custom-call | flops 12000000000 | bytes 10000 | tf_op jit(solution)/shard_map/filter_forward/pallas_call | solution.py:798
  30.6 2.5 arrange.2.refs_1_.refs_5_.refs_4_
  33.1 1.8 copy_after.1.refs_14_
  34.8 3.4 collective-permute-start.2
  38.3 10.9 %mixer_forward.2 = (f32[512,1152]{1,0:T(8,128)}, f32[4,256,384]{2,1,0:T(8,128)}, f32[512,384]{1,0:T(8,128)}, bf16[512,768]{1,0:T(8,128)(2,1)}) custom-call(s32[7]{0:T(128)} %stack.149.at_ref.refs_0_, f32[512,768]{1,0:T(8,128)} %arrange.2.refs_1_.refs_5_.refs_4_, f32[2,8,768]{2,1,0:T(8,128)} %pad_maximum_fusion.5.refs_2_.refs_4_.refs_5_.vec_ref.refs_10_.refs_8_, ...), custom_call_target="tpu_custom_call" | custom-call | flops 11000000512 | bytes 10000 | tf_op jit(solution)/shard_map/mixer_forward/pallas_call | solution.py:868
  51.6 2.7 arrange.3.refs_8_.refs_1_
  54.3 15.7 %collective-permute-done.3.refs_3_ = bf16[512,768]{1,0:T(8,128)(2,1)S(1)} collective-permute-done((bf16[512,768]{1,0:T(8,128)(2,1)}, bf16[512,768]{1,0:T(8,128)(2,1)S(1)}, u32[]{:S(2)}, u32[]{:S(2)}) %collective-permute-start.3) | collective-permute-done | bytes 786464 | tf_op jit(solution)/shard_map/ppermute | solution.py:1069
  71.0 9.7 %ff_forward.2 = (f32[512,768]{1,0:T(8,128)}, f32[512,1536]{1,0:T(8,128)}, bf16[512,768]{1,0:T(8,128)(2,1)}) custom-call(s32[7]{0:T(128)} %stack.149.at_ref.refs_0_, f32[512,768]{1,0:T(8,128)} %arrange.2.refs_1_.refs_5_.refs_4_, bf16[512,768]{1,0:T(8,128)(2,1)} %behind.5.refs_2_, bf16[512,768]{1,0:T(8,128)(2,1)} %copy-done.26, ...), custom_call_target="tpu_custom_call" | custom-call | flops 10000000000 | bytes 10000 | tf_op jit(solution)/shard_map/ff_forward/pallas_call | solution.py:899
  81.2 18.8 %collective-permute-done.4.refs_3_ = bf16[512,768]{1,0:T(8,128)(2,1)S(1)} collective-permute-done((bf16[512,768]{1,0:T(8,128)(2,1)}, bf16[512,768]{1,0:T(8,128)(2,1)S(1)}, u32[]{:S(2)}, u32[]{:S(2)}) %collective-permute-start.4) | collective-permute-done | bytes 786464 | tf_op jit(solution)/shard_map/ppermute | solution.py:1069
  100.8 12.2 %mixer_forward.3 = (f32[512,768]{1,0:T(8,128)}, f32[512,1152]{1,0:T(8,128)}, f32[4,256,384]{2,1,0:T(8,128)}, f32[512,384]{1,0:T(8,128)}, bf16[512,768]{1,0:T(8,128)(2,1)}) custom-call(s32[7]{0:T(128)} %stack.149.at_ref.refs_0_, f32[512,768]{1,0:T(8,128)} %get-tuple-element.126.refs_1_.refs_6_.refs_4_, bf16[512,768]{1,0:T(8,128)(2,1)} %get-tuple-element.127.refs_2_, ...), custom_call_target="tpu_custom_call" | custom-call | flops 11000000512 | bytes 10000 | tf_op jit(solution)/shard_map/mixer_forward/pallas_call | solution.py:868
  113.3 18.0 %collective-permute-done.5.refs_3_ = bf16[512,768]{1,0:T(8,128)(2,1)S(1)} collective-permute-done((bf16[512,768]{1,0:T(8,128)(2,1)}, bf16[512,768]{1,0:T(8,128)(2,1)S(1)}, u32[]{:S(2)}, u32[]{:S(2)}) %collective-permute-start.5) | collective-permute-done | bytes 786464 | tf_op jit(solution)/shard_map/ppermute | solution.py:1069
  132.2 9.7 %ff_forward.3 = (f32[512,768]{1,0:T(8,128)}, f32[512,1536]{1,0:T(8,128)}, bf16[512,384]{1,0:T(8,128)(2,1)}, bf16[512,384]{1,0:T(8,128)(2,1)}) custom-call(s32[7]{0:T(128)} %stack.149.at_ref.refs_0_, f32[512,768]{1,0:T(8,128)} %get-tuple-element.128.refs_1_.refs_5_.refs_4_, bf16[512,768]{1,0:T(8,128)(2,1)} %get-tuple-element.129.refs_2_, ...), custom_call_target="tpu_custom_call" | custom-call | flops 10000000000 | bytes 10000 | tf_op jit(solution)/shard_map/ff_forward/pallas_call | solution.py:899
  142.2 12.5 %ff_backward.2 = (bf16[512,2304]{1,0:T(8,128)(2,1)}, bf16[512,2304]{1,0:T(8,128)(2,1)}, f32[1,1536]{1,0:T(1,128)}, f32[1,768]{1,0:T(1,128)}, bf16[512,768]{1,0:T(8,128)(2,1)}) custom-call(s32[7]{0:T(128)} %stack.149.at_ref.refs_0_, f32[512,768]{1,0:T(8,128)} %arrange.3.refs_8_.refs_1_, f32[512,768]{1,0:T(8,128)} %get-tuple-element.130.x_ref.refs_2_.refs_4_, ...), custom_call_target="tpu_custom_call" | custom-call | flops 10000000000 | bytes 10000 | tf_op jit(solution)/shard_map/ff_backward/pallas_call | solution.py:925
  155.5 3.4 collective-permute-start.7
  161.6 6.5 %ff_weights.2 = (bf16[4,96,768]{2,1,0:T(8,128)(2,1)}, bf16[4,96,768]{2,1,0:T(8,128)(2,1)}, bf16[4,96,768]{2,1,0:T(8,128)(2,1)}, bf16[4,96,768]{2,1,0:T(8,128)(2,1)}) custom-call(s32[7]{0:T(128)} %stack.149.at_ref.refs_0_, bf16[512,2304]{1,0:T(8,128)(2,1)} %get-tuple-element.140.mine_ref, bf16[512,2304]{1,0:T(8,128)(2,1)} %copy-done.20), custom_call_target="tpu_custom_call" | custom-call | flops 7000000000 | bytes 10000 | tf_op jit(solution)/shard_map/ff_weights/pallas_call | solution.py:938
  169.6 2.7 collective-permute-start.10
  173.8 3.6 collective-permute-done.7.refs_3_
  178.2 19.4 %mixer_backward.2 = (f32[512,768]{1,0:T(8,128)}, f32[2,768]{1,0:T(2,128)}, f32[1,768]{1,0:T(1,128)}, f32[1,1152]{1,0:T(1,128)}, f32[3,1152]{1,0:T(4,128)}, /*ind...) custom-call(s32[7]{0:T(128)} %stack.149.at_ref.refs_0_, ...), custom_call_target="tpu_custom_call" | custom-call | flops 15000000512 | bytes 10000 | tf_op jit(solution)/shard_map/mixer_backward/pallas_call | solution.py:956
  199.0 3.2 collective-permute-start.12
  202.2 3.1 finish_result.1.refs_15_
  206.8 4.9 mixer_weights.2
  213.2 2.7 collective-permute-start.15
  217.4 3.3 collective-permute-done.12.refs_3_
  221.6 14.9 %ff_backward.3 = (f32[512,768]{1,0:T(8,128)}, f32[2,768]{1,0:T(2,128)}, bf16[512,2304]{1,0:T(8,128)(2,1)}, bf16[512,2304]{1,0:T(8,128)(2,1)}, f32[1,1536]{1,0:T(...) custom-call(s32[7]{0:T(128)} %stack.149.at_ref.refs_0_, f32[512,768]{1,0:T(8,128)} %get-tuple-element.146.refs_1_, ...), custom_call_target="tpu_custom_call" | custom-call | flops 10000000000 | bytes 10000 | tf_op jit(solution)/shard_map/ff_backward/pallas_call | solution.py:925
  237.4 3.2 collective-permute-start.17
  243.6 6.4 %ff_weights.3 = (bf16[4,96,768]{2,1,0:T(8,128)(2,1)}, bf16[4,96,768]{2,1,0:T(8,128)(2,1)}, bf16[4,96,768]{2,1,0:T(8,128)(2,1)}, bf16[4,96,768]{2,1,0:T(8,128)(2,1)}) custom-call(s32[7]{0:T(128)} %stack.149.at_ref.refs_0_, bf16[512,2304]{1,0:T(8,128)(2,1)} %get-tuple-element.164.mine_ref, bf16[512,2304]{1,0:T(8,128)(2,1)} %copy-done.21), custom_call_target="tpu_custom_call" | custom-call | flops 7000000000 | bytes 10000 | tf_op jit(solution)/shard_map/ff_weights/pallas_call | solution.py:938
  251.4 2.7 collective-permute-start.20
  255.7 3.4 collective-permute-done.17.refs_3_
  260.0 19.7 %mixer_backward.3 = (f32[512,768]{1,0:T(8,128)}, f32[2,768]{1,0:T(2,128)}, f32[1,768]{1,0:T(1,128)}, f32[1,1152]{1,0:T(1,128)}, f32[3,1152]{1,0:T(4,128)}, /*ind...) custom-call(s32[7]{0:T(128)} %stack.149.at_ref.refs_0_, ...), custom_call_target="tpu_custom_call" | custom-call | flops 15000000512 | bytes 10000 | tf_op jit(solution)/shard_map/mixer_backward/pallas_call | solution.py:956
  280.9 3.2 add_parts.12
  286.6 2.4 collective-permute-start.41
  290.2 3.2 collective-permute-done.40.refs_2_
  295.8 2.1 add_parts.13.refs_0_
  298.9 5.1 collective-permute-done.42.refs_1_
  304.7 1.8 add_parts.14
  306.8 7.1 %filter_backward.1 = (f32[2,64,384]{2,1,0:T(8,128)}, f32[64,384]{1,0:T(8,128)}) custom-call(s32[7]{0:T(128)} %stack.149.at_ref.refs_0_, f32[512,128]{1,0:T(8,128)} %constant.31.clone.feats_ref, f32[512,128]{1,0:T(8,128)} %constant.32.clone.times_ref, f32[2,128,128]{2,1,0:T(8,128)} %get-tuple-element.176.inner_ref, ...), custom_call_target="tpu_custom_call" | custom-call | flops 8000000000 | bytes 10000 | tf_op jit(solution)/shard_map/filter_backward/pallas_call | solution.py:813
  313.9 42.4 %all-gather.3.cloned.1.call-done = bf16[1536,1152]{1,0:T(8,128)(2,1)} async-done(((bf16[96,1152]{1,0:T(8,128)(2,1)}), bf16[1536,1152]{1,0:T(8,128)(2,1)}) %all-gather.3.cloned.1.call-update) | async-done | bytes 3538960 | tf_op jit(solution)/shard_map/all_gather | solution.py:1104
  356.9 2.0 pack_small.1
  359.4 3.6 collective-permute-done.24.refs_1_
  363.7 5.3 %mixer_weights.3 = (bf16[4,112,384]{2,1,0:T(8,128)(2,1)}, bf16[4,112,384]{2,1,0:T(8,128)(2,1)}, bf16[4,112,384]{2,1,0:T(8,128)(2,1)}, bf16[4,112,384]{2,1,0:T(8,128)(2,1)}) custom-call(s32[7]{0:T(128)} %stack.149.at_ref.refs_0_, bf16[512,2304]{1,0:T(8,128)(2,1)} %get-tuple-element.174.mine_ref, bf16[512,2304]{1,0:T(8,128)(2,1)} %collective-permute-done.23.got_ref, ...), custom_call_target="tpu_custom_call" | custom-call | flops 5000000000 | bytes 10000 | tf_op jit(solution)/shard_map/mixer_weights/pallas_call | solution.py:974
  369.3 2.7 collective-permute-start.26
  373.4 7.9 %collective-permute-done.25.refs_1_ = bf16[4,112,384]{2,1,0:T(8,128)(2,1)S(1)} collective-permute-done((bf16[4,112,384]{2,1,0:T(8,128)(2,1)}, bf16[4,112,384]{2,1,0:T(8,128)(2,1)S(1)}, u32[]{:S(2)}, u32[]{:S(2)}) %collective-permute-start.25) | collective-permute-done | bytes 344096 | tf_op jit(solution)/shard_map/ppermute | solution.py:1078
  383.0 2.1 add_parts.9
  386.6 1.8 collective-permute-start.29
  389.8 2.5 add_parts.15
  393.0 2.9 collective-permute-start.46
  396.6 1.7 add_parts.10.refs_0_
  402.1 1.9 add_parts.16.refs_0_
  410.7 2.5 collective-permute-start.32
  419.2 2.4 collective-permute-start.36
  421.6 4.5 collective-permute-done.51
  426.1 2.5 collective-permute-start.35
  434.7 2.0 collective-permute-start.54
  436.8 2.9 collective-permute-start.22
  439.9 2.8 collective-permute-done.53
  442.6 6.2 %collective-permute-done.52 = bf16[4,96,768]{2,1,0:T(8,128)(2,1)S(1)} collective-permute-done((bf16[4,96,768]{2,1,0:T(8,128)(2,1)S(1)}, bf16[4,96,768]{2,1,0:T(8,128)(2,1)S(1)}, u32[]{:S(2)}, u32[]{:S(2)}) %collective-permute-start.52) | collective-permute-done | bytes 589856 | tf_op jit(solution)/shard_map/ppermute | solution.py:1078
  449.3 7.2 %collective-permute-done.22.refs_3_ = bf16[512,768]{1,0:T(8,128)(2,1)S(1)} collective-permute-done((bf16[512,768]{1,0:T(8,128)(2,1)S(1)}, bf16[512,768]{1,0:T(8,128)(2,1)S(1)}, u32[]{:S(2)}, u32[]{:S(2)}) %collective-permute-start.22) | collective-permute-done | bytes 786464 | tf_op jit(solution)/shard_map/ppermute | solution.py:1069
  457.3 4.4 finish_grad.1
  461.7 7.6 %place_mixer.2 = (f32[2,3,768,384]{3,2,1,0:T(8,128)}, f32[2,384,768]{2,1,0:T(8,128)}) custom-call(s32[7]{0:T(128)} %stack.149.at_ref.refs_0_, bf16[1,4,4,96,1152]{4,3,2,1,0:T(8,128)(2,1)} %bitcast.94, bf16[1,4,4,96,1152]{4,3,2,1,0:T(8,128)(2,1)} %collective-permute-done.43.refs_2_), custom_call_target="tpu_custom_call" | custom-call | flops 6000000000 | bytes 10000 | tf_op jit(solution)/shard_map/place_mixer/pallas_call | solution.py:1029
  469.4 6.5 %place_mixer.3 = (f32[2,3,768,384]{3,2,1,0:T(8,128)}, f32[2,384,768]{2,1,0:T(8,128)}, f32[256,384]{1,0:T(8,128)}) custom-call(s32[7]{0:T(128)} %stack.149.at_ref.refs_0_, bf16[4,4,112,384]{3,2,1,0:T(8,128)(2,1)} %copy-done.6, bf16[4,4,112,384]{3,2,1,0:T(8,128)(2,1)} %collective-permute-done.38.refs_2_, ...), custom_call_target="tpu_custom_call", output_to_operand_aliasing={{0}: (3, {}), {1}: (4, {})} | custom-call | flops 6000000000 | bytes 10000 | tf_op jit(solution)/shard_map/place_mixer/pallas_call | solution.py:1029
  477.7 2.9 collective-permute-start.44
  480.7 7.2 %place_ff.2 = (f32[2,768,1536]{2,1,0:T(8,128)}, f32[2,1536,768]{2,1,0:T(8,128)}) custom-call(s32[7]{0:T(128)} %stack.149.at_ref.refs_0_, bf16[1,4,4,96,1152]{4,3,2,1,0:T(8,128)(2,1)} %bitcast.95, bf16[1,4,4,96,1152]{4,3,2,1,0:T(8,128)(2,1)} %collective-permute-done.43.refs_2_), custom_call_target="tpu_custom_call" | custom-call | flops 6000000000 | bytes 10000 | tf_op jit(solution)/shard_map/place_ff/pallas_call | solution.py:1029
  487.9 6.5 %place_ff.3 = (f32[2,768,1536]{2,1,0:T(8,128)}, f32[2,1536,768]{2,1,0:T(8,128)}) custom-call(s32[7]{0:T(128)} %stack.149.at_ref.refs_0_, bf16[4,4,96,768]{3,2,1,0:T(8,128)(2,1)} %copy-done, bf16[4,4,96,768]{3,2,1,0:T(8,128)(2,1)} %collective-permute-done.55.refs_2_, ...), custom_call_target="tpu_custom_call", output_to_operand_aliasing={{0}: (3, {}), {1}: (4, {})} | custom-call | flops 6000000000 | bytes 10000 | tf_op jit(solution)/shard_map/place_ff/pallas_call | solution.py:1029
  (240 shorter events, 91.4 us)
Async XLA Ops:
  7.2 349.1 %all-gather.3.cloned.1.call-start = ((), (), s32[]{:S(2)}) async-start(), calls=%async_computation | async-start | bytes 3760128 | tf_op jit(solution)/shard_map/all_gather | solution.py:1104
  9.5 19.8 %collective-permute-start.1 = (f32[2,8,384]{2,1,0:T(8,128)S(1)}, f32[2,8,384]{2,1,0:T(8,128)S(1)}, u32[]{:S(2)}, u32[]{:S(2)}) collective-permute-start(f32[2,8,384]{2,1,0:T(8,128)S(1)} %stack.152), channel_id=1, source_target_pairs={{0,1},{1,0},{2,3},{3,2},{4,5},{5,4},{6,7},{7,6},{8,9},{9,8},{10,11... | collective-permute-start | bytes 73736 | tf_op jit(solution)/shard_map/ppermute | solution.py:1069
  13.4 16.4 %collective-permute-start = (bf16[512,384]{1,0:T(8,128)(2,1)}, bf16[512,384]{1,0:T(8,128)(2,1)S(1)}, u32[]{:S(2)}, u32[]{:S(2)}) collective-permute-start(bf16[512,384]{1,0:T(8,128)(2,1)} %own_ref.2), channel_id=1, source_target_pairs={{0,1},{1,0},{2,3},{3,2},{4,5},{5,4},{6,7},{7,6},{8,9},{9,8},{10,11... | collective-permute-start | bytes 1179656 | tf_op jit(solution)/shard_map/ppermute | solution.py:1069
  17.4 9.3 %copy-start.18 = (f32[2,384]{1,0:T(2,128)S(1)}, f32[2,384]{1,0:T(2,128)}, u32[]{:S(2)}) copy-start(f32[2,384]{1,0:T(2,128)} %param.38) | copy-start | bytes 9220
  17.4 9.9 %copy-start.16 = (f32[2,3,384]{2,0,1:T(2,128)S(1)}, f32[2,3,384]{2,0,1:T(2,128)}, u32[]{:S(2)}) copy-start(f32[2,3,384]{2,0,1:T(2,128)} %param.33) | copy-start | bytes 27652
  17.4 10.5 %copy-start.17 = (f32[2,3,384]{2,0,1:T(2,128)S(1)}, f32[2,3,384]{2,0,1:T(2,128)}, u32[]{:S(2)}) copy-start(f32[2,3,384]{2,0,1:T(2,128)} %param.31) | copy-start | bytes 27652
  17.4 11.1 %copy-start.14 = (f32[2,3,3,384]{3,0,2,1:T(2,128)S(1)}, f32[2,3,3,384]{3,0,2,1:T(2,128)}, u32[]{:S(2)}) copy-start(f32[2,3,3,384]{3,0,2,1:T(2,128)} %param.32) | copy-start | bytes 82948
  34.8 14.3 %collective-permute-start.2 = (bf16[512,384]{1,0:T(8,128)(2,1)}, bf16[512,384]{1,0:T(8,128)(2,1)S(1)}, u32[]{:S(2)}, u32[]{:S(2)}) collective-permute-start(bf16[512,384]{1,0:T(8,128)(2,1)} %copy_after.1.refs_14_), channel_id=1, source_target_pairs={{0,1},{1,0},{2,3},{3,2},{4,5},{5,4},{6,7},{7,6},{8,9},{9,8},{10,11... | collective-permute-start | bytes 1179656 | tf_op jit(solution)/shard_map/ppermute | solution.py:1069
  49.9 20.2 %collective-permute-start.3 = (bf16[512,768]{1,0:T(8,128)(2,1)}, bf16[512,768]{1,0:T(8,128)(2,1)S(1)}, u32[]{:S(2)}, u32[]{:S(2)}) collective-permute-start(bf16[512,768]{1,0:T(8,128)(2,1)} %behind.5.refs_2_), channel_id=1, source_target_pairs={{0,1},{1,0},{2,3},{3,2},{4,5},{5,4},{6,7},{7,6},{8,9},{9,8},{10,11... | collective-permute-start | bytes 2359304 | tf_op jit(solution)/shard_map/ppermute | solution.py:1069
  80.6 19.3 %collective-permute-start.4 = (bf16[512,768]{1,0:T(8,128)(2,1)}, bf16[512,768]{1,0:T(8,128)(2,1)S(1)}, u32[]{:S(2)}, u32[]{:S(2)}) collective-permute-start(bf16[512,768]{1,0:T(8,128)(2,1)} %get-tuple-element.127.refs_2_), channel_id=1, source_target_pairs={{0,1},{1,0},{2,3},{3,2},{4,5},{5,4},{6,7},{7,6},{8,9},{9,8},{10,11... | collective-permute-start | bytes 2359304 | tf_op jit(solution)/shard_map/ppermute | solution.py:1069
  113.0 18.3 %collective-permute-start.5 = (bf16[512,768]{1,0:T(8,128)(2,1)}, bf16[512,768]{1,0:T(8,128)(2,1)S(1)}, u32[]{:S(2)}, u32[]{:S(2)}) collective-permute-start(bf16[512,768]{1,0:T(8,128)(2,1)} %get-tuple-element.129.refs_2_), channel_id=1, source_target_pairs={{0,1},{1,0},{2,3},{3,2},{4,5},{5,4},{6,7},{7,6},{8,9},{9,8},{10,11... | collective-permute-start | bytes 2359304 | tf_op jit(solution)/shard_map/ppermute | solution.py:1069
  141.9 12.9 %collective-permute-start.6 = (bf16[512,384]{1,0:T(8,128)(2,1)}, bf16[512,384]{1,0:T(8,128)(2,1)S(1)}, u32[]{:S(2)}, u32[]{:S(2)}) collective-permute-start(bf16[512,384]{1,0:T(8,128)(2,1)} %get-tuple-element.132), channel_id=1, source_target_pairs={{0,1},{1,0},{2,3},{3,2},{4,5},{5,4},{6,7},{7,6},{8,9},{9,8},{10,11... | collective-permute-start | bytes 1179656 | tf_op jit(solution)/shard_map/ppermute | solution.py:1069
  155.5 4.7 collective-permute-start.8
  155.5 21.9 %collective-permute-start.7 = (bf16[512,768]{1,0:T(8,128)(2,1)}, bf16[512,768]{1,0:T(8,128)(2,1)S(1)}, u32[]{:S(2)}, u32[]{:S(2)}) collective-permute-start(bf16[512,768]{1,0:T(8,128)(2,1)} %get-tuple-element.136.refs_2_), channel_id=1, source_target_pairs={{0,1},{1,0},{2,3},{3,2},{4,5},{5,4},{6,7},{7,6},{8,9},{9,8},{10,11... | collective-permute-start | bytes 2359304 | tf_op jit(solution)/shard_map/ppermute | solution.py:1069
  168.1 29.6 %collective-permute-start.9 = (bf16[4,96,768]{2,1,0:T(8,128)(2,1)}, bf16[4,96,768]{2,1,0:T(8,128)(2,1)S(1)}, u32[]{:S(2)}, u32[]{:S(2)}) collective-permute-start(bf16[4,96,768]{2,1,0:T(8,128)(2,1)} %get-tuple-element.143.refs_21_), channel_id=1, source_target_pairs={{0,4},{2,18},{4,8},{6,22},{8,12},{10,26},{12,0},{14,30},{16,20},{1... | collective-permute-start | bytes 1769480 | tf_op jit(solution)/shard_map/ppermute | solution.py:1078
  169.6 28.1 %collective-permute-start.10 = (bf16[4,96,768]{2,1,0:T(8,128)(2,1)}, bf16[4,96,768]{2,1,0:T(8,128)(2,1)S(1)}, u32[]{:S(2)}, u32[]{:S(2)}) collective-permute-start(bf16[4,96,768]{2,1,0:T(8,128)(2,1)} %get-tuple-element.144.refs_22_), channel_id=1, source_target_pairs={{0,8},{2,34},{4,12},{6,38},{8,0},{10,42},{12,4},{14,46},{16,24},{1... | collective-permute-start | bytes 1769480 | tf_op jit(solution)/shard_map/ppermute | solution.py:1078
  172.3 25.4 %collective-permute-start.11 = (bf16[4,96,768]{2,1,0:T(8,128)(2,1)}, bf16[4,96,768]{2,1,0:T(8,128)(2,1)S(1)}, u32[]{:S(2)}, u32[]{:S(2)}) collective-permute-start(bf16[4,96,768]{2,1,0:T(8,128)(2,1)} %get-tuple-element.145.refs_23_), channel_id=1, source_target_pairs={{0,12},{2,50},{4,0},{6,54},{8,4},{10,58},{12,8},{14,62},{16,28},{1... | collective-permute-start | bytes 1769480 | tf_op jit(solution)/shard_map/ppermute | solution.py:1078
  199.0 6.4 %collective-permute-start.13 = (bf16[512,2304]{1,0:T(8,128)(2,1)}, bf16[512,2304]{1,0:T(8,128)(2,1)S(1)}, u32[]{:S(2)}, u32[]{:S(2)}) collective-permute-start(bf16[512,2304]{1,0:T(8,128)(2,1)} %get-tuple-element.152), channel_id=1, source_target_pairs={{0,2},{2,0},{1,3},{3,1},{4,6},{6,4},{5,7},{7,5},{8,10},{10,8},{9,1... | collective-permute-start | bytes 7077896 | tf_op jit(solution)/shard_map/ppermute | solution.py:1069
  199.0 21.7 %collective-permute-start.12 = (bf16[512,768]{1,0:T(8,128)(2,1)}, bf16[512,768]{1,0:T(8,128)(2,1)S(1)}, u32[]{:S(2)}, u32[]{:S(2)}) collective-permute-start(bf16[512,768]{1,0:T(8,128)(2,1)} %get-tuple-element.149.refs_2_), channel_id=1, source_target_pairs={{0,1},{1,0},{2,3},{3,2},{4,5},{5,4},{6,7},{7,6},{8,9},{9,8},{10,11... | collective-permute-start | bytes 2359304 | tf_op jit(solution)/shard_map/ppermute | solution.py:1069
  211.7 24.7 %collective-permute-start.14 = (bf16[4,96,384]{2,1,0:T(8,128)(2,1)}, bf16[4,96,384]{2,1,0:T(8,128)(2,1)S(1)}, u32[]{:S(2)}, u32[]{:S(2)}) collective-permute-start(bf16[4,96,384]{2,1,0:T(8,128)(2,1)} %get-tuple-element.154.refs_12_), channel_id=1, source_target_pairs={{0,4},{2,18},{4,8},{6,22},{8,12},{10,26},{12,0},{14,30},{16,20},{1... | collective-permute-start | bytes 884744 | tf_op jit(solution)/shard_map/ppermute | solution.py:1078
  213.2 23.3 %collective-permute-start.15 = (bf16[4,96,384]{2,1,0:T(8,128)(2,1)}, bf16[4,96,384]{2,1,0:T(8,128)(2,1)S(1)}, u32[]{:S(2)}, u32[]{:S(2)}) collective-permute-start(bf16[4,96,384]{2,1,0:T(8,128)(2,1)} %get-tuple-element.155.refs_13_), channel_id=1, source_target_pairs={{0,8},{2,34},{4,12},{6,38},{8,0},{10,42},{12,4},{14,46},{16,24},{1... | collective-permute-start | bytes 884744 | tf_op jit(solution)/shard_map/ppermute | solution.py:1078
  215.9 20.6 %collective-permute-start.16 = (bf16[4,96,384]{2,1,0:T(8,128)(2,1)}, bf16[4,96,384]{2,1,0:T(8,128)(2,1)S(1)}, u32[]{:S(2)}, u32[]{:S(2)}) collective-permute-start(bf16[4,96,384]{2,1,0:T(8,128)(2,1)} %get-tuple-element.156.refs_14_), channel_id=1, source_target_pairs={{0,12},{2,50},{4,0},{6,54},{8,4},{10,58},{12,8},{14,62},{16,28},{1... | collective-permute-start | bytes 884744 | tf_op jit(solution)/shard_map/ppermute | solution.py:1078
  237.4 4.7 collective-permute-start.18
  237.4 21.7 %collective-permute-start.17 = (bf16[512,768]{1,0:T(8,128)(2,1)}, bf16[512,768]{1,0:T(8,128)(2,1)S(1)}, u32[]{:S(2)}, u32[]{:S(2)}) collective-permute-start(bf16[512,768]{1,0:T(8,128)(2,1)} %get-tuple-element.160.refs_2_), channel_id=1, source_target_pairs={{0,1},{1,0},{2,3},{3,2},{4,5},{5,4},{6,7},{7,6},{8,9},{9,8},{10,11... | collective-permute-start | bytes 2359304 | tf_op jit(solution)/shard_map/ppermute | solution.py:1069
  249.9 29.8 %collective-permute-start.19 = (bf16[4,96,768]{2,1,0:T(8,128)(2,1)}, bf16[4,96,768]{2,1,0:T(8,128)(2,1)S(1)}, u32[]{:S(2)}, u32[]{:S(2)}) collective-permute-start(bf16[4,96,768]{2,1,0:T(8,128)(2,1)} %get-tuple-element.167.refs_21_), channel_id=1, source_target_pairs={{0,4},{2,18},{4,8},{6,22},{8,12},{10,26},{12,0},{14,30},{16,20},{1... | collective-permute-start | bytes 1769480 | tf_op jit(solution)/shard_map/ppermute | solution.py:1078
  251.4 28.3 %collective-permute-start.20 = (bf16[4,96,768]{2,1,0:T(8,128)(2,1)}, bf16[4,96,768]{2,1,0:T(8,128)(2,1)S(1)}, u32[]{:S(2)}, u32[]{:S(2)}) collective-permute-start(bf16[4,96,768]{2,1,0:T(8,128)(2,1)} %get-tuple-element.168.refs_22_), channel_id=1, source_target_pairs={{0,8},{2,34},{4,12},{6,38},{8,0},{10,42},{12,4},{14,46},{16,24},{1... | collective-permute-start | bytes 1769480 | tf_op jit(solution)/shard_map/ppermute | solution.py:1078
  254.2 25.6 %collective-permute-start.21 = (bf16[4,96,768]{2,1,0:T(8,128)(2,1)}, bf16[4,96,768]{2,1,0:T(8,128)(2,1)S(1)}, u32[]{:S(2)}, u32[]{:S(2)}) collective-permute-start(bf16[4,96,768]{2,1,0:T(8,128)(2,1)} %get-tuple-element.169.refs_23_), channel_id=1, source_target_pairs={{0,12},{2,50},{4,0},{6,54},{8,4},{10,58},{12,8},{14,62},{16,28},{1... | collective-permute-start | bytes 1769480 | tf_op jit(solution)/shard_map/ppermute | solution.py:1078
  284.1 6.1 %collective-permute-start.39 = (bf16[96,1152]{1,0:T(8,128)(2,1)}, bf16[96,1152]{1,0:T(8,128)(2,1)S(1)}, u32[]{:S(2)}, u32[]{:S(2)}) collective-permute-start(bf16[96,1152]{1,0:T(8,128)(2,1)} %get-tuple-element.213), channel_id=1, source_target_pairs={{0,16},{2,6},{4,20},{6,10},{8,24},{10,14},{12,28},{14,2},{16,32},{... | collective-permute-start | bytes 663560 | tf_op jit(solution)/shard_map/ppermute | solution.py:1078
  285.7 7.8 %collective-permute-start.40 = (bf16[96,1152]{1,0:T(8,128)(2,1)}, bf16[96,1152]{1,0:T(8,128)(2,1)S(1)}, u32[]{:S(2)}, u32[]{:S(2)}) collective-permute-start(bf16[96,1152]{1,0:T(8,128)(2,1)} %get-tuple-element.214), channel_id=1, source_target_pairs={{0,32},{2,10},{4,36},{6,14},{8,40},{10,2},{12,44},{14,6},{16,48},{... | collective-permute-start | bytes 663560 | tf_op jit(solution)/shard_map/ppermute | solution.py:1078
  286.6 8.5 %collective-permute-start.41 = (bf16[96,1152]{1,0:T(8,128)(2,1)}, bf16[96,1152]{1,0:T(8,128)(2,1)S(1)}, u32[]{:S(2)}, u32[]{:S(2)}) collective-permute-start(bf16[96,1152]{1,0:T(8,128)(2,1)} %get-tuple-element.215), channel_id=1, source_target_pairs={{0,48},{2,14},{4,52},{6,2},{8,56},{10,6},{12,60},{14,10},{16,0},{1... | collective-permute-start | bytes 663560 | tf_op jit(solution)/shard_map/ppermute | solution.py:1078
  297.9 6.1 %collective-permute-start.42 = (bf16[96,1152]{1,0:T(8,128)(2,1)}, bf16[96,1152]{1,0:T(8,128)(2,1)S(1)}, u32[]{:S(2)}, u32[]{:S(2)}) collective-permute-start(bf16[96,1152]{1,0:T(8,128)(2,1)} %add_parts.13.refs_0_), channel_id=1, source_target_pairs={{0,64},{64,0},{1,65},{65,1},{2,66},{66,2},{3,67},{67,3},{4,68},{68... | collective-permute-start | bytes 663560 | tf_op jit(solution)/shard_map/ppermute | solution.py:1069
  306.5 56.5 %collective-permute-start.23 = (bf16[512,2304]{1,0:T(8,128)(2,1)S(1)}, bf16[512,2304]{1,0:T(8,128)(2,1)}, u32[]{:S(2)}, u32[]{:S(2)}) collective-permute-start(bf16[512,2304]{1,0:T(8,128)(2,1)S(1)} %copy-done.5), channel_id=1, source_target_pairs={{0,2},{2,0},{1,3},{3,1},{4,6},{6,4},{5,7},{7,5},{8,10},{10,8},{9,1... | collective-permute-start | bytes 7077896 | tf_op jit(solution)/shard_map/ppermute | solution.py:1069
  356.3 105.4 %collective-permute-start.43 = (bf16[1,4,4,96,1152]{4,3,2,1,0:T(8,128)(2,1)}, bf16[1,4,4,96,1152]{4,3,2,1,0:T(8,128)(2,1)}, u32[]{:S(2)}, u32[]{:S(2)}) collective-permute-start(bf16[1,4,4,96,1152]{4,3,2,1,0:T(8,128)(2,1)} %bitcast.93), channel_id=1, source_target_pairs={{0,2},{2,0},{1,3},{3,1},{4,6},{6,4},{5,7},{7,5},{8,10},{10,8},{9,1... | collective-permute-start | bytes 10616840 | tf_op jit(solution)/shard_map/ppermute | solution.py:1069
  358.9 4.2 collective-permute-start.24
  369.0 12.4 %collective-permute-start.25 = (bf16[4,112,384]{2,1,0:T(8,128)(2,1)}, bf16[4,112,384]{2,1,0:T(8,128)(2,1)S(1)}, u32[]{:S(2)}, u32[]{:S(2)}) collective-permute-start(bf16[4,112,384]{2,1,0:T(8,128)(2,1)} %get-tuple-element.205.refs_7_), channel_id=1, source_target_pairs={{0,4},{2,18},{4,8},{6,22},{8,12},{10,26},{12,0},{14,30},{16,20},{1... | collective-permute-start | bytes 1032200 | tf_op jit(solution)/shard_map/ppermute | solution.py:1078
  369.3 12.1 %collective-permute-start.26 = (bf16[4,112,384]{2,1,0:T(8,128)(2,1)}, bf16[4,112,384]{2,1,0:T(8,128)(2,1)S(1)}, u32[]{:S(2)}, u32[]{:S(2)}) collective-permute-start(bf16[4,112,384]{2,1,0:T(8,128)(2,1)} %get-tuple-element.206.refs_8_), channel_id=1, source_target_pairs={{0,8},{2,34},{4,12},{6,38},{8,0},{10,42},{12,4},{14,46},{16,24},{1... | collective-permute-start | bytes 1032200 | tf_op jit(solution)/shard_map/ppermute | solution.py:1078
  371.9 10.3 %collective-permute-start.27 = (bf16[4,112,384]{2,1,0:T(8,128)(2,1)}, bf16[4,112,384]{2,1,0:T(8,128)(2,1)S(1)}, u32[]{:S(2)}, u32[]{:S(2)}) collective-permute-start(bf16[4,112,384]{2,1,0:T(8,128)(2,1)} %get-tuple-element.207.refs_9_), channel_id=1, source_target_pairs={{0,12},{2,50},{4,0},{6,54},{8,4},{10,58},{12,8},{14,62},{16,28},{1... | collective-permute-start | bytes 1032200 | tf_op jit(solution)/shard_map/ppermute | solution.py:1078
  385.1 7.9 %collective-permute-start.28 = (bf16[112,384]{1,0:T(8,128)(2,1)}, bf16[112,384]{1,0:T(8,128)(2,1)S(1)}, u32[]{:S(2)}, u32[]{:S(2)}) collective-permute-start(bf16[112,384]{1,0:T(8,128)(2,1)} %get-tuple-element.209), channel_id=1, source_target_pairs={{0,16},{2,6},{4,20},{6,10},{8,24},{10,14},{12,28},{14,2},{16,32},{... | collective-permute-start | bytes 258056 | tf_op jit(solution)/shard_map/ppermute | solution.py:1078
  386.6 9.3 %collective-permute-start.29 = (bf16[112,384]{1,0:T(8,128)(2,1)}, bf16[112,384]{1,0:T(8,128)(2,1)S(1)}, u32[]{:S(2)}, u32[]{:S(2)}) collective-permute-start(bf16[112,384]{1,0:T(8,128)(2,1)} %get-tuple-element.210), channel_id=1, source_target_pairs={{0,32},{2,10},{4,36},{6,14},{8,40},{10,2},{12,44},{14,6},{16,48},{... | collective-permute-start | bytes 258056 | tf_op jit(solution)/shard_map/ppermute | solution.py:1078
  388.4 7.5 %collective-permute-start.30 = (bf16[112,384]{1,0:T(8,128)(2,1)}, bf16[112,384]{1,0:T(8,128)(2,1)S(1)}, u32[]{:S(2)}, u32[]{:S(2)}) collective-permute-start(bf16[112,384]{1,0:T(8,128)(2,1)} %get-tuple-element.211), channel_id=1, source_target_pairs={{0,48},{2,14},{4,52},{6,2},{8,56},{10,6},{12,60},{14,10},{16,0},{1... | collective-permute-start | bytes 258056 | tf_op jit(solution)/shard_map/ppermute | solution.py:1078
  392.4 7.4 %collective-permute-start.45 = (bf16[96,768]{1,0:T(8,128)(2,1)}, bf16[96,768]{1,0:T(8,128)(2,1)S(1)}, u32[]{:S(2)}, u32[]{:S(2)}) collective-permute-start(bf16[96,768]{1,0:T(8,128)(2,1)} %get-tuple-element.222), channel_id=1, source_target_pairs={{0,16},{2,6},{4,20},{6,10},{8,24},{10,14},{12,28},{14,2},{16,32},{... | collective-permute-start | bytes 442376 | tf_op jit(solution)/shard_map/ppermute | solution.py:1078
  393.0 6.9 %collective-permute-start.46 = (bf16[96,768]{1,0:T(8,128)(2,1)}, bf16[96,768]{1,0:T(8,128)(2,1)S(1)}, u32[]{:S(2)}, u32[]{:S(2)}) collective-permute-start(bf16[96,768]{1,0:T(8,128)(2,1)} %get-tuple-element.223), channel_id=1, source_target_pairs={{0,32},{2,10},{4,36},{6,14},{8,40},{10,2},{12,44},{14,6},{16,48},{... | collective-permute-start | bytes 442376 | tf_op jit(solution)/shard_map/ppermute | solution.py:1078
  395.9 5.5 %collective-permute-start.47 = (bf16[96,768]{1,0:T(8,128)(2,1)}, bf16[96,768]{1,0:T(8,128)(2,1)S(1)}, u32[]{:S(2)}, u32[]{:S(2)}) collective-permute-start(bf16[96,768]{1,0:T(8,128)(2,1)} %get-tuple-element.224), channel_id=1, source_target_pairs={{0,48},{2,14},{4,52},{6,2},{8,56},{10,6},{12,60},{14,10},{16,0},{1... | collective-permute-start | bytes 442376 | tf_op jit(solution)/shard_map/ppermute | solution.py:1078
  398.3 7.2 %collective-permute-start.31 = (bf16[112,384]{1,0:T(8,128)(2,1)}, bf16[112,384]{1,0:T(8,128)(2,1)S(1)}, u32[]{:S(2)}, u32[]{:S(2)}) collective-permute-start(bf16[112,384]{1,0:T(8,128)(2,1)} %add_parts.10.refs_0_), channel_id=1, source_target_pairs={{0,64},{64,0},{1,65},{65,1},{2,66},{66,2},{3,67},{67,3},{4,68},{68... | collective-permute-start | bytes 258056 | tf_op jit(solution)/shard_map/ppermute | solution.py:1069
  403.9 9.3 %collective-permute-start.48 = (bf16[96,768]{1,0:T(8,128)(2,1)}, bf16[96,768]{1,0:T(8,128)(2,1)S(1)}, u32[]{:S(2)}, u32[]{:S(2)}) collective-permute-start(bf16[96,768]{1,0:T(8,128)(2,1)} %add_parts.16.refs_0_), channel_id=1, source_target_pairs={{0,64},{64,0},{1,65},{65,1},{2,66},{66,2},{3,67},{67,3},{4,68},{68... | collective-permute-start | bytes 442376 | tf_op jit(solution)/shard_map/ppermute | solution.py:1069
  407.7 11.4 %copy-start.13 = (bf16[112,384]{1,0:T(8,128)(2,1)S(1)}, bf16[112,384]{1,0:T(8,128)(2,1)}, u32[]{:S(2)}) copy-start(bf16[112,384]{1,0:T(8,128)(2,1)} %add_parts.11) | copy-start | bytes 258052
  407.7 29.0 %copy-start.1 = (bf16[512,768]{1,0:T(8,128)(2,1)S(1)}, bf16[512,768]{1,0:T(8,128)(2,1)}, u32[]{:S(2)}) copy-start(bf16[512,768]{1,0:T(8,128)(2,1)} %get-tuple-element.173.refs_2_.refs_8_) | copy-start | bytes 2359300
  407.7 8.1 %collective-permute-start.34 = (bf16[112,384]{1,0:T(8,128)(2,1)}, bf16[112,384]{1,0:T(8,128)(2,1)S(1)}, u32[]{:S(2)}, u32[]{:S(2)}) collective-permute-start(bf16[112,384]{1,0:T(8,128)(2,1)} %add_parts.11), channel_id=1, source_target_pairs={{0,48},{2,14},{4,52},{6,2},{8,56},{10,6},{12,60},{14,10},{16,0},{1... | collective-permute-start | bytes 258056 | tf_op jit(solution)/shard_map/ppermute | solution.py:1078
  409.1 8.3 %collective-permute-start.33 = (bf16[112,384]{1,0:T(8,128)(2,1)}, bf16[112,384]{1,0:T(8,128)(2,1)S(1)}, u32[]{:S(2)}, u32[]{:S(2)}) collective-permute-start(bf16[112,384]{1,0:T(8,128)(2,1)} %add_parts.11), channel_id=1, source_target_pairs={{0,32},{2,10},{4,36},{6,14},{8,40},{10,2},{12,44},{14,6},{16,48},{... | collective-permute-start | bytes 258056 | tf_op jit(solution)/shard_map/ppermute | solution.py:1078
  410.7 8.4 %collective-permute-start.32 = (bf16[112,384]{1,0:T(8,128)(2,1)}, bf16[112,384]{1,0:T(8,128)(2,1)S(1)}, u32[]{:S(2)}, u32[]{:S(2)}) collective-permute-start(bf16[112,384]{1,0:T(8,128)(2,1)} %add_parts.11), channel_id=1, source_target_pairs={{0,16},{2,6},{4,20},{6,10},{8,24},{10,14},{12,28},{14,2},{16,32},{... | collective-permute-start | bytes 258056 | tf_op jit(solution)/shard_map/ppermute | solution.py:1078
  415.6 10.4 %collective-permute-start.51 = (bf16[96,768]{1,0:T(8,128)(2,1)}, bf16[96,768]{1,0:T(8,128)(2,1)S(1)}, u32[]{:S(2)}, u32[]{:S(2)}) collective-permute-start(bf16[96,768]{1,0:T(8,128)(2,1)} %add_parts.17), channel_id=1, source_target_pairs={{0,48},{2,14},{4,52},{6,2},{8,56},{10,6},{12,60},{14,10},{16,0},{1... | collective-permute-start | bytes 442376 | tf_op jit(solution)/shard_map/ppermute | solution.py:1078
  415.9 12.6 %collective-permute-start.50 = (bf16[96,768]{1,0:T(8,128)(2,1)}, bf16[96,768]{1,0:T(8,128)(2,1)S(1)}, u32[]{:S(2)}, u32[]{:S(2)}) collective-permute-start(bf16[96,768]{1,0:T(8,128)(2,1)} %add_parts.17), channel_id=1, source_target_pairs={{0,32},{2,10},{4,36},{6,14},{8,40},{10,2},{12,44},{14,6},{16,48},{... | collective-permute-start | bytes 442376 | tf_op jit(solution)/shard_map/ppermute | solution.py:1078
  417.5 12.0 %collective-permute-start.49 = (bf16[96,768]{1,0:T(8,128)(2,1)}, bf16[96,768]{1,0:T(8,128)(2,1)S(1)}, u32[]{:S(2)}, u32[]{:S(2)}) collective-permute-start(bf16[96,768]{1,0:T(8,128)(2,1)} %add_parts.17), channel_id=1, source_target_pairs={{0,16},{2,6},{4,20},{6,10},{8,24},{10,14},{12,28},{14,2},{16,32},{... | collective-permute-start | bytes 442376 | tf_op jit(solution)/shard_map/ppermute | solution.py:1078
  419.2 12.9 %collective-permute-start.36 = (bf16[4,112,384]{2,1,0:T(8,128)(2,1)S(1)}, bf16[4,112,384]{2,1,0:T(8,128)(2,1)S(1)}, u32[]{:S(2)}, u32[]{:S(2)}) collective-permute-start(bf16[4,112,384]{2,1,0:T(8,128)(2,1)S(1)} %get-tuple-element.270), channel_id=1, source_target_pairs={{0,8},{2,34},{4,12},{6,38},{8,0},{10,42},{12,4},{14,46},{16,24},{1... | collective-permute-start | bytes 1032200 | tf_op jit(solution)/shard_map/ppermute | solution.py:1078
  426.1 8.7 %collective-permute-start.35 = (bf16[4,112,384]{2,1,0:T(8,128)(2,1)S(1)}, bf16[4,112,384]{2,1,0:T(8,128)(2,1)S(1)}, u32[]{:S(2)}, u32[]{:S(2)}) collective-permute-start(bf16[4,112,384]{2,1,0:T(8,128)(2,1)S(1)} %get-tuple-element.270), channel_id=1, source_target_pairs={{0,4},{2,18},{4,8},{6,22},{8,12},{10,26},{12,0},{14,30},{16,20},{1... | collective-permute-start | bytes 1032200 | tf_op jit(solution)/shard_map/ppermute | solution.py:1078
  428.5 8.3 %collective-permute-start.37 = (bf16[4,112,384]{2,1,0:T(8,128)(2,1)S(1)}, bf16[4,112,384]{2,1,0:T(8,128)(2,1)S(1)}, u32[]{:S(2)}, u32[]{:S(2)}) collective-permute-start(bf16[4,112,384]{2,1,0:T(8,128)(2,1)S(1)} %get-tuple-element.270), channel_id=1, source_target_pairs={{0,12},{2,50},{4,0},{6,54},{8,4},{10,58},{12,8},{14,62},{16,28},{1... | collective-permute-start | bytes 1032200 | tf_op jit(solution)/shard_map/ppermute | solution.py:1078
  430.5 12.1 %collective-permute-start.53 = (bf16[4,96,768]{2,1,0:T(8,128)(2,1)S(1)}, bf16[4,96,768]{2,1,0:T(8,128)(2,1)S(1)}, u32[]{:S(2)}, u32[]{:S(2)}) collective-permute-start(bf16[4,96,768]{2,1,0:T(8,128)(2,1)S(1)} %get-tuple-element.268), channel_id=1, source_target_pairs={{0,8},{2,34},{4,12},{6,38},{8,0},{10,42},{12,4},{14,46},{16,24},{1... | collective-permute-start | bytes 1769480 | tf_op jit(solution)/shard_map/ppermute | solution.py:1078
  432.1 16.8 %collective-permute-start.52 = (bf16[4,96,768]{2,1,0:T(8,128)(2,1)S(1)}, bf16[4,96,768]{2,1,0:T(8,128)(2,1)S(1)}, u32[]{:S(2)}, u32[]{:S(2)}) collective-permute-start(bf16[4,96,768]{2,1,0:T(8,128)(2,1)S(1)} %get-tuple-element.268), channel_id=1, source_target_pairs={{0,4},{2,18},{4,8},{6,22},{8,12},{10,26},{12,0},{14,30},{16,20},{1... | collective-permute-start | bytes 1769480 | tf_op jit(solution)/shard_map/ppermute | solution.py:1078
  434.7 14.1 %collective-permute-start.54 = (bf16[4,96,768]{2,1,0:T(8,128)(2,1)S(1)}, bf16[4,96,768]{2,1,0:T(8,128)(2,1)S(1)}, u32[]{:S(2)}, u32[]{:S(2)}) collective-permute-start(bf16[4,96,768]{2,1,0:T(8,128)(2,1)S(1)} %get-tuple-element.268), channel_id=1, source_target_pairs={{0,12},{2,50},{4,0},{6,54},{8,4},{10,58},{12,8},{14,62},{16,28},{1... | collective-permute-start | bytes 1769480 | tf_op jit(solution)/shard_map/ppermute | solution.py:1078
  436.8 19.7 %collective-permute-start.22 = (bf16[512,768]{1,0:T(8,128)(2,1)S(1)}, bf16[512,768]{1,0:T(8,128)(2,1)S(1)}, u32[]{:S(2)}, u32[]{:S(2)}) collective-permute-start(bf16[512,768]{1,0:T(8,128)(2,1)S(1)} %copy-done.1), channel_id=1, source_target_pairs={{0,1},{1,0},{2,3},{3,2},{4,5},{5,4},{6,7},{7,6},{8,9},{9,8},{10,11... | collective-permute-start | bytes 2359304 | tf_op jit(solution)/shard_map/ppermute | solution.py:1069
  442.6 26.7 %collective-permute-start.38 = (bf16[4,4,112,384]{3,2,1,0:T(8,128)(2,1)S(1)}, bf16[4,4,112,384]{3,2,1,0:T(8,128)(2,1)}, u32[]{:S(2)}, u32[]{:S(2)}) collective-permute-start(bf16[4,4,112,384]{3,2,1,0:T(8,128)(2,1)S(1)} %pad_maximum_fusion.1.refs_1_), channel_id=1, source_target_pairs={{0,2},{2,0},{1,3},{3,1},{4,6},{6,4},{5,7},{7,5},{8,10},{10,8},{9,1... | collective-permute-start | bytes 4128776 | tf_op jit(solution)/shard_map/ppermute | solution.py:1069
  449.2 12.6 %copy-start = (bf16[4,4,96,768]{3,2,1,0:T(8,128)(2,1)}, bf16[4,4,96,768]{3,2,1,0:T(8,128)(2,1)S(1)}, u32[]{:S(2)}) copy-start(bf16[4,4,96,768]{3,2,1,0:T(8,128)(2,1)S(1)} %pad_maximum_fusion.refs_1_) | copy-start | bytes 7077892
  449.2 38.8 %collective-permute-start.55 = (bf16[4,4,96,768]{3,2,1,0:T(8,128)(2,1)S(1)}, bf16[4,4,96,768]{3,2,1,0:T(8,128)(2,1)}, u32[]{:S(2)}, u32[]{:S(2)}) collective-permute-start(bf16[4,4,96,768]{3,2,1,0:T(8,128)(2,1)S(1)} %pad_maximum_fusion.refs_1_), channel_id=1, source_target_pairs={{0,2},{2,0},{1,3},{3,1},{4,6},{6,4},{5,7},{7,5},{8,10},{10,8},{9,1... | collective-permute-start | bytes 7077896 | tf_op jit(solution)/shard_map/ppermute | solution.py:1069
  477.7 21.6 %collective-permute-start.44 = (f32[72,384]{1,0:T(8,128)S(1)}, f32[72,384]{1,0:T(8,128)S(1)}, u32[]{:S(2)}, u32[]{:S(2)}) collective-permute-start(f32[72,384]{1,0:T(8,128)S(1)} %slice.100), channel_id=1, source_target_pairs={{0,1},{1,0},{2,3},{3,2},{4,5},{5,4},{6,7},{7,6},{8,9},{9,8},{10,11... | collective-permute-start | bytes 331784 | tf_op jit(solution)/shard_map/ppermute | solution.py:1069
  (41 other events, 61.6 us)
Sparse Core Ops, SparseCore 0:
  306.6 49.6 all-gather.2
